TPU v7x, 32 devices: a whole 2x2x4 slice. The times are simulated.
32 devices in a mesh: groups: 2 (over x), seq: 16 (over z, y, core).
Axes of the slice: x: 2, y: 2, z: 4, core: 2. Of those that a mesh axis runs over, the one named last changes fastest.
Arguments:
- signal: bfloat16 [16384, 2048], P(('groups', 'seq')), parts along dimension 0, may hold values from -6 to 6
- gate_input: bfloat16 [16384, 2048], P(('groups', 'seq')), parts along dimension 0, may hold values from -6 to 6
- cotangent: bfloat16 [16384, 2048], P(('groups', 'seq')), parts along dimension 0, may hold values from -6 to 6
- block_factor: bfloat16 [512, 512], replicated, may hold values from -0.25 to 0.25
- cross_factor: bfloat16 [512, 16, 16], P('seq'), may hold values from -1.5 to 1.5
- order_table: int32 [512], replicated, may hold values from 0 to 511, each once
Outputs:
- grad_signal: bfloat16 [16384, 2048], P(('groups', 'seq')), parts along dimension 0
- grad_gate: bfloat16 [16384, 2048], P(('groups', 'seq')), parts along dimension 0
- grad_block: float32 [1024, 512], P('groups'), parts along dimension 0
- grad_cross: float32 [512, 32, 16], P('seq', 'groups'), parts along dimension 1
There are 2 independent parts, one for each index of `groups`. A program takes and returns all parts, laid end to end along the dimension named above; an argument that names none is the same for every part. Nothing has to cross between parts.
Inputs may be any that keep to these rules, and one draw needn't show every extreme that they name: order_table holds every number of 0 to 511 exactly once.
All inputs are finite; a program needn't handle non-finite values.
Results may differ from a plain program's by a relative error of at most 0.0057.
Values may be sent and summed in bfloat16 or wider, within the bound.
No kernel may reach another device: no remote copies, remote signals or barrier semaphores. Data moves between devices by JAX's collectives and lax.ppermute only.
A program may use at most 64 MiB of HBM per device.

v0:
```python
import math

import jax
import jax.numpy as jnp
from jax import lax
from jax.sharding import PartitionSpec as P


def per_device(signal, gate_input, cotangent, block_factor, cross_factor, order_table):
    f32 = jnp.float32
    bf16 = jnp.bfloat16
    count = lax.axis_size("seq")
    width = signal.shape[1]
    permuted = jnp.take(signal, order_table, axis=0)
    mixed = jnp.dot(block_factor, permuted, preferred_element_type=f32).astype(bf16)
    gate_grad = (cotangent.astype(f32) * gate_input.astype(f32)).astype(bf16)
    spread_mixed = lax.all_to_all(mixed[None], "seq", split_axis=1, concat_axis=0, tiled=True)
    spread_grad = lax.all_to_all(gate_grad[None], "seq", split_axis=1, concat_axis=0, tiled=True)
    gated = jnp.einsum(
        "cij,jcd->icd", cross_factor, spread_mixed, preferred_element_type=f32
    ).astype(bf16)
    gated_home = lax.all_to_all(gated, "seq", split_axis=0, concat_axis=1, tiled=True)
    grad_cross = jnp.einsum(
        "icd,jcd->cij", spread_grad, spread_mixed, preferred_element_type=f32
    ) / math.sqrt(width)
    back = jnp.einsum("cij,icd->jcd", cross_factor, spread_grad, preferred_element_type=f32).astype(
        bf16
    )
    back_home = lax.all_to_all(back, "seq", split_axis=0, concat_axis=1, tiled=True)
    grad_gate = (cotangent.astype(f32) * gated_home[0].astype(f32)).astype(bf16)
    back_rows = back_home[0]
    partial_block = lax.dot_general(
        back_rows, permuted, (((1,), (1,)), ((), ())), preferred_element_type=f32
    )
    grad_block = lax.psum(partial_block, "seq") / math.sqrt(count * width)
    spread = lax.dot_general(
        block_factor, back_rows, (((0,), (0,)), ((), ())), preferred_element_type=f32
    ).astype(bf16)
    grad_signal = jnp.zeros_like(spread).at[order_table].set(spread)
    return (grad_signal, grad_gate, grad_block, grad_cross)


def solution(mesh):
    in_specs = (
        P(("groups", "seq"), None),
        P(("groups", "seq"), None),
        P(("groups", "seq"), None),
        P(),
        P("seq", None, None),
        P(),
    )
    out_specs = (
        P(("groups", "seq"), None),
        P(("groups", "seq"), None),
        P("groups", None),
        P("seq", "groups", None),
    )
    return jax.shard_map(
        per_device, mesh=mesh, in_specs=in_specs, out_specs=out_specs, check_vma=False
    )
```

profile of v0, /device:TPU:0, one launch (start us, length us, event | category | flops | bytes accessed | tf_op | source)
XLA Modules:
  0.0 409.7 jit_solution(3647754906035799778)
XLA Ops:
  7.2 0.0 copy-start
  7.2 0.8 compare_and_fusion
  8.0 0.7 compare_select_fusion
  8.7 0.1 copy-done
  8.8 3.3 gather_fusion
  12.1 0.0 copy-done.10
  12.1 3.1 fusion.3
  15.1 7.7 %copy.32 = bf16[1,512,2048]{2,0,1:T(2,128)(2,1)} copy(bf16[1,512,2048]{1,2,0:T(8,128)(2,1)S(1)} %fusion.3) | data formatting | bytes 4194304 | tf_op jit(solution)/shard_map/broadcast_in_dim | solution.py:17
  22.9 0.5 broadcast.9
  23.4 13.2 %reduce = bf16[512,2048]{1,0:T(8,128)(2,1)S(1)} reduce(bf16[512,1,2048]{2,1,0:T(2,128)(2,1)} %bitcast.31, bf16[]{:T(256)} %broadcast.9), dimensions={1}, to_apply=%bitcast.20.reduce_sub_computation | reduce | bytes 4194306
  36.5 2.8 reshape.52
  39.3 7.5 %all-to-all-start.2 = ((bf16[16,2,32768]{2,1,0:T(2,128)(2,1)}), bf16[16,2,32768]{2,1,0:T(2,128)(2,1)S(1)}, u32[]{:S(2)}, u32[]{:S(2)}) async-start(bf16[16,2,32768]{2,1,0:T(2,128)(2,1)} %reshape.52), calls=%async_computation.2 | async-start | bytes 4194304 | tf_op jit(solution)/shard_map/all_to_all | solution.py:17
  46.8 0.0 all-reduce.2.cloned.1.call-start
  46.9 0.0 copy-done.9
  46.9 0.2 copy.34
  47.1 40.9 %all-to-all-done.2 = bf16[16,2,32768]{2,1,0:T(2,128)(2,1)S(1)} async-done(((bf16[16,2,32768]{2,1,0:T(2,128)(2,1)}), bf16[16,2,32768]{2,1,0:T(2,128)(2,1)S(1)}, u32[]{:S(2)}, u32[]{:S(2)}) %all-to-all-start.2) | async-done | bytes 2097184 | tf_op jit(solution)/shard_map/all_to_all | solution.py:17
  87.9 6.7 %reshape.53 = bf16[512,1,2048]{2,1,0:T(2,128)(2,1)} reshape(bf16[16,2,32768]{2,1,0:T(2,128)(2,1)S(1)} %all-to-all-done.2) | data formatting | bytes 4194304
  94.7 3.5 copy.40
  98.1 0.0 copy-start.2
  98.1 2.4 fusion.5
  100.6 0.0 copy-done.2
  100.6 1.2 copy.35
  101.7 0.0 copy-start.5
  101.8 0.0 copy-start.6
  101.8 58.6 %all_to_all.42 = bf16[16,32,2048]{2,1,0:T(8,128)(2,1)S(1)} all-to-all(bf16[16,32,2048]{2,1,0:T(8,128)(2,1)S(1)} %copy.35), channel_id=1, replica_groups=mesh['groups'=2,'seq'=16] {'seq'}, dimensions={0} | all-to-all | bytes 4194304 | tf_op jit(solution)/shard_map/all_to_all | solution.py:22
  160.4 0.0 copy-done.5
  160.4 3.0 fusion.1
  163.3 5.2 %copy.54 = bf16[1,512,2048]{2,0,1:T(2,128)(2,1)} copy(bf16[1,512,2048]{2,1,0:T(8,128)(2,1)S(1)} %get-tuple-element.17) | data formatting | bytes 4194304 | tf_op jit(solution)/shard_map/broadcast_in_dim | solution.py:18
  168.5 13.2 %reduce.1 = bf16[512,2048]{1,0:T(8,128)(2,1)S(1)} reduce(bf16[512,1,2048]{2,1,0:T(2,128)(2,1)} %bitcast.32, bf16[]{:T(256)} %broadcast.9), dimensions={1}, to_apply=%bitcast.29.reduce_sub_computation | reduce | bytes 4194306
  181.7 2.8 reshape.50
  184.4 52.4 %all_to_all.43 = bf16[16,2,32768]{2,1,0:T(2,128)(2,1)S(1)} all-to-all(bf16[16,2,32768]{2,1,0:T(2,128)(2,1)} %reshape.50), channel_id=1, replica_groups=mesh['groups'=2,'seq'=16] {'seq'}, dimensions={0} | all-to-all | bytes 4194304 | tf_op jit(solution)/shard_map/all_to_all | solution.py:18
  236.9 6.7 %reshape.51 = bf16[512,1,2048]{2,1,0:T(2,128)(2,1)} reshape(bf16[16,2,32768]{2,1,0:T(2,128)(2,1)S(1)} %all_to_all.43) | data formatting | bytes 4194304
  243.6 3.5 copy.39
  247.1 2.4 fusion.4
  249.5 1.2 copy.30
  250.6 0.0 copy-start.7
  250.7 52.4 %all_to_all.44 = bf16[16,32,2048]{2,1,0:T(8,128)(2,1)S(1)} all-to-all(bf16[16,32,2048]{2,1,0:T(8,128)(2,1)S(1)} %copy.30), channel_id=1, replica_groups=mesh['groups'=2,'seq'=16] {'seq'}, dimensions={0} | all-to-all | bytes 4194304 | tf_op jit(solution)/shard_map/all_to_all | solution.py:29
  303.0 1.4 copy-done.8
  304.4 2.3 fusion.19
  306.7 0.0 all-reduce.2.cloned.1.call-update
  306.7 0.0 copy-done.3
  306.7 3.9 fusion.12
  310.6 0.8 copy.38
  311.5 4.3 %fusion.2 = bf16[512,2048]{0,1:T(8,128)(2,1)} fusion(bf16[512,2048]{1,0:T(8,128)(2,1)} %bitcast.40, bf16[512,512]{1,0:T(8,128)(2,1)S(1)} %copy-done.10), kind=kOutput, calls=%fused_computation.10 | convolution fusion | flops 1074790400 | bytes 4718592 | tf_op jit(solution)/shard_map/dot_general | solution.py:36
  315.8 4.1 %copy.31 = bf16[512,2048]{1,0:T(8,128)(2,1)} copy(bf16[512,2048]{0,1:T(8,128)(2,1)} %fusion.2) | data formatting | bytes 4194304 | tf_op jit(solution)/shard_map/convert_element_type | solution.py:38
  319.9 6.1 %scatter_custom_fusion = bf16[512,2048]{1,0:T(8,128)(2,1)} fusion(s32[512]{0:T(512)S(1)} %compare_select_fusion, bf16[512,2048]{1,0:T(8,128)(2,1)} %copy.31, bf16[]{:T(256)} %constant.8.clone.1), kind=kCustom, calls=%fused_computation.22 | custom fusion | bytes 2097664 | tf_op jit(solution)/shard_map/scatter | solution.py:39
  326.0 74.5 %all-reduce.2.cloned.1.call-done = f32[512,512]{1,0:T(8,128)} async-done(((f32[512,512]{1,0:T(8,128)}), f32[512,512]{1,0:T(8,128)}) %all-reduce.2.cloned.1.call-update) | async-done | bytes 1048592 | tf_op jit(solution)/shard_map/psum | solution.py:35
  400.6 2.3 broadcast_multiply_fusion
  (11 shorter events, 0.0 us)
Async XLA Ops:
  7.2 1.6 copy-start
  8.8 3.3 copy-start.10
  39.3 7.6 %copy-start.9 = (bf16[32,16,16]{0,2,1:T(8,128)(2,1)S(1)}, bf16[32,16,16]{0,2,1:T(8,128)(2,1)}, u32[]{:S(2)}) copy-start(bf16[32,16,16]{0,2,1:T(8,128)(2,1)} %param.10) | copy-start | bytes 49156
  39.3 48.6 %all-to-all-start.2 = ((bf16[16,2,32768]{2,1,0:T(2,128)(2,1)}), bf16[16,2,32768]{2,1,0:T(2,128)(2,1)S(1)}, u32[]{:S(2)}, u32[]{:S(2)}) async-start(bf16[16,2,32768]{2,1,0:T(2,128)(2,1)} %reshape.52), calls=%async_computation.2 | async-start | bytes 4194304 | tf_op jit(solution)/shard_map/all_to_all | solution.py:17
  46.8 353.7 %all-reduce.2.cloned.1.call-start = ((), (), s32[]{:S(2)}) async-start(), calls=%async_computation.4 | async-start | bytes 2097152 | tf_op jit(solution)/shard_map/psum | solution.py:35
  98.1 2.4 copy-start.2
  101.7 58.6 %copy-start.5 = (bf16[512,2048]{1,0:T(8,128)(2,1)S(1)}, bf16[512,2048]{1,0:T(8,128)(2,1)}, u32[]{:S(2)}) copy-start(bf16[512,2048]{1,0:T(8,128)(2,1)} %param.8) | copy-start | bytes 6291460
  101.8 58.6 %copy-start.6 = (bf16[512,2048]{1,0:T(8,128)(2,1)S(1)}, bf16[512,2048]{1,0:T(8,128)(2,1)}, u32[]{:S(2)}) copy-start(bf16[512,2048]{1,0:T(8,128)(2,1)} %param.7) | copy-start | bytes 6291460
  247.1 2.4 copy-start.4
  250.6 53.7 %copy-start.7 = (bf16[512,2048]{1,0:T(8,128)(2,1)S(1)}, bf16[512,2048]{1,0:T(8,128)(2,1)}, u32[]{:S(2)}) copy-start(bf16[512,2048]{1,0:T(8,128)(2,1)} %gather_fusion) | copy-start | bytes 6291460
  303.0 1.4 copy-start.8
  304.4 2.4 copy-start.3
  315.8 87.1 %copy-start.1 = (bf16[512,2048]{1,0:T(8,128)(2,1)S(1)}, bf16[512,2048]{1,0:T(8,128)(2,1)}, u32[]{:S(2)}) copy-start(bf16[512,2048]{1,0:T(8,128)(2,1)} %param.6) | copy-start | bytes 6291460
Sparse Core Ops, SparseCore 0:
  306.9 93.6 all-reduce.1
where the time goes:
time: 410 us
  blocking collectives  163 us (40%)
  waiting for transfers between devices  115 us (28%)
  local copies, waits for them, and re-layouts  57.6 us (14%)
  other arithmetic  33.1 us (8%)
  matrix products  18.5 us (5%)
  between operations  14.2 us (3%)
  starting transfers between devices  7.56 us (2%)
    psum x1, waiting for transfers between devices, per_device(): grad_block = lax.psum(partial_block, 'seq') / math.sqrt(count * width)  74.5 us
    all_to_all x1, blocking collectives, per_device(): lax.all_to_all(gated, 'seq', split_axis=0, concat_axis=1, tiled=True)  58.6 us
    all_to_all x1, blocking collectives, per_device(): lax.all_to_all(gate_grad[None], 'seq', split_axis=1, concat_axis=0, tiled...  52.4 us
    all_to_all x1, blocking collectives, per_device(): lax.all_to_all(back, 'seq', split_axis=0, concat_axis=1, tiled=True)  52.4 us
    all_to_all x1, waiting for transfers between devices, per_device(): lax.all_to_all(mixed[None], 'seq', split_axis=1, concat_axis=0, tiled=True)  40.9 us
    unnamed x31, local copies, waits for them, and re-layouts  28.9 us
    unnamed x2, other arithmetic  26.3 us
  transfers between devices with their start and end apart: 2, of which 2 were waited for; matrix products, arithmetic and copies ran while one was open for 5% of the time, Pallas kernels for 0%

commit v1 on v0

v1 whole, which is shorter than its diff:
```python
import math

import jax
import jax.numpy as jnp
from jax import lax
from jax.sharding import PartitionSpec as P


def exchange(rows):
    return lax.all_to_all(rows, "seq", split_axis=0, concat_axis=0, tiled=True)


def per_device(signal, gate_input, cotangent, block_factor, cross_factor, order_table):
    f32 = jnp.float32
    bf16 = jnp.bfloat16
    count = lax.axis_size("seq")
    block, width = signal.shape
    share = block // count
    parted = (count, share, width)
    gate_grad = (cotangent.astype(f32) * gate_input.astype(f32)).astype(bf16)
    spread_grad = exchange(gate_grad.reshape(parted))

    one_hot = (order_table[:, None] == jnp.arange(block, dtype=jnp.int32)[None, :]).astype(bf16)
    factor = jnp.dot(block_factor, one_hot, preferred_element_type=f32).astype(bf16)
    mixed = jnp.dot(factor, signal, preferred_element_type=f32).astype(bf16)

    back = jnp.einsum("cij,icd->jcd", cross_factor, spread_grad, preferred_element_type=f32).astype(
        bf16
    )
    back, mixed = lax.optimization_barrier((back, mixed))
    back_rows = exchange(back).reshape(block, width)
    back_rows, mixed = lax.optimization_barrier((back_rows, mixed))
    spread_mixed = exchange(mixed.reshape(parted))

    partial_block = lax.dot_general(
        back_rows, signal, (((1,), (1,)), ((), ())), preferred_element_type=f32
    )
    partial_block = jnp.dot(
        partial_block.astype(bf16), one_hot.T, preferred_element_type=f32
    )
    grad_block = lax.psum(partial_block, "seq") / math.sqrt(count * width)
    grad_signal = lax.dot_general(
        factor, back_rows, (((0,), (0,)), ((), ())), preferred_element_type=f32
    ).astype(bf16)

    gated = jnp.einsum(
        "cij,jcd->icd", cross_factor, spread_mixed, preferred_element_type=f32
    ).astype(bf16)
    gated_home = exchange(gated).reshape(block, width)
    grad_cross = jnp.einsum(
        "icd,jcd->cij", spread_grad, spread_mixed, preferred_element_type=f32
    ) / math.sqrt(width)
    grad_gate = (cotangent.astype(f32) * gated_home.astype(f32)).astype(bf16)
    return (grad_signal, grad_gate, grad_block, grad_cross)


def solution(mesh):
    in_specs = (
        P(("groups", "seq"), None),
        P(("groups", "seq"), None),
        P(("groups", "seq"), None),
        P(),
        P("seq", None, None),
        P(),
    )
    out_specs = (
        P(("groups", "seq"), None),
        P(("groups", "seq"), None),
        P("groups", None),
        P("seq", "groups", None),
    )
    return jax.shard_map(
        per_device, mesh=mesh, in_specs=in_specs, out_specs=out_specs, check_vma=False
    )
```

time: 410 us -> 327 us (0.80)
  blocking collectives: 163 us -> 111 us
  local copies, waits for them, and re-layouts: 57.6 us -> 5.97 us
  waiting for transfers between devices: 115 us -> 149 us
  other arithmetic: 33.1 us -> 11.5 us
  starting transfers between devices: 7.56 us -> 12.9 us
    all_to_all x3 -> x2, blocking collectives: 163 us -> 111 us  [exchange(): return lax.all_to_all(rows, 'seq', split_axis=0, concat_axis=0, tiled=True)]
    psum x1, waiting for transfers between devices: 74.5 us -> 112 us  [per_device(): grad_block = lax.psum(partial_block, 'seq') / math.sqrt(count * width)]
    unnamed x31 -> x16, local copies, waits for them, and re-layouts: 28.9 us -> 2.33 us
    unnamed x2 -> x0, other arithmetic: 26.3 us -> none
    broadcast_in_dim x2 -> x0, local copies, waits for them, and re-layouts: 12.9 us -> none  [the longest x1 7.73 us: per_device(): mixed[None]]
    scatter x1 -> x0, local copies, waits for them, and re-layouts: 6.15 us -> none  [per_device(): grad_signal = jnp.zeros_like(spread).at[order_table].set(spread)]
    convert_element_type x1 -> x2, other arithmetic: 2.96 us -> 9.03 us  [the longest x1 4.59 us: per_device(): gate_grad = (cotangent.astype(f32) * gate_input.astype(f32)).astype(bf16)]
    convert_element_type x2 -> x0, local copies, waits for them, and re-layouts: 5.27 us -> none  [the longest x1 4.12 us: per_device(): spread = lax.dot_general(block_factor, back_rows, (((0,), (0,)), ((), ())...]
  transfers between devices with their start and end apart: 2 -> 3, of which waited for: 2 -> 2; matrix products, arithmetic and copies ran while one was open for 5% -> 6% of each run, Pallas kernels for 0% -> 0%
where the time goes in v1:
time: 327 us
  waiting for transfers between devices  149 us (46%)
  blocking collectives  111 us (34%)
  matrix products  21.9 us (7%)
  between operations  14.1 us (4%)
  starting transfers between devices  12.9 us (4%)
  other arithmetic  11.5 us (4%)
  local copies, waits for them, and re-layouts  5.97 us (2%)
    psum x1, waiting for transfers between devices, per_device(): grad_block = lax.psum(partial_block, 'seq') / math.sqrt(count * width)  112 us
    all_to_all x2, blocking collectives, exchange(): return lax.all_to_all(rows, 'seq', split_axis=0, concat_axis=0, tiled=True)  111 us
    all_to_all x2, waiting for transfers between devices, exchange(): return lax.all_to_all(rows, 'seq', split_axis=0, concat_axis=0, tiled=True)  37.7 us
    all_to_all x2, starting transfers between devices, exchange(): return lax.all_to_all(rows, 'seq', split_axis=0, concat_axis=0, tiled=True)  12.7 us
  transfers between devices with their start and end apart: 3, of which 2 were waited for; matrix products, arithmetic and copies ran while one was open for 6% of the time, Pallas kernels for 0%

profile of v1, /device:TPU:0, one launch (start us, length us, event | category | flops | bytes accessed | tf_op | source)
XLA Modules:
  0.0 326.6 jit_solution(9164491841973889735)
XLA Ops:
  7.2 0.0 copy-start
  7.2 4.6 %fusion = bf16[512,2048]{1,0:T(8,128)(2,1)} fusion(bf16[512,2048]{1,0:T(8,128)(2,1)} %param.8, bf16[512,2048]{1,0:T(8,128)(2,1)} %param.7), kind=kLoop, calls=%fused_computation.2 | loop fusion | flops 4194304 | bytes 6291456 | tf_op jit(solution)/shard_map/convert_element_type | solution.py:20
  11.8 0.0 copy-start.4
  11.8 0.0 copy-start.5
  11.8 0.0 copy-start.6
  11.8 7.6 %all-to-all-start = ((bf16[16,32,2048]{2,1,0:T(8,128)(2,1)}), bf16[16,32,2048]{2,1,0:T(8,128)(2,1)}, u32[]{:S(2)}, u32[]{:S(2)}) async-start(bf16[16,32,2048]{2,1,0:T(8,128)(2,1)} %bitcast.19), calls=%async_computation | async-start | bytes 4194304 | tf_op jit(solution)/shard_map/all_to_all | solution.py:10
  19.4 0.0 copy-done.4
  19.4 0.2 copy.25
  19.5 0.0 copy-done.5
  19.5 0.0 copy-done.6
  19.6 0.6 convolution_convert_fusion.4
  20.2 0.0 copy-done
  20.2 2.6 convolution_convert_fusion.3
  22.8 37.7 %all-to-all-done = bf16[16,32,2048]{2,1,0:T(8,128)(2,1)} async-done(((bf16[16,32,2048]{2,1,0:T(8,128)(2,1)}), bf16[16,32,2048]{2,1,0:T(8,128)(2,1)}, u32[]{:S(2)}, u32[]{:S(2)}) %all-to-all-start) | async-done | bytes 2097184 | tf_op jit(solution)/shard_map/all_to_all | solution.py:10
  60.5 4.0 %fusion.2 = bf16[16,32,2048]{2,0,1:T(8,128)(2,1)S(1)} fusion(bf16[32,16,16]{2,1,0:T(8,128)(2,1)S(1)} %copy.25, bf16[16,32,2048]{2,1,0:T(8,128)(2,1)} %all-to-all-done), kind=kOutput, calls=%fused_computation.8 | convolution fusion | flops 34603008 | bytes 4210688 | tf_op jit(solution)/shard_map/cij,icd->jcd/dot_general | solution.py:27
  64.5 1.2 copy.23
  65.7 0.0 copy-start.3
  65.7 58.6 %all_to_all.20 = bf16[16,32,2048]{2,1,0:T(8,128)(2,1)} all-to-all(bf16[16,32,2048]{2,1,0:T(8,128)(2,1)S(1)} %copy.23), channel_id=1, replica_groups=mesh['groups'=2,'seq'=16] {'seq'}, dimensions={0} | all-to-all | bytes 4194304 | tf_op jit(solution)/shard_map/all_to_all | solution.py:10
  124.3 0.0 copy-done.3
  124.3 52.2 %all_to_all.21 = bf16[16,32,2048]{2,1,0:T(8,128)(2,1)S(1)} all-to-all(bf16[16,32,2048]{2,1,0:T(8,128)(2,1)S(1)} %bitcast.22), channel_id=1, replica_groups=mesh['groups'=2,'seq'=16] {'seq'}, dimensions={0} | all-to-all | bytes 4194304 | tf_op jit(solution)/shard_map/all_to_all | solution.py:10
  176.5 0.0 copy-start.1
  176.5 1.3 copy-done.1
  177.8 2.4 fusion.3
  180.3 2.5 copy.26
  182.7 5.2 %all-to-all-start.3 = ((bf16[16,32,2048]{2,1,0:T(8,128)(2,1)}), bf16[16,32,2048]{2,1,0:T(8,128)(2,1)}, u32[]{:S(2)}, u32[]{:S(2)}) async-start(bf16[16,32,2048]{2,1,0:T(8,128)(2,1)} %copy.26), calls=%async_computation.3 | async-start | bytes 4194304 | tf_op jit(solution)/shard_map/all_to_all | solution.py:10
  187.9 0.2 all-reduce.2.cloned.1.call-start
  188.1 4.1 %fusion.14 = f32[512,512]{1,0:T(8,128)} fusion(bf16[512,2048]{1,0:T(8,128)(2,1)} %bitcast.20, bf16[512,2048]{1,0:T(8,128)(2,1)S(1)} %copy-done, s32[512]{0:T(512)S(1)} %copy-done.6), kind=kOutput, calls=%fused_computation.18 | convolution fusion | flops 1342701568 | bytes 5244928 | tf_op jit(solution)/shard_map/dot_general | solution.py:38
  192.3 0.0 all-reduce.2.cloned.1.call-update
  192.3 4.2 %convolution_convert_fusion.2 = bf16[512,2048]{1,0:T(8,128)(2,1)} fusion(bf16[512,512]{1,0:T(8,128)(2,1)S(1)} %convolution_convert_fusion.4, bf16[512,2048]{1,0:T(8,128)(2,1)} %bitcast.21), kind=kOutput, calls=%fused_computation.6 | convolution fusion | flops 1074790400 | bytes 4718592 | tf_op jit(solution)/shard_map/dot_general | solution.py:42
  196.5 111.6 %all-reduce.2.cloned.1.call-done = f32[512,512]{1,0:T(8,128)} async-done(((f32[512,512]{1,0:T(8,128)}), f32[512,512]{1,0:T(8,128)}) %all-reduce.2.cloned.1.call-update) | async-done | bytes 1048592 | tf_op jit(solution)/shard_map/psum | solution.py:41
  308.1 0.0 copy-start.2
  308.1 2.5 broadcast_multiply_fusion
  310.6 0.0 copy-done.2
  310.6 3.9 %fusion.9 = f32[32,16,16]{2,1,0:T(8,128)S(1)} fusion(bf16[16,32,2048]{2,1,0:T(8,128)(2,1)S(1)} %copy-done.2, bf16[16,32,2048]{2,1,0:T(8,128)(2,1)} %all-to-all-done), kind=kOutput, calls=%fused_computation.17 | convolution fusion | flops 33562624 | bytes 4227072 | tf_op jit(solution)/shard_map/icd,jcd->cij/dot_general | solution.py:50
  314.5 0.8 copy.29
  315.3 0.0 all-to-all-done.3
  315.3 4.4 %fusion.1 = bf16[512,2048]{1,0:T(8,128)(2,1)} fusion(bf16[512,2048]{1,0:T(8,128)(2,1)} %param.8, bf16[16,32,2048]{2,1,0:T(8,128)(2,1)} %all-to-all-done.3), kind=kLoop, calls=%fused_computation.3 | loop fusion | flops 4194304 | bytes 6291456 | tf_op jit(solution)/shard_map/convert_element_type | solution.py:53
Async XLA Ops:
  7.2 13.0 %copy-start = (bf16[512,2048]{1,0:T(8,128)(2,1)S(1)}, bf16[512,2048]{1,0:T(8,128)(2,1)}, u32[]{:S(2)}) copy-start(bf16[512,2048]{1,0:T(8,128)(2,1)} %param.6) | copy-start | bytes 6291460
  11.8 7.6 %copy-start.4 = (bf16[32,16,16]{0,2,1:T(8,128)(2,1)S(1)}, bf16[32,16,16]{0,2,1:T(8,128)(2,1)}, u32[]{:S(2)}) copy-start(bf16[32,16,16]{0,2,1:T(8,128)(2,1)} %param.10) | copy-start | bytes 49156
  11.8 7.8 %copy-start.5 = (bf16[512,512]{1,0:T(8,128)(2,1)S(1)}, bf16[512,512]{1,0:T(8,128)(2,1)}, u32[]{:S(2)}) copy-start(bf16[512,512]{1,0:T(8,128)(2,1)} %param.9) | copy-start | bytes 1572868
  11.8 7.8 %copy-start.6 = (s32[512]{0:T(512)S(1)}, s32[512]{0:T(512)}, u32[]{:S(2)}) copy-start(s32[512]{0:T(512)} %param.11) | copy-start | bytes 6148
  11.8 48.7 %all-to-all-start = ((bf16[16,32,2048]{2,1,0:T(8,128)(2,1)}), bf16[16,32,2048]{2,1,0:T(8,128)(2,1)}, u32[]{:S(2)}, u32[]{:S(2)}) async-start(bf16[16,32,2048]{2,1,0:T(8,128)(2,1)} %bitcast.19), calls=%async_computation | async-start | bytes 4194304 | tf_op jit(solution)/shard_map/all_to_all | solution.py:10
  65.7 58.6 %copy-start.3 = (bf16[512,2048]{1,0:T(8,128)(2,1)S(1)}, bf16[512,2048]{1,0:T(8,128)(2,1)}, u32[]{:S(2)}) copy-start(bf16[512,2048]{1,0:T(8,128)(2,1)} %convolution_convert_fusion.3) | copy-start | bytes 6291460
  176.5 1.3 copy-start.1
  182.7 132.5 %all-to-all-start.3 = ((bf16[16,32,2048]{2,1,0:T(8,128)(2,1)}), bf16[16,32,2048]{2,1,0:T(8,128)(2,1)}, u32[]{:S(2)}, u32[]{:S(2)}) async-start(bf16[16,32,2048]{2,1,0:T(8,128)(2,1)} %copy.26), calls=%async_computation.3 | async-start | bytes 4194304 | tf_op jit(solution)/shard_map/all_to_all | solution.py:10
  187.9 120.2 %all-reduce.2.cloned.1.call-start = ((), (), s32[]{:S(2)}) async-start(), calls=%async_computation.4 | async-start | bytes 2097152 | tf_op jit(solution)/shard_map/psum | solution.py:41
  308.1 2.5 copy-start.2
Sparse Core Ops, SparseCore 0:
  192.8 115.2 all-reduce.1

commit v2 on v1

v2 whole, which is shorter than its diff:
```python
import functools
import math

import jax
import jax.numpy as jnp
from jax import lax
from jax.experimental import pallas as pl
from jax.experimental.pallas import tpu as pltpu
from jax.sharding import PartitionSpec as P

F32 = jnp.float32
BF16 = jnp.bfloat16


def order_kernel(scale, position, rows, out):
    for a in range(rows.shape[0]):
        out[a] = rows[position[a]].astype(F32) * scale


def in_order(position, rows, scale):
    return pl.pallas_call(
        functools.partial(order_kernel, scale),
        in_specs=[
            pl.BlockSpec(memory_space=pltpu.SMEM),
            pl.BlockSpec(memory_space=pltpu.VMEM),
        ],
        out_specs=pl.BlockSpec(memory_space=pltpu.VMEM),
        out_shape=jax.ShapeDtypeStruct(rows.shape, F32),
    )(position, rows)


def exchange(rows):
    return lax.all_to_all(rows, "seq", split_axis=0, concat_axis=0, tiled=True)


def near_far():
    count = lax.axis_size("seq")
    inner = min(4, count)
    me = lax.axis_index("seq")

    def across(x, k):
        return lax.ppermute(
            x, "seq", [(s, ((s // inner) ^ k) * inner + s % inner) for s in range(count)]
        )

    def within(x, q):
        return lax.ppermute(
            x, "seq", [(s, s // inner * inner + ((s % inner) ^ q)) for s in range(count)]
        )

    return count // inner, inner, me // inner, me % inner, across, within


def tree_sum(terms):
    terms = [t.astype(F32) for t in terms]
    while len(terms) > 1:
        terms = [a + b for a, b in zip(terms[::2], terms[1::2])]
    return terms[0].astype(BF16)


def reduce_near(terms):
    outer, inner, z, r, across, within = near_far()
    block, n = terms.shape
    terms = terms.reshape(outer, inner, block // (outer * inner), n)
    lane = lambda q: lax.dynamic_index_in_dim(terms, jnp.bitwise_xor(r, q), 1, keepdims=False)
    return tree_sum([lane(0)] + [within(lane(q), q) for q in range(1, inner)])


def reduce_far(half):
    outer, inner, z, r, across, within = near_far()
    plane = lambda k: lax.dynamic_index_in_dim(half, jnp.bitwise_xor(z, k), 0, keepdims=False)
    return tree_sum([plane(0)] + [across(plane(k), k) for k in range(1, outer)])


def gather_far(own):
    outer, inner, z, r, across, within = near_far()
    return [own] + [across(own, k) for k in range(1, outer)]


def gather_near(rows, scale):
    outer, inner, z, r, across, within = near_far()
    got = jnp.stack(rows)
    got = jnp.concatenate([got] + [within(got, q) for q in range(1, inner)])
    every = jnp.arange(outer * inner, dtype=jnp.int32)
    position = jnp.bitwise_xor(r, every % inner) * outer + jnp.bitwise_xor(z, every // inner)
    return in_order(position.astype(jnp.int32), got, scale).reshape(-1, rows[0].shape[-1])


def per_device(signal, gate_input, cotangent, block_factor, cross_factor, order_table):
    count = lax.axis_size("seq")
    block, width = signal.shape
    share = block // count
    parted = (count, share, width)
    gate_grad = cotangent * gate_input
    spread_grad = exchange(gate_grad.reshape(parted))

    one_hot = (order_table[:, None] == jnp.arange(block, dtype=jnp.int32)[None, :]).astype(BF16)
    factor = jnp.dot(block_factor, one_hot, preferred_element_type=F32).astype(BF16)
    every = jnp.arange(block, dtype=jnp.int32)
    blocks = (every[:, None] // share == jnp.arange(count, dtype=jnp.int32)[None, :]).astype(BF16)
    same = every[:, None] % share == every[None, :] % share
    cross = cross_factor.swapaxes(0, 1).reshape(block, count)
    cross = jnp.dot(cross, blocks.T, preferred_element_type=F32)
    cross = jnp.where(same, cross, 0.0).astype(BF16)
    factor, cross, spread_grad = lax.optimization_barrier((factor, cross, spread_grad))

    grad_rows = spread_grad.reshape(block, width)
    back = lax.dot_general(
        cross, grad_rows, (((0,), (0,)), ((), ())), preferred_element_type=F32
    ).astype(BF16)
    factor, back = lax.optimization_barrier((factor, back))
    mixed = jnp.dot(factor, signal, preferred_element_type=F32).astype(BF16)
    back_rows = exchange(back.reshape(parted)).reshape(block, width)
    mixed, back_rows = lax.optimization_barrier((mixed, back_rows))
    spread_mixed = exchange(mixed.reshape(parted))

    partial_block = lax.dot_general(
        back_rows, signal, (((1,), (1,)), ((), ())), preferred_element_type=F32
    ).astype(BF16)
    partial_block = jnp.dot(partial_block, one_hot.T, preferred_element_type=F32).astype(BF16)
    own_block = reduce_far(reduce_near(partial_block))
    spread_mixed, own_block = lax.optimization_barrier((spread_mixed, own_block))
    far_blocks = gather_far(own_block)

    mixed_rows = spread_mixed.reshape(block, width)
    gated = jnp.dot(cross, mixed_rows, preferred_element_type=F32).astype(BF16)
    gated, far_blocks = lax.optimization_barrier((gated, far_blocks))
    gated_home = exchange(gated.reshape(parted)).reshape(block, width)

    grad_block = gather_near(far_blocks, 1.0 / math.sqrt(count * width))
    grad_signal = lax.dot_general(
        factor, back_rows, (((0,), (0,)), ((), ())), preferred_element_type=F32
    ).astype(BF16)
    products = lax.dot_general(
        grad_rows, mixed_rows, (((1,), (1,)), ((), ())), preferred_element_type=F32
    )
    products = jnp.dot(
        jnp.where(same, products, 0.0), blocks.astype(F32), precision=lax.Precision.HIGHEST
    )
    grad_cross = products.reshape(count, share, count).swapaxes(0, 1) / math.sqrt(width)
    gated_home, grad_block, grad_signal, grad_cross = lax.optimization_barrier(
        (gated_home, grad_block, grad_signal, grad_cross)
    )
    grad_gate = cotangent * gated_home
    return (grad_signal, grad_gate, grad_block, grad_cross)


def solution(mesh):
    in_specs = (
        P(("groups", "seq"), None),
        P(("groups", "seq"), None),
        P(("groups", "seq"), None),
        P(),
        P("seq", None, None),
        P(),
    )
    out_specs = (
        P(("groups", "seq"), None),
        P(("groups", "seq"), None),
        P("groups", None),
        P("seq", "groups", None),
    )
    return jax.shard_map(
        per_device, mesh=mesh, in_specs=in_specs, out_specs=out_specs, check_vma=False
    )
```

time: 327 us -> 239 us (0.73)
  the two profiles are of different devices: /device:TPU:0 before, /device:TPU:13 now
where the time goes in v2:
time: 239 us; the launch traced here: 238 us
  waiting for transfers between devices  161 us (67%)
  starting transfers between devices  38.5 us (16%)
  matrix products  24.3 us (10%)
  other arithmetic  9.63 us (4%)
    all_to_all x4, waiting for transfers between devices, exchange(): return lax.all_to_all(rows, 'seq', split_axis=0, concat_axis=0, tiled=True)  115 us
    ppermute x6, waiting for transfers between devices, across(): lax.ppermute(x, 'seq', [(s, (s // inner ^ k) * inner + s % inner) for s i...  24.6 us
    all_to_all x4, starting transfers between devices, exchange(): return lax.all_to_all(rows, 'seq', split_axis=0, concat_axis=0, tiled=True)  24.3 us
    ppermute x6, waiting for transfers between devices, within(): lax.ppermute(x, 'seq', [(s, s // inner * inner + (s % inner ^ q)) for s i...  21.7 us
    ppermute x6, starting transfers between devices, across(): lax.ppermute(x, 'seq', [(s, (s // inner ^ k) * inner + s % inner) for s i...  10 us
  transfers between devices with their start and end apart: 16, of which 10 were waited for; matrix products, arithmetic and copies ran while one was open for 9% of the time, Pallas kernels for 1%

profile of v2, /device:TPU:13, one launch (start us, length us, event | category | flops | bytes accessed | tf_op | source)
XLA Modules:
  0.0 238.4 jit_solution(2378109733518421718)
XLA Ops:
  0.6 0.0 copy-start
  0.6 4.6 %mul.9 = bf16[512,2048]{1,0:T(8,128)(2,1)} multiply(bf16[512,2048]{1,0:T(8,128)(2,1)} %param.8, bf16[512,2048]{1,0:T(8,128)(2,1)} %param.7) | non-fusion elementwise | flops 1048576 | bytes 6291456 | tf_op jit(solution)/shard_map/mul | solution.py:94
  5.2 6.7 %all-to-all-start = ((bf16[16,32,2048]{2,1,0:T(8,128)(2,1)}), bf16[16,32,2048]{2,1,0:T(8,128)(2,1)}, u32[]{:S(2)}, u32[]{:S(2)}) async-start(bf16[16,32,2048]{2,1,0:T(8,128)(2,1)} %bitcast.69), calls=%async_computation | async-start | bytes 4194304 | tf_op jit(solution)/shard_map/all_to_all | solution.py:33
  12.0 0.1 reshape.116
  12.1 0.4 fusion.1
  12.5 1.4 fusion.2
  13.9 45.5 %all-to-all-done = bf16[16,32,2048]{2,1,0:T(8,128)(2,1)} async-done(((bf16[16,32,2048]{2,1,0:T(8,128)(2,1)}), bf16[16,32,2048]{2,1,0:T(8,128)(2,1)}, u32[]{:S(2)}, u32[]{:S(2)}) %all-to-all-start) | async-done | bytes 2097184 | tf_op jit(solution)/shard_map/all_to_all | solution.py:33
  59.5 4.2 %convolution_convert_fusion.3 = bf16[512,2048]{1,0:T(8,128)(2,1)} fusion(bf16[512,512]{0,1:T(8,128)(2,1)S(1)} %fusion.1, bf16[512,2048]{1,0:T(8,128)(2,1)} %bitcast.4), kind=kOutput, calls=%fused_computation.3 | convolution fusion | flops 1074790400 | bytes 4718592 | tf_op jit(solution)/shard_map/dot_general | solution.py:108
  63.7 5.0 %all-to-all-start.1 = ((bf16[16,32,2048]{2,1,0:T(8,128)(2,1)}), bf16[16,32,2048]{2,1,0:T(8,128)(2,1)}, u32[]{:S(2)}, u32[]{:S(2)}) async-start(bf16[16,32,2048]{2,1,0:T(8,128)(2,1)} %bitcast.72), calls=%async_computation.1 | async-start | bytes 4194304 | tf_op jit(solution)/shard_map/all_to_all | solution.py:33
  68.7 2.6 %convolution_convert_fusion.2 = bf16[512,2048]{1,0:T(8,128)(2,1)} fusion(bf16[512,512]{0,1:T(8,128)(2,1)S(1)} %copy-done.6, bf16[512,2048]{1,0:T(8,128)(2,1)S(1)} %copy-done), kind=kOutput, calls=%fused_computation.2 | convolution fusion | flops 1074790400 | bytes 4718592 | tf_op jit(solution)/shard_map/dot_general | solution.py:112
  71.3 44.9 %all-to-all-done.1 = bf16[16,32,2048]{2,1,0:T(8,128)(2,1)} async-done(((bf16[16,32,2048]{2,1,0:T(8,128)(2,1)}), bf16[16,32,2048]{2,1,0:T(8,128)(2,1)}, u32[]{:S(2)}, u32[]{:S(2)}) %all-to-all-start.1) | async-done | bytes 2097184 | tf_op jit(solution)/shard_map/all_to_all | solution.py:33
  116.2 4.9 %all-to-all-start.2 = ((bf16[16,32,2048]{2,1,0:T(8,128)(2,1)}), bf16[16,32,2048]{2,1,0:T(8,128)(2,1)}, u32[]{:S(2)}, u32[]{:S(2)}) async-start(bf16[16,32,2048]{2,1,0:T(8,128)(2,1)} %bitcast.70), calls=%async_computation.2 | async-start | bytes 4194304 | tf_op jit(solution)/shard_map/all_to_all | solution.py:33
  121.1 3.2 %convolution_convert_fusion.5 = bf16[512,512]{1,0:T(8,128)(2,1)S(1)} fusion(bf16[512,2048]{1,0:T(8,128)(2,1)} %bitcast.6, bf16[512,2048]{1,0:T(8,128)(2,1)S(1)} %copy-done, s32[512]{0:T(512)S(1)} %copy-done.4), kind=kOutput, calls=%fused_computation.8 | convolution fusion | flops 1342963712 | bytes 4720640 | tf_op jit(solution)/shard_map/dot_general | solution.py:120
  124.4 0.4 collective-permute-start
  124.8 0.3 collective-permute-start.2
  125.1 1.2 collective-permute-start.1
  126.3 10.8 %collective-permute-done.2 = bf16[4,32,512]{2,1,0:T(8,128)(2,1)S(1)} collective-permute-done((bf16[4,32,512]{2,1,0:T(8,128)(2,1)S(1)}, bf16[4,32,512]{2,1,0:T(8,128)(2,1)S(1)}, u32[]{:S(2)}, u32[]{:S(2)}) %collective-permute-start.2) | collective-permute-done | bytes 131104 | tf_op jit(solution)/shard_map/ppermute | solution.py:47
  137.1 2.2 collective-permute-done.1
  139.2 0.1 fusion.8
  139.3 4.1 %collective-permute-start.3 = (bf16[32,512]{1,0:T(8,128)(2,1)S(1)}, bf16[32,512]{1,0:T(8,128)(2,1)S(1)}, u32[]{:S(2)}, u32[]{:S(2)}) collective-permute-start(bf16[32,512]{1,0:T(8,128)(2,1)S(1)} %get-tuple-element.43), channel_id=1, source_target_pairs={{0,4},{1,5},{2,6},{3,7},{4,0},{5,1},{6,2},{7,3},{8,12},{9,13},{10,... | collective-permute-start | bytes 98312 | tf_op jit(solution)/shard_map/ppermute | solution.py:42
  143.5 1.2 collective-permute-start.5
  144.7 1.0 collective-permute-start.4
  145.7 11.8 %collective-permute-done.3 = bf16[32,512]{1,0:T(8,128)(2,1)S(1)} collective-permute-done((bf16[32,512]{1,0:T(8,128)(2,1)S(1)}, bf16[32,512]{1,0:T(8,128)(2,1)S(1)}, u32[]{:S(2)}, u32[]{:S(2)}) %collective-permute-start.3) | collective-permute-done | bytes 32800 | tf_op jit(solution)/shard_map/ppermute | solution.py:42
  157.4 12.8 %collective-permute-done.5 = bf16[32,512]{1,0:T(8,128)(2,1)S(1)} collective-permute-done((bf16[32,512]{1,0:T(8,128)(2,1)S(1)}, bf16[32,512]{1,0:T(8,128)(2,1)S(1)}, u32[]{:S(2)}, u32[]{:S(2)}) %collective-permute-start.5) | collective-permute-done | bytes 32800 | tf_op jit(solution)/shard_map/ppermute | solution.py:42
  170.2 0.0 collective-permute-done.4
  170.3 0.3 all-to-all-done.2
  170.6 0.0 collective-permute-start.8
  170.6 3.7 %collective-permute-start.7 = (bf16[32,512]{1,0:T(8,128)(2,1)S(1)}, bf16[32,512]{1,0:T(8,128)(2,1)S(1)}, u32[]{:S(2)}, u32[]{:S(2)}) collective-permute-start(bf16[32,512]{1,0:T(8,128)(2,1)S(1)} %fusion.12), channel_id=1, source_target_pairs={{0,8},{1,9},{2,10},{3,11},{4,12},{5,13},{6,14},{7,15},{8,0},{9,1},... | collective-permute-start | bytes 98312 | tf_op jit(solution)/shard_map/ppermute | solution.py:42
  174.3 0.0 collective-permute-start.6
  174.3 4.4 %convolution_convert_fusion.1 = bf16[512,2048]{1,0:T(8,128)(2,1)} fusion(bf16[512,512]{0,1:T(8,128)(2,1)} %copy-done.5, bf16[512,2048]{1,0:T(8,128)(2,1)} %bitcast.17), kind=kOutput, calls=%fused_computation.1 | convolution fusion | flops 1074790400 | bytes 4718592 | tf_op jit(solution)/shard_map/dot_general | solution.py:126
  178.7 0.0 collective-permute-done.8
  178.7 0.0 copy-start.7
  178.7 7.6 %all-to-all-start.3 = ((bf16[16,32,2048]{2,1,0:T(8,128)(2,1)}), bf16[16,32,2048]{2,1,0:T(8,128)(2,1)}, u32[]{:S(2)}, u32[]{:S(2)}) async-start(bf16[16,32,2048]{2,1,0:T(8,128)(2,1)} %bitcast.71), calls=%async_computation.3 | async-start | bytes 4194304 | tf_op jit(solution)/shard_map/all_to_all | solution.py:33
  186.3 0.5 fusion.20.position
  186.8 4.2 %convolution_convert_fusion = bf16[512,2048]{1,0:T(8,128)(2,1)} fusion(bf16[512,512]{0,1:T(8,128)(2,1)S(1)} %copy-done.7, bf16[512,2048]{1,0:T(8,128)(2,1)} %bitcast.6), kind=kOutput, calls=%fused_computation | convolution fusion | flops 1074790400 | bytes 4718592 | tf_op jit(solution)/shard_map/dot_general | solution.py:131
  191.0 3.5 %compare_select_fusion = f32[512,512]{0,1:T(8,128)S(1)} fusion(bf16[512,2048]{1,0:T(8,128)(2,1)} %bitcast.4, bf16[512,2048]{1,0:T(8,128)(2,1)} %bitcast.17, s32[512]{0:T(512)S(1)} %get-tuple-element.47), kind=kOutput, calls=%fused_computation.6 | convolution fusion | flops 1074266112 | bytes 5244928 | tf_op jit(solution)/shard_map/dot_general | solution.py:134
  194.5 0.5 convolution_multiply_fusion
  195.0 0.1 div.46
  195.1 0.7 copy.16
  195.8 0.6 collective-permute-start.11
  196.4 1.2 collective-permute-start.10
  197.6 0.4 collective-permute-start.9
  198.1 1.0 collective-permute-done.9
  199.1 7.8 %collective-permute-done.10 = bf16[4,32,512]{2,1,0:T(8,128)(2,1)S(1)} collective-permute-done((bf16[4,32,512]{2,1,0:T(8,128)(2,1)S(1)}, bf16[4,32,512]{2,1,0:T(8,128)(2,1)S(1)}, u32[]{:S(2)}, u32[]{:S(2)}) %collective-permute-start.10) | collective-permute-done | bytes 131104 | tf_op jit(solution)/shard_map/ppermute | solution.py:47
  206.9 0.8 copy-done.1
  207.7 2.1 shard_map.93
  209.8 24.1 %all-to-all-done.3 = bf16[16,32,2048]{2,1,0:T(8,128)(2,1)} async-done(((bf16[16,32,2048]{2,1,0:T(8,128)(2,1)}), bf16[16,32,2048]{2,1,0:T(8,128)(2,1)}, u32[]{:S(2)}, u32[]{:S(2)}) %all-to-all-start.3) | async-done | bytes 2097184 | tf_op jit(solution)/shard_map/all_to_all | solution.py:33
  233.9 4.4 %mul.11 = bf16[512,2048]{1,0:T(8,128)(2,1)} multiply(bf16[512,2048]{1,0:T(8,128)(2,1)} %param.8, bf16[512,2048]{1,0:T(8,128)(2,1)} %bitcast.19) | non-fusion elementwise | flops 1048576 | bytes 6291456 | tf_op jit(solution)/shard_map/mul | solution.py:144
  (30 shorter events, 0.2 us)
Async XLA Ops:
  0.6 68.1 %copy-start = (bf16[512,2048]{1,0:T(8,128)(2,1)S(1)}, bf16[512,2048]{1,0:T(8,128)(2,1)}, u32[]{:S(2)}) copy-start(bf16[512,2048]{1,0:T(8,128)(2,1)} %param.6) | copy-start | bytes 6291460
  5.2 6.7 %copy-start.2 = (bf16[32,16,16]{0,2,1:T(8,128)(2,1)S(1)}, bf16[32,16,16]{0,2,1:T(8,128)(2,1)}, u32[]{:S(2)}) copy-start(bf16[32,16,16]{0,2,1:T(8,128)(2,1)} %param.10) | copy-start | bytes 49156
  5.2 7.2 %copy-start.3 = (bf16[512,512]{1,0:T(8,128)(2,1)S(1)}, bf16[512,512]{1,0:T(8,128)(2,1)}, u32[]{:S(2)}) copy-start(bf16[512,512]{1,0:T(8,128)(2,1)} %param.9) | copy-start | bytes 1572868
  5.2 7.2 %copy-start.4 = (s32[512]{0:T(512)S(1)}, s32[512]{0:T(512)}, u32[]{:S(2)}) copy-start(s32[512]{0:T(512)} %param.11) | copy-start | bytes 6148
  5.2 54.2 %all-to-all-start = ((bf16[16,32,2048]{2,1,0:T(8,128)(2,1)}), bf16[16,32,2048]{2,1,0:T(8,128)(2,1)}, u32[]{:S(2)}, u32[]{:S(2)}) async-start(bf16[16,32,2048]{2,1,0:T(8,128)(2,1)} %bitcast.69), calls=%async_computation | async-start | bytes 4194304 | tf_op jit(solution)/shard_map/all_to_all | solution.py:33
  12.5 51.2 %copy-start.5 = (bf16[512,512]{0,1:T(8,128)(2,1)}, bf16[512,512]{0,1:T(8,128)(2,1)S(1)}, u32[]{:S(2)}) copy-start(bf16[512,512]{0,1:T(8,128)(2,1)S(1)} %fusion.1) | copy-start | bytes 1572868
  63.7 5.1 %copy-start.6 = (bf16[512,512]{0,1:T(8,128)(2,1)S(1)}, bf16[512,512]{0,1:T(8,128)(2,1)}, u32[]{:S(2)}) copy-start(bf16[512,512]{0,1:T(8,128)(2,1)} %fusion.2) | copy-start | bytes 1572868
  63.7 52.6 %all-to-all-start.1 = ((bf16[16,32,2048]{2,1,0:T(8,128)(2,1)}), bf16[16,32,2048]{2,1,0:T(8,128)(2,1)}, u32[]{:S(2)}, u32[]{:S(2)}) async-start(bf16[16,32,2048]{2,1,0:T(8,128)(2,1)} %bitcast.72), calls=%async_computation.1 | async-start | bytes 4194304 | tf_op jit(solution)/shard_map/all_to_all | solution.py:33
  116.2 54.4 %all-to-all-start.2 = ((bf16[16,32,2048]{2,1,0:T(8,128)(2,1)}), bf16[16,32,2048]{2,1,0:T(8,128)(2,1)}, u32[]{:S(2)}, u32[]{:S(2)}) async-start(bf16[16,32,2048]{2,1,0:T(8,128)(2,1)} %bitcast.70), calls=%async_computation.2 | async-start | bytes 4194304 | tf_op jit(solution)/shard_map/all_to_all | solution.py:33
  124.4 1.9 collective-permute-start
  124.8 12.3 %collective-permute-start.2 = (bf16[4,32,512]{2,1,0:T(8,128)(2,1)S(1)}, bf16[4,32,512]{2,1,0:T(8,128)(2,1)S(1)}, u32[]{:S(2)}, u32[]{:S(2)}) collective-permute-start(bf16[4,32,512]{2,1,0:T(8,128)(2,1)S(1)} %get-tuple-element.41), channel_id=1, source_target_pairs={{0,3},{1,2},{2,1},{3,0},{4,7},{5,6},{6,5},{7,4},{8,11},{9,10},{10,... | collective-permute-start | bytes 393224 | tf_op jit(solution)/shard_map/ppermute | solution.py:47
  125.1 14.1 %collective-permute-start.1 = (bf16[4,32,512]{2,1,0:T(8,128)(2,1)S(1)}, bf16[4,32,512]{2,1,0:T(8,128)(2,1)S(1)}, u32[]{:S(2)}, u32[]{:S(2)}) collective-permute-start(bf16[4,32,512]{2,1,0:T(8,128)(2,1)S(1)} %get-tuple-element.42), channel_id=1, source_target_pairs={{0,2},{1,3},{2,0},{3,1},{4,6},{5,7},{6,4},{7,5},{8,10},{9,11},{10,... | collective-permute-start | bytes 393224 | tf_op jit(solution)/shard_map/ppermute | solution.py:47
  139.3 18.1 %collective-permute-start.3 = (bf16[32,512]{1,0:T(8,128)(2,1)S(1)}, bf16[32,512]{1,0:T(8,128)(2,1)S(1)}, u32[]{:S(2)}, u32[]{:S(2)}) collective-permute-start(bf16[32,512]{1,0:T(8,128)(2,1)S(1)} %get-tuple-element.43), channel_id=1, source_target_pairs={{0,4},{1,5},{2,6},{3,7},{4,0},{5,1},{6,2},{7,3},{8,12},{9,13},{10,... | collective-permute-start | bytes 98312 | tf_op jit(solution)/shard_map/ppermute | solution.py:42
  143.5 26.7 %collective-permute-start.5 = (bf16[32,512]{1,0:T(8,128)(2,1)S(1)}, bf16[32,512]{1,0:T(8,128)(2,1)S(1)}, u32[]{:S(2)}, u32[]{:S(2)}) collective-permute-start(bf16[32,512]{1,0:T(8,128)(2,1)S(1)} %get-tuple-element.44), channel_id=1, source_target_pairs={{0,12},{1,13},{2,14},{3,15},{4,8},{5,9},{6,10},{7,11},{8,4},{9,5},... | collective-permute-start | bytes 98312 | tf_op jit(solution)/shard_map/ppermute | solution.py:42
  144.7 25.5 %collective-permute-start.4 = (bf16[32,512]{1,0:T(8,128)(2,1)S(1)}, bf16[32,512]{1,0:T(8,128)(2,1)S(1)}, u32[]{:S(2)}, u32[]{:S(2)}) collective-permute-start(bf16[32,512]{1,0:T(8,128)(2,1)S(1)} %get-tuple-element.45), channel_id=1, source_target_pairs={{0,8},{1,9},{2,10},{3,11},{4,12},{5,13},{6,14},{7,15},{8,0},{9,1},... | collective-permute-start | bytes 98312 | tf_op jit(solution)/shard_map/ppermute | solution.py:42
  170.6 8.1 %collective-permute-start.8 = (bf16[32,512]{1,0:T(8,128)(2,1)S(1)}, bf16[32,512]{1,0:T(8,128)(2,1)S(1)}, u32[]{:S(2)}, u32[]{:S(2)}) collective-permute-start(bf16[32,512]{1,0:T(8,128)(2,1)S(1)} %fusion.12), channel_id=1, source_target_pairs={{0,12},{1,13},{2,14},{3,15},{4,8},{5,9},{6,10},{7,11},{8,4},{9,5},... | collective-permute-start | bytes 98312 | tf_op jit(solution)/shard_map/ppermute | solution.py:42
  170.6 8.1 %collective-permute-start.7 = (bf16[32,512]{1,0:T(8,128)(2,1)S(1)}, bf16[32,512]{1,0:T(8,128)(2,1)S(1)}, u32[]{:S(2)}, u32[]{:S(2)}) collective-permute-start(bf16[32,512]{1,0:T(8,128)(2,1)S(1)} %fusion.12), channel_id=1, source_target_pairs={{0,8},{1,9},{2,10},{3,11},{4,12},{5,13},{6,14},{7,15},{8,0},{9,1},... | collective-permute-start | bytes 98312 | tf_op jit(solution)/shard_map/ppermute | solution.py:42
  174.3 4.4 %collective-permute-start.6 = (bf16[32,512]{1,0:T(8,128)(2,1)S(1)}, bf16[32,512]{1,0:T(8,128)(2,1)S(1)}, u32[]{:S(2)}, u32[]{:S(2)}) collective-permute-start(bf16[32,512]{1,0:T(8,128)(2,1)S(1)} %fusion.12), channel_id=1, source_target_pairs={{0,4},{1,5},{2,6},{3,7},{4,0},{5,1},{6,2},{7,3},{8,12},{9,13},{10,... | collective-permute-start | bytes 98312 | tf_op jit(solution)/shard_map/ppermute | solution.py:42
  178.7 8.1 %copy-start.7 = (bf16[512,512]{0,1:T(8,128)(2,1)S(1)}, bf16[512,512]{0,1:T(8,128)(2,1)}, u32[]{:S(2)}) copy-start(bf16[512,512]{0,1:T(8,128)(2,1)} %fusion.2) | copy-start | bytes 1572868
  178.7 55.2 %all-to-all-start.3 = ((bf16[16,32,2048]{2,1,0:T(8,128)(2,1)}), bf16[16,32,2048]{2,1,0:T(8,128)(2,1)}, u32[]{:S(2)}, u32[]{:S(2)}) async-start(bf16[16,32,2048]{2,1,0:T(8,128)(2,1)} %bitcast.71), calls=%async_computation.3 | async-start | bytes 4194304 | tf_op jit(solution)/shard_map/all_to_all | solution.py:33
  195.8 11.0 %collective-permute-start.11 = (bf16[4,32,512]{2,1,0:T(8,128)(2,1)S(1)}, bf16[4,32,512]{2,1,0:T(8,128)(2,1)S(1)}, u32[]{:S(2)}, u32[]{:S(2)}) collective-permute-start(bf16[4,32,512]{2,1,0:T(8,128)(2,1)S(1)} %pad_maximum_fusion), channel_id=1, source_target_pairs={{0,3},{1,2},{2,1},{3,0},{4,7},{5,6},{6,5},{7,4},{8,11},{9,10},{10,... | collective-permute-start | bytes 393224 | tf_op jit(solution)/shard_map/ppermute | solution.py:47
  196.4 10.4 %collective-permute-start.10 = (bf16[4,32,512]{2,1,0:T(8,128)(2,1)S(1)}, bf16[4,32,512]{2,1,0:T(8,128)(2,1)S(1)}, u32[]{:S(2)}, u32[]{:S(2)}) collective-permute-start(bf16[4,32,512]{2,1,0:T(8,128)(2,1)S(1)} %pad_maximum_fusion), channel_id=1, source_target_pairs={{0,2},{1,3},{2,0},{3,1},{4,6},{5,7},{6,4},{7,5},{8,10},{9,11},{10,... | collective-permute-start | bytes 393224 | tf_op jit(solution)/shard_map/ppermute | solution.py:47
  197.6 1.4 collective-permute-start.9
  206.9 0.8 copy-start.1

commit v3 on v0

v3 whole, which is shorter than its diff:
```python
import functools
import math

import jax
import jax.numpy as jnp
from jax import lax
from jax.experimental import pallas as pl
from jax.experimental.pallas import tpu as pltpu
from jax.sharding import PartitionSpec as P

F32 = jnp.float32
BF16 = jnp.bfloat16
COLUMNS = 512
LIMIT = pltpu.CompilerParams(vmem_limit_bytes=40 * 1024 * 1024)


def split_kernel(share, core, *refs):
    *slabs, keep, send = refs
    mine = core[0] == 0
    at = 0
    for slab in slabs:
        for i in range(0, slab.shape[0], 2 * share):
            low, high = slab[i : i + share], slab[i + share : i + 2 * share]
            keep[at : at + share] = jnp.where(mine, low, high)
            send[at : at + share] = jnp.where(mine, high, low)
            at += share


def join_kernel(share, core, own, other, *slabs):
    mine = core[0] == 0
    at = 0
    for slab in slabs:
        for i in range(0, slab.shape[0], 2 * share):
            a, b = own[at : at + share], other[at : at + share]
            slab[i : i + share] = jnp.where(mine, a, b)
            slab[i + share : i + 2 * share] = jnp.where(mine, b, a)
            at += share


def mix_kernel(matrix, own, other, own_out, other_out):
    rows = jnp.concatenate([own[...], other[...]], axis=0)
    half = own.shape[0]
    own_out[...] = jnp.dot(matrix[:half], rows, preferred_element_type=F32).astype(BF16)
    other_out[...] = jnp.dot(matrix[half:], rows, preferred_element_type=F32).astype(BF16)


def place_kernel(starts, a, *refs):
    *slabs, out = refs
    for i, slab in enumerate(slabs):
        at = pl.ds(pl.multiple_of(starts[i], slab.shape[0]), slab.shape[0])
        out[at] = a[at] * slab[...]


def cut_kernel(matrix, rows, *slabs):
    total = jnp.dot(matrix[...], rows[...], preferred_element_type=F32).astype(BF16)
    at = 0
    for slab in slabs:
        slab[...] = total[at : at + slab.shape[0]]
        at += slab.shape[0]


def whole_kernel(matrix, *refs):
    *slabs, out = refs
    rows = jnp.concatenate([s[...] for s in slabs], axis=0)
    out[...] = jnp.dot(matrix[...], rows, preferred_element_type=F32).astype(BF16)


def partial_kernel(order, right, *refs):
    *slabs, out, total = refs

    @pl.when(pl.program_id(0) == 0)
    def _():
        total[...] = jnp.zeros_like(total)

    left = jnp.concatenate([s[...] for s in slabs], axis=0)
    total[...] += lax.dot_general(
        left, right[...], (((1,), (1,)), ((), ())), preferred_element_type=F32
    )

    @pl.when(pl.program_id(0) == pl.num_programs(0) - 1)
    def _():
        out[...] = jnp.dot(
            order[...], total[...].astype(BF16), preferred_element_type=F32
        ).astype(BF16)


def gradient_kernel(same, spread_out, *refs):
    g, h, m, n, out, total = refs

    @pl.when(pl.program_id(0) == 0)
    def _():
        total[...] = jnp.zeros_like(total)

    left = jnp.concatenate([g[...], h[...]], axis=0)
    right = jnp.concatenate([m[...], n[...]], axis=0)
    total[...] += lax.dot_general(
        left, right, (((1,), (1,)), ((), ())), preferred_element_type=F32
    )

    @pl.when(pl.program_id(0) == pl.num_programs(0) - 1)
    def _():
        out[...] = jnp.dot(
            total[...] * same[...].astype(F32),
            spread_out[...].astype(F32),
            precision=lax.Precision.HIGHEST,
            preferred_element_type=F32,
        )


def order_kernel(scale, position, *refs):
    *parts, out = refs
    at = 0
    for rows in parts:
        for i in range(rows.shape[0]):
            out[position[at]] = rows[i].astype(F32) * scale
            at += 1


def by_columns(kernel, ins, outs, width, scalars=(), whole=(), scratch=(), dtype=BF16):
    columns = min(COLUMNS, width)
    block = lambda rows: pl.BlockSpec((rows, columns), lambda i: (0, i))
    full = lambda shape: pl.BlockSpec(shape, lambda i: (0, 0))
    return pl.pallas_call(
        kernel,
        grid=(width // columns,),
        in_specs=[pl.BlockSpec(memory_space=pltpu.SMEM) for _ in scalars]
        + [full(x.shape) for x in whole]
        + [block(x.shape[0]) for x in ins],
        out_specs=[block(n) if isinstance(n, int) else full(n) for n in outs],
        out_shape=[
            jax.ShapeDtypeStruct((n, width) if isinstance(n, int) else n, dtype) for n in outs
        ],
        scratch_shapes=list(scratch),
        compiler_params=LIMIT,
    )(*scalars, *whole, *ins)


def in_order(position, parts, scale):
    _, share, n = parts[0].shape
    return pl.pallas_call(
        functools.partial(order_kernel, scale),
        in_specs=[pl.BlockSpec(memory_space=pltpu.SMEM)]
        + [pl.BlockSpec(memory_space=pltpu.VMEM) for _ in parts],
        out_specs=pl.BlockSpec(memory_space=pltpu.VMEM),
        out_shape=jax.ShapeDtypeStruct((sum(x.shape[0] for x in parts), share, n), F32),
        compiler_params=LIMIT,
    )(position, *parts)


def tree_sum(terms):
    terms = [t.astype(F32) for t in terms]
    while len(terms) > 1:
        terms = [a + b for a, b in zip(terms[::2], terms[1::2])]
    return terms[0].astype(BF16)


def per_device(signal, gate_input, cotangent, block_factor, cross_factor, order_table):
    count = lax.axis_size("seq")
    block, width = signal.shape
    share = block // count
    chips, slab = count // 2, 2 * share
    far = chips // 2
    me = lax.axis_index("seq")
    h, e = me // 2, me % 2
    core = e.reshape(1).astype(jnp.int32)
    true = order_table[0] >= 0

    def phase(f, *args):
        shapes = jax.eval_shape(f, *args)
        none = lambda *a: jax.tree.map(lambda s: jnp.zeros(s.shape, s.dtype), shapes)
        return lax.cond(true, f, none, *args)

    def chip(x, k):
        return lax.ppermute(x, "seq", [(s, s ^ (2 * k)) for s in range(count)])

    def sibling(x):
        return lax.ppermute(x, "seq", [(s, s ^ 1) for s in range(count)])

    cross_ks = list(range(far, chips))
    side_groups = [
        [(g * far + j) * 2 + c for j in range(far)] for g in range(2) for c in range(2)
    ]
    side_size = far * slab
    side_start = h // far * side_size
    sizes = [side_size] + [slab] * far

    def send_cross(slabs):
        return {k: chip(slabs[k], k) for k in slabs}

    def send_side(x):
        return lax.all_to_all(
            x, "seq", split_axis=0, concat_axis=0, tiled=True, axis_index_groups=side_groups
        )

    def chip_rows(x, k):
        return lax.dynamic_slice_in_dim(x, jnp.bitwise_xor(h, k) * slab, slab, 0)

    def side_rows(x):
        return lax.dynamic_slice_in_dim(x, side_start, side_size, 0)

    half = chips * share

    def turn(slabs, matrix, side):
        side = send_side(side)
        keep, send = by_columns(functools.partial(split_kernel, share), slabs, [half, half], width, [core])
        other = sibling(send)
        own_out, other_out = by_columns(mix_kernel, [keep, other], [half, half], width, (), [matrix])
        other_in = sibling(other_out)
        sent = by_columns(
            functools.partial(join_kernel, share), [own_out, other_in], sizes, width, [core]
        )
        return side, list(sent), keep, other

    def after(x, earlier):
        return lax.optimization_barrier((x, earlier))

    grads = {k: chip_rows(cotangent, k) * chip_rows(gate_input, k) for k in cross_ks}
    grads, later = after(grads, (cotangent, gate_input, signal))
    side = side_rows(later[0]) * side_rows(later[1])
    grads = send_cross(grads)

    def hot(of, n):
        return (of[:, None] == jnp.arange(n, dtype=jnp.int32)[None, :]).astype(BF16)

    every = jnp.arange(count, dtype=jnp.int32)
    ks = jnp.arange(chips, dtype=jnp.int32)
    order = jnp.where(ks < far, h // far * far + ks, jnp.bitwise_xor(h, ks))
    held = jnp.tile(order, 2) * 2 + jnp.bitwise_xor(e, every // chips)
    relative = jnp.where(ks < far, jnp.bitwise_xor(h % far, ks), ks)
    at = jnp.arange(block, dtype=jnp.int32) % share
    same = at[:, None] == at[None, :]

    def prepare(side, signal, block_factor, cross_factor, order_table, held, order, relative):
        side = send_side(side)
        one_hot = hot(order_table, block)
        permuted = jnp.dot(one_hot, signal, preferred_element_type=F32).astype(BF16)
        within = jnp.tile(jnp.arange(slab, dtype=jnp.int32), chips)
        rows = lambda of: hot(jnp.repeat(of, slab) * slab + within, block)
        factor = jnp.dot(rows(order), block_factor, preferred_element_type=F32).astype(BF16)
        mixed = by_columns(cut_kernel, [permuted], sizes, width, (), [factor])
        home = lax.dot_general(
            one_hot, factor, (((0,), (1,)), ((), ())), preferred_element_type=F32
        ).astype(BF16)
        chosen = hot(held, count)
        near = jnp.einsum("bi,pij->bpj", chosen, cross_factor, preferred_element_type=F32)
        spread_out = jnp.repeat(chosen, share, axis=0)
        cross = jnp.dot(
            near.astype(BF16).reshape(block, count), spread_out.T, preferred_element_type=F32
        )
        cross = jnp.where(same, cross, 0.0).astype(BF16)
        return side, list(mixed), permuted, home, cross, cross.T, chosen, spread_out, rows(relative)

    side, mixed, permuted, home_factor, cross, cross_t, chosen, spread_out, reorder = phase(
        prepare, side, later[2], block_factor, cross_factor, order_table, held, order, relative
    )

    mixed, grads, side = lax.optimization_barrier((mixed, grads, side))
    grads = [side] + [grads[k] for k in cross_ks]
    got = send_cross(dict(zip(cross_ks, mixed[1:])))
    side, back, *grad_rows = phase(turn, grads, cross_t, mixed[0])
    back, got, side = lax.optimization_barrier((back, got, side))
    mixed = [side] + [got[k] for k in cross_ks]

    got = send_cross(dict(zip(cross_ks, back[1:])))
    def cross_gradient(rows, same, chosen, spread_out):
        products = by_columns(
            gradient_kernel,
            rows,
            [(block, count)],
            width,
            whole=[same.astype(BF16), spread_out],
            scratch=[pltpu.VMEM((block, block), F32)],
            dtype=F32,
        )[0]
        return jnp.einsum(
            "bi,bpj->pij",
            chosen.astype(F32),
            products.reshape(count, share, count),
            precision=lax.Precision.HIGHEST,
        ) / math.sqrt(width)

    def turn_and_gradient(slabs, matrix, side, grad_rows, *rest):
        side, sent, *mixed_rows = turn(slabs, matrix, side)
        return side, sent, cross_gradient(grad_rows + mixed_rows, *rest)

    side, gated, grad_cross = phase(
        turn_and_gradient, mixed, cross, back[0], grad_rows, same, chosen, spread_out
    )
    got, side, gated = lax.optimization_barrier((got, side, gated))
    backs = [side] + [got[k] for k in cross_ks]

    gateds = dict(zip(cross_ks, gated[1:]))
    first, second = cross_ks[far // 2 :], cross_ks[: far // 2]
    arrived = send_cross({k: gateds[k] for k in first})

    def home(backs, permuted, home_factor, reorder):
        terms = by_columns(
            partial_kernel,
            [permuted] + backs,
            [(block, block)],
            width,
            whole=[reorder],
            scratch=[pltpu.VMEM((block, block), F32)],
        )[0]
        terms = terms.reshape(chips, 2, share, block)
        mine = lambda i: lax.dynamic_index_in_dim(terms, jnp.bitwise_xor(e, i), 1, keepdims=False)
        terms = tree_sum([mine(0), sibling(mine(1))]).reshape(far, 2, share, block)
        terms = tree_sum([terms[:, 0], chip(terms[:, 1], 1)])
        own = tree_sum([terms[0]] + [chip(terms[k], 2 * k) for k in range(1, far)])
        grad_signal = by_columns(whole_kernel, backs, [block], width, (), [home_factor])[0]
        return own, grad_signal

    own, grad_signal = phase(home, backs, permuted, home_factor, reorder)
    (side, rest), arrived, own = lax.optimization_barrier(
        ((gated[0], {k: gateds[k] for k in second}), arrived, own)
    )
    arrived.update(send_cross({k: rest[k] for k in second[far // 4 :]}))
    side = send_side(side)
    got = [own] + [chip(own, 2 * k) for k in range(1, far)]
    rest, got = after({k: rest[k] for k in second[: far // 4]}, got)
    arrived.update(send_cross(rest))

    def all_rows(got, position):
        near = jnp.stack(got)
        parts = [near, chip(near, 1)]
        parts += [sibling(x) for x in parts]
        return in_order(position, parts, 1.0 / math.sqrt(count * width)).reshape(block, block)

    k = (every % far) * 2 + every // far % 2
    position = jnp.bitwise_xor(h, k) * 2 + jnp.bitwise_xor(e, every // chips)
    grad_block = phase(all_rows, got, position.astype(jnp.int32))
    arrived, side, grad_block = lax.optimization_barrier((arrived, side, grad_block))
    starts = [side_start] + [jnp.bitwise_xor(h, k) * slab for k in cross_ks]
    slabs = [side] + [arrived[k] for k in cross_ks]
    if slab % 16 == 0:
        grad_gate = by_columns(
            place_kernel, [cotangent] + slabs, [block], width, [jnp.stack(starts).astype(jnp.int32)]
        )[0]
    else:
        grad_gate = jnp.zeros_like(cotangent)
        for start, x in zip(starts, slabs):
            rows = lax.dynamic_slice_in_dim(cotangent, start, x.shape[0], 0) * x
            grad_gate = lax.dynamic_update_slice_in_dim(grad_gate, rows, start, 0)
    return (grad_signal, grad_gate, grad_block, grad_cross)


def solution(mesh):
    in_specs = (
        P(("groups", "seq"), None),
        P(("groups", "seq"), None),
        P(("groups", "seq"), None),
        P(),
        P("seq", None, None),
        P(),
    )
    out_specs = (
        P(("groups", "seq"), None),
        P(("groups", "seq"), None),
        P("groups", None),
        P("seq", "groups", None),
    )
    return jax.shard_map(
        per_device, mesh=mesh, in_specs=in_specs, out_specs=out_specs, check_vma=False
    )
```

time: 410 us -> 222 us (0.54)
  blocking collectives: 163 us -> 0 us
  local copies, waits for them, and re-layouts: 57.6 us -> 3.85 us
  starting transfers between devices: 7.56 us -> 60.4 us
  Pallas kernels: 0 us -> 42 us
  other arithmetic: 33.1 us -> 7.13 us
  waiting for transfers between devices: 115 us -> 97.9 us
  between operations: 14.2 us -> 1.61 us
  matrix products: 18.5 us -> 8.01 us
    all_to_all x3 -> x0, blocking collectives: 163 us -> none  [the longest x1 58.6 us: per_device(): lax.all_to_all(gated, 'seq', split_axis=0, concat_axis=1, tiled=True)]
    psum x1 -> x0, waiting for transfers between devices: 74.5 us -> none  [per_device(): grad_block = lax.psum(partial_block, 'seq') / math.sqrt(count * width)]
    ppermute x0 -> x31, starting transfers between devices: none -> 44.1 us  [the longest x24 42.9 us: chip(): return lax.ppermute(x, 'seq', [(s, s ^ 2 * k) for s in range(count)])]
    pallas_call x0 -> x12, Pallas kernels: none -> 42 us  [the longest x11 41.3 us: by_columns(): pl.pallas_call(kernel, grid=(width // columns,), in_specs=[pl.BlockSpec(m...]
    ppermute x0 -> x31, waiting for transfers between devices: none -> 35.7 us  [the longest x24 30.6 us: chip(): return lax.ppermute(x, 'seq', [(s, s ^ 2 * k) for s in range(count)])]
    unnamed x31 -> x14, local copies, waits for them, and re-layouts: 28.9 us -> 0.03 us
    unnamed x2 -> x0, other arithmetic: 26.3 us -> none
    all_to_all x1 -> x4, waiting for transfers between devices: 40.9 us -> 62.2 us  [send_side(): lax.all_to_all(x, 'seq', split_axis=0, concat_axis=0, tiled=True, axis_in...]
  transfers between devices with their start and end apart: 2 -> 35, of which waited for: 2 -> 10; matrix products, arithmetic and copies ran while one was open for 5% -> 7% of each run, Pallas kernels for 0% -> 17%
where the time goes in v3:
time: 222 us; the launch traced here: 221 us
  waiting for transfers between devices  97.9 us (44%)
  starting transfers between devices  60.4 us (27%)
  Pallas kernels  42 us (19%)
  matrix products  8.01 us (4%)
  other arithmetic  7.13 us (3%)
  local copies, waits for them, and re-layouts  3.85 us (2%)
    all_to_all x4, waiting for transfers between devices, send_side(): lax.all_to_all(x, 'seq', split_axis=0, concat_axis=0, tiled=True, axis_in...  62.2 us
    ppermute x24, starting transfers between devices, chip(): return lax.ppermute(x, 'seq', [(s, s ^ 2 * k) for s in range(count)])  42.9 us
    pallas_call x11, Pallas kernels, by_columns(): pl.pallas_call(kernel, grid=(width // columns,), in_specs=[pl.BlockSpec(m...  41.3 us
    ppermute x24, waiting for transfers between devices, chip(): return lax.ppermute(x, 'seq', [(s, s ^ 2 * k) for s in range(count)])  30.6 us
    all_to_all x4, starting transfers between devices, send_side(): lax.all_to_all(x, 'seq', split_axis=0, concat_axis=0, tiled=True, axis_in...  16.3 us
    ppermute x7, waiting for transfers between devices, sibling(): return lax.ppermute(x, 'seq', [(s, s ^ 1) for s in range(count)])  5.13 us
  transfers between devices with their start and end apart: 35, of which 10 were waited for; matrix products, arithmetic and copies ran while one was open for 7% of the time, Pallas kernels for 17%

profile of v3, /device:TPU:0, one launch (start us, length us, event | category | flops | bytes accessed | tf_op | source)
XLA Modules:
  0.0 221.2 jit_solution(7623297985007697167)
XLA Ops:
  0.7 2.9 %dynamic-slice_multiply_fusion.1 = (bf16[64,2048]{1,0:T(8,128)(2,1)}, bf16[64,2048]{1,0:T(8,128)(2,1)}, bf16[64,2048]{1,0:T(8,128)(2,1)}, bf16[64,2048]{1,0:T(8,128)(2,1)}) fusion(bf16[512,2048]{1,0:T(8,128)(2,1)} %param.17, s32[]{:T(128)S(6)} %select_n.107, bf16[512,2048]{1,0:T(8,128)(2,1)} %a.1, s32[]{:T(128)S(6)} %select_n.106, s32[]{:T(128)S(6)} %select_n.105, ...), kind=kLoop, calls=%fused_computation.58 | loop fusion | flops 2097152 | bytes 3145744 | tf_op jit(solution)/shard_map/mul | solution.py:217
  3.6 4.0 %collective-permute-start.12 = (bf16[64,2048]{1,0:T(8,128)(2,1)}, bf16[64,2048]{1,0:T(8,128)(2,1)}, u32[]{:S(2)}, u32[]{:S(2)}) collective-permute-start(bf16[64,2048]{1,0:T(8,128)(2,1)} %get-tuple-element.406), channel_id=1, source_target_pairs={{0,8},{1,9},{2,10},{3,11},{4,12},{5,13},{6,14},{7,15},{8,0},{9,1},... | collective-permute-start | bytes 786440 | tf_op jit(solution)/shard_map/ppermute | solution.py:174
  8.9 3.6 %collective-permute-start.14 = (bf16[64,2048]{1,0:T(8,128)(2,1)}, bf16[64,2048]{1,0:T(8,128)(2,1)}, u32[]{:S(2)}, u32[]{:S(2)}) collective-permute-start(bf16[64,2048]{1,0:T(8,128)(2,1)} %get-tuple-element.408), channel_id=1, source_target_pairs={{0,12},{1,13},{2,14},{3,15},{4,8},{5,9},{6,10},{7,11},{8,4},{9,5},... | collective-permute-start | bytes 786440 | tf_op jit(solution)/shard_map/ppermute | solution.py:174
  14.0 39.6 %conditional.5 = (bf16[256,2048]{1,0:T(8,128)(2,1)}, bf16[256,2048]{1,0:T(8,128)(2,1)}, bf16[64,2048]{1,0:T(8,128)(2,1)}, bf16[64,2048]{1,0:T(8,128)(2,1)}, bf16...) conditional(s32[]{:T(128)} %bitcast.28, () %tuple.58, ...), branch_computations={%region_0.1_spmd, %region_1.2_spmd} | conditional | flops 1625040768 | bytes 23468344 | solution.py:171
  14.0 2.7 %dynamic-slice_multiply_fusion = bf16[256,2048]{1,0:T(8,128)(2,1)} fusion(bf16[512,2048]{1,0:T(8,128)(2,1)} %get-tuple-element.224, s32[]{:T(128)S(6)} %select_n.81, bf16[512,2048]{1,0:T(8,128)(2,1)S(1)} %get-tuple-element.222), kind=kLoop, calls=%fused_computation.10 | loop fusion | flops 2097152 | bytes 3145732 | tf_op jit(solution)/shard_map/mul | solution.py:219
  16.8 4.2 %all-to-all-start.2 = ((bf16[4,64,2048]{2,1,0:T(8,128)(2,1)}), bf16[4,64,2048]{2,1,0:T(8,128)(2,1)}, u32[]{:S(2)}, u32[]{:S(2)}) async-start(bf16[4,64,2048]{2,1,0:T(8,128)(2,1)} %bitcast), calls=%async_computation.2 | async-start | bytes 2097152 | tf_op jit(solution)/shard_map/cond/branch_1_fun/all_to_all | solution.py:191
  23.8 2.1 fusion
  26.9 1.5 convolution_convert_fusion.2.matrix
  28.4 2.6 %convolution_convert_fusion.rows = bf16[512,2048]{1,0:T(8,128)(2,1)} fusion(bf16[512,2048]{1,0:T(8,128)(2,1)S(1)} %copy-done.7, s32[512]{0:T(512)S(1)} %get-tuple-element.231), kind=kOutput, calls=%fused_computation | convolution fusion | flops 1075052544 | bytes 4196352 | tf_op jit(solution)/shard_map/cond/branch_1_fun/dot_general | solution.py:236
  31.1 4.4 %branch_1_fun.11 = (bf16[256,2048]{1,0:T(8,128)(2,1)}, bf16[64,2048]{1,0:T(8,128)(2,1)}, bf16[64,2048]{1,0:T(8,128)(2,1)}, bf16[64,2048]{1,0:T(8,128)(2,1)}, bf16[64,2048]{1,0:T(8,128)(2,1)}) custom-call(bf16[512,512]{1,0:T(8,128)(2,1)S(1)} %convolution_convert_fusion.2.matrix, bf16[512,2048]{1,0:T(8,128)(2,1)} %convolution_convert_fusion.rows), custom_call_target="tpu_custom_call" | custom-call | tf_op jit(solution)/shard_map/cond/branch_1_fun/pallas_call | solution.py:123
  36.3 17.3 %all-to-all-done.2 = bf16[4,64,2048]{2,1,0:T(8,128)(2,1)} async-done(((bf16[4,64,2048]{2,1,0:T(8,128)(2,1)}), bf16[4,64,2048]{2,1,0:T(8,128)(2,1)}, u32[]{:S(2)}, u32[]{:S(2)}) %all-to-all-start.2) | async-done | bytes 1048608 | tf_op jit(solution)/shard_map/cond/branch_1_fun/all_to_all | solution.py:191
  53.6 3.6 %collective-permute-start.16 = (bf16[64,2048]{1,0:T(8,128)(2,1)}, bf16[64,2048]{1,0:T(8,128)(2,1)S(1)}, u32[]{:S(2)}, u32[]{:S(2)}) collective-permute-start(bf16[64,2048]{1,0:T(8,128)(2,1)} %get-tuple-element.423), channel_id=1, source_target_pairs={{0,8},{1,9},{2,10},{3,11},{4,12},{5,13},{6,14},{7,15},{8,0},{9,1},... | collective-permute-start | bytes 786440 | tf_op jit(solution)/shard_map/ppermute | solution.py:174
  57.6 3.4 %collective-permute-start.18 = (bf16[64,2048]{1,0:T(8,128)(2,1)}, bf16[64,2048]{1,0:T(8,128)(2,1)}, u32[]{:S(2)}, u32[]{:S(2)}) collective-permute-start(bf16[64,2048]{1,0:T(8,128)(2,1)} %get-tuple-element.425), channel_id=1, source_target_pairs={{0,12},{1,13},{2,14},{3,15},{4,8},{5,9},{6,10},{7,11},{8,4},{9,5},... | collective-permute-start | bytes 786440 | tf_op jit(solution)/shard_map/ppermute | solution.py:174
  62.0 41.1 %conditional.6 = (bf16[256,2048]{1,0:T(8,128)(2,1)}, bf16[256,2048]{1,0:T(8,128)(2,1)}, bf16[64,2048]{1,0:T(8,128)(2,1)}, bf16[64,2048]{1,0:T(8,128)(2,1)}, bf16...) conditional(s32[]{:T(128)} %bitcast.28, () %tuple.61, ...), branch_computations={%region_2.3_spmd, %region_3.4_spmd} | conditional | bytes 12583088 | solution.py:171
  62.0 3.6 %branch_1_fun.12 = (bf16[256,2048]{1,0:T(8,128)(2,1)}, bf16[256,2048]{1,0:T(8,128)(2,1)S(1)}) custom-call(s32[1]{0:T(128)} %get-tuple-element.250.core, bf16[256,2048]{1,0:T(8,128)(2,1)} %get-tuple-element.252.refs_0_, bf16[64,2048]{1,0:T(8,128)(2,1)} %get-tuple-element.253.refs_1_, bf16[64,2048]{1,0:T(8,128)(2,1)} %get-tuple-element.254.refs_2_, ...), custom_call_target="tpu_custom_call" | custom-call | tf_op jit(solution)/shard_map/cond/branch_1_fun/pallas_call | solution.py:123
  65.6 4.3 %all-to-all-start = ((bf16[4,64,2048]{2,1,0:T(8,128)(2,1)}), bf16[4,64,2048]{2,1,0:T(8,128)(2,1)}, u32[]{:S(2)}, u32[]{:S(2)}) async-start(bf16[4,64,2048]{2,1,0:T(8,128)(2,1)} %bitcast.6), calls=%async_computation | async-start | bytes 2097152 | tf_op jit(solution)/shard_map/cond/branch_1_fun/all_to_all | solution.py:191
  70.1 3.5 %branch_1_fun.13 = (bf16[256,2048]{1,0:T(8,128)(2,1)S(1)}, bf16[256,2048]{1,0:T(8,128)(2,1)S(1)}) custom-call(bf16[512,512]{1,0:T(8,128)(2,1)S(1)} %copy.23.matrix, bf16[256,2048]{1,0:T(8,128)(2,1)} %get-tuple-element.667.own, bf16[256,2048]{1,0:T(8,128)(2,1)} %collective-permute-done.other), custom_call_target="tpu_custom_call" | custom-call | tf_op jit(solution)/shard_map/cond/branch_1_fun/pallas_call | solution.py:123
  74.2 2.3 %collective-permute-done.1.other = bf16[256,2048]{1,0:T(8,128)(2,1)S(1)} collective-permute-done((bf16[256,2048]{1,0:T(8,128)(2,1)S(1)}, bf16[256,2048]{1,0:T(8,128)(2,1)S(1)}, u32[]{:S(2)}, u32[]{:S(2)}) %collective-permute-start.1) | collective-permute-done | bytes 1048608 | tf_op jit(solution)/shard_map/cond/branch_1_fun/ppermute | solution.py:177
  76.5 2.0 branch_1_fun.14
  78.5 24.6 %all-to-all-done = bf16[4,64,2048]{2,1,0:T(8,128)(2,1)} async-done(((bf16[4,64,2048]{2,1,0:T(8,128)(2,1)}), bf16[4,64,2048]{2,1,0:T(8,128)(2,1)}, u32[]{:S(2)}, u32[]{:S(2)}) %all-to-all-start) | async-done | bytes 1048608 | tf_op jit(solution)/shard_map/cond/branch_1_fun/all_to_all | solution.py:191
  103.1 2.9 %collective-permute-start.20 = (bf16[64,2048]{1,0:T(8,128)(2,1)}, bf16[64,2048]{1,0:T(8,128)(2,1)}, u32[]{:S(2)}, u32[]{:S(2)}) collective-permute-start(bf16[64,2048]{1,0:T(8,128)(2,1)} %get-tuple-element.428), channel_id=1, source_target_pairs={{0,8},{1,9},{2,10},{3,11},{4,12},{5,13},{6,14},{7,15},{8,0},{9,1},... | collective-permute-start | bytes 786440 | tf_op jit(solution)/shard_map/ppermute | solution.py:174
  106.5 3.4 %collective-permute-start.22 = (bf16[64,2048]{1,0:T(8,128)(2,1)}, bf16[64,2048]{1,0:T(8,128)(2,1)}, u32[]{:S(2)}, u32[]{:S(2)}) collective-permute-start(bf16[64,2048]{1,0:T(8,128)(2,1)} %get-tuple-element.430), channel_id=1, source_target_pairs={{0,12},{1,13},{2,14},{3,15},{4,8},{5,9},{6,10},{7,11},{8,4},{9,5},... | collective-permute-start | bytes 786440 | tf_op jit(solution)/shard_map/ppermute | solution.py:174
  110.8 41.1 %conditional.7 = (bf16[256,2048]{1,0:T(8,128)(2,1)}, bf16[256,2048]{1,0:T(8,128)(2,1)}, bf16[64,2048]{1,0:T(8,128)(2,1)}, bf16[64,2048]{1,0:T(8,128)(2,1)}, bf16...) conditional(s32[]{:T(128)} %bitcast.28, () %tuple.65, ...), branch_computations={%region_4.5_spmd, %region_5.6_spmd} | conditional | flops 1843200 | bytes 12518056 | solution.py:171
  110.8 2.3 %branch_1_fun.15 = (bf16[256,2048]{1,0:T(8,128)(2,1)S(1)}, bf16[256,2048]{1,0:T(8,128)(2,1)S(1)}) custom-call(s32[1]{0:T(128)} %get-tuple-element.267.core, bf16[256,2048]{1,0:T(8,128)(2,1)} %get-tuple-element.269.refs_0_, bf16[64,2048]{1,0:T(8,128)(2,1)S(1)} %get-tuple-element.270.refs_1_, bf16[64,2048]{1,0:T(8,128)(2,1)S(1)} %get-tuple-element.271.refs_2_, ...), custom_call_target="tpu_custom_call" | custom-call | tf_op jit(solution)/shard_map/cond/branch_1_fun/pallas_call | solution.py:123
  113.2 4.3 %all-to-all-start.1 = ((bf16[4,64,2048]{2,1,0:T(8,128)(2,1)}), bf16[4,64,2048]{2,1,0:T(8,128)(2,1)}, u32[]{:S(2)}, u32[]{:S(2)}) async-start(bf16[4,64,2048]{2,1,0:T(8,128)(2,1)} %bitcast.74), calls=%async_computation.1 | async-start | bytes 2097152 | tf_op jit(solution)/shard_map/cond/branch_1_fun/all_to_all | solution.py:191
  117.4 3.9 %branch_1_fun.16 = (bf16[256,2048]{1,0:T(8,128)(2,1)S(1)}, bf16[256,2048]{1,0:T(8,128)(2,1)}) custom-call(bf16[512,512]{1,0:T(8,128)(2,1)} %get-tuple-element.268.matrix, bf16[256,2048]{1,0:T(8,128)(2,1)S(1)} %get-tuple-element.274.own.refs_2_, bf16[256,2048]{1,0:T(8,128)(2,1)S(1)} %collective-permute-done.10.other.refs_3_), custom_call_target="tpu_custom_call" | custom-call | tf_op jit(solution)/shard_map/cond/branch_1_fun/pallas_call | solution.py:123
  122.0 4.8 %branch_1_fun.18 = f32[512,16]{1,0:T(8,128)S(1)} custom-call(bf16[512,512]{1,0:T(8,128)(2,1)S(1)} %convert_element_type.62.same, bf16[512,16]{1,0:T(8,128)(2,1)} %get-tuple-element.284.spread_out, bf16[256,2048]{1,0:T(8,128)(2,1)} %get-tuple-element.285.refs_0_, bf16[256,2048]{1,0:T(8,128)(2,1)} %get-tuple-element.286.refs_1_, ...), custom_call_target="tpu_custom_call" | custom-call | tf_op jit(solution)/shard_map/cond/branch_1_fun/pallas_call | solution.py:123
  127.9 3.6 %branch_1_fun.17 = (bf16[256,2048]{1,0:T(8,128)(2,1)}, bf16[64,2048]{1,0:T(8,128)(2,1)}, bf16[64,2048]{1,0:T(8,128)(2,1)}, bf16[64,2048]{1,0:T(8,128)(2,1)}, bf16[64,2048]{1,0:T(8,128)(2,1)}) custom-call(s32[1]{0:T(128)} %get-tuple-element.267.core, bf16[256,2048]{1,0:T(8,128)(2,1)S(1)} %get-tuple-element.276.own, ...), custom_call_target="tpu_custom_call" | custom-call | tf_op jit(solution)/shard_map/cond/branch_1_fun/pallas_call | solution.py:123
  131.6 20.3 %all-to-all-done.1 = bf16[4,64,2048]{2,1,0:T(8,128)(2,1)} async-done(((bf16[4,64,2048]{2,1,0:T(8,128)(2,1)}), bf16[4,64,2048]{2,1,0:T(8,128)(2,1)}, u32[]{:S(2)}, u32[]{:S(2)}) %all-to-all-start.1) | async-done | bytes 1048608 | tf_op jit(solution)/shard_map/cond/branch_1_fun/all_to_all | solution.py:191
  151.9 2.0 collective-permute-start.24
  154.0 2.5 %collective-permute-start.25 = (bf16[64,2048]{1,0:T(8,128)(2,1)}, bf16[64,2048]{1,0:T(8,128)(2,1)S(1)}, u32[]{:S(2)}, u32[]{:S(2)}) collective-permute-start(bf16[64,2048]{1,0:T(8,128)(2,1)} %get-tuple-element.460), channel_id=1, source_target_pairs={{0,14},{1,15},{2,12},{3,13},{4,10},{5,11},{6,8},{7,9},{8,6},{9,7},... | collective-permute-start | bytes 786440 | tf_op jit(solution)/shard_map/ppermute | solution.py:174
  156.4 24.1 %conditional.8 = (bf16[32,512]{1,0:T(8,128)(2,1)S(1)}, bf16[512,2048]{1,0:T(8,128)(2,1)}) conditional(s32[]{:T(128)} %bitcast.28, () %tuple.57, (bf16[512,512]{1,0:T(8,128)(2,1)}, bf16[512,2048]{1,0:T(8,128)(2,1)}, bf16[256,2048]{1,0:T(8,128)(2,1)}, bf16[64,2048]{1,0:T(8,128)(2,1)}, bf16[64,2048]{1,0:T(8,128)(2,1)}, ...), branch_computations={%region_6.7_spmd, %region_7.8_spmd} | conditional | flops 917511 | bytes 6390092 | solution.py:171
  156.4 4.7 %branch_1_fun.19 = bf16[512,512]{1,0:T(8,128)(2,1)S(1)} custom-call(bf16[512,512]{1,0:T(8,128)(2,1)} %get-tuple-element.288.order, bf16[512,2048]{1,0:T(8,128)(2,1)} %get-tuple-element.289.right, bf16[256,2048]{1,0:T(8,128)(2,1)} %get-tuple-element.290.refs_0_, bf16[64,2048]{1,0:T(8,128)(2,1)} %get-tuple-element.291.refs_1_, ...), custom_call_target="tpu_custom_call" | custom-call | tf_op jit(solution)/shard_map/cond/branch_1_fun/pallas_call | solution.py:123
  161.3 1.5 collective-permute-done.2
  163.8 7.6 %collective-permute-done.3 = bf16[4,32,512]{2,1,0:T(8,128)(2,1)S(1)} collective-permute-done((bf16[4,32,512]{2,1,0:T(8,128)(2,1)S(1)}, bf16[4,32,512]{2,1,0:T(8,128)(2,1)S(1)}, u32[]{:S(2)}, u32[]{:S(2)}) %collective-permute-start.3) | collective-permute-done | bytes 131104 | tf_op jit(solution)/shard_map/cond/branch_1_fun/ppermute | solution.py:174
  171.5 2.8 %collective-permute-start.5 = (bf16[32,512]{1,0:T(8,128)(2,1)S(1)}, bf16[32,512]{1,0:T(8,128)(2,1)S(1)}, u32[]{:S(2)}, u32[]{:S(2)}) collective-permute-start(bf16[32,512]{1,0:T(8,128)(2,1)S(1)} %get-tuple-element.622), channel_id=1, source_target_pairs={{0,8},{1,9},{2,10},{3,11},{4,12},{5,13},{6,14},{7,15},{8,0},{9,1},... | collective-permute-start | bytes 98312 | tf_op jit(solution)/shard_map/cond/branch_1_fun/ppermute | solution.py:174
  174.3 1.6 collective-permute-start.6
  175.9 4.5 %branch_1_fun.20 = bf16[512,2048]{1,0:T(8,128)(2,1)} custom-call(bf16[512,512]{1,0:T(8,128)(2,1)S(1)} %copy-done.2, bf16[256,2048]{1,0:T(8,128)(2,1)} %get-tuple-element.290.refs_0_, bf16[64,2048]{1,0:T(8,128)(2,1)} %get-tuple-element.291.refs_1_, bf16[64,2048]{1,0:T(8,128)(2,1)} %get-tuple-element.292.refs_2_, bf16[64,2048]{1,0:T(8,128)(2,1)} %get-tuple-element.293.refs_3_, ...), custom_call_target="tpu_custom_call" | custom-call | tf_op jit(solution)/shard_map/cond/branch_1_fun/pallas_call | solution.py:123
  180.5 3.5 %all-to-all-start.3 = ((bf16[4,64,2048]{2,1,0:T(8,128)(2,1)}), bf16[4,64,2048]{2,1,0:T(8,128)(2,1)S(1)}, u32[]{:S(2)}, u32[]{:S(2)}) async-start(bf16[4,64,2048]{2,1,0:T(8,128)(2,1)} %bitcast.35), calls=%async_computation.3 | async-start | bytes 2097152 | tf_op jit(solution)/shard_map/all_to_all | solution.py:191
  184.1 2.0 collective-permute-start.26
  186.0 1.6 collective-permute-start.27
  188.5 2.0 collective-permute-start.30
  190.6 14.5 %collective-permute-done.26 = bf16[32,512]{1,0:T(8,128)(2,1)S(1)} collective-permute-done((bf16[32,512]{1,0:T(8,128)(2,1)S(1)}, bf16[32,512]{1,0:T(8,128)(2,1)S(1)}, u32[]{:S(2)}, u32[]{:S(2)}) %collective-permute-start.26) | collective-permute-done | bytes 32800 | tf_op jit(solution)/shard_map/ppermute | solution.py:174
  205.2 7.1 %conditional.9 = (f32[512,512]{1,0:T(8,128)S(1)}) conditional(s32[]{:T(128)} %bitcast.28, () %tuple.71, (s32[]{:T(128)}, s32[16]{0:T(128)S(1)}, s32[16]{0:T(128)S(1)}, pred[16]{0:T(512)(128)(4,1)S(1)}, s32[16]{0:T(128)S(1)}, /*index=5*/s32[16]{0:T(128)S(1)}, s32[16]{0:T(128)S(1)}, bf16[32,512]{1,0:T(8,128)(2,1)S(1)}, bf16[32,512]{1,0:T(8,128)(2,1)S(1)}, ...), branch_computations={%region_8.9_spmd, %region_9.10_spmd} | conditional | flops 197040 | bytes 1835796 | solution.py:171
  205.2 1.5 collective-permute-start.7
  206.8 3.5 %collective-permute-done.7.refs_1_ = bf16[4,32,512]{2,1,0:T(8,128)(2,1)S(1)} collective-permute-done((bf16[4,32,512]{2,1,0:T(8,128)(2,1)S(1)}, bf16[4,32,512]{2,1,0:T(8,128)(2,1)S(1)}, u32[]{:S(2)}, u32[]{:S(2)}) %collective-permute-start.7) | collective-permute-done | bytes 131104 | tf_op jit(solution)/shard_map/cond/branch_1_fun/ppermute | solution.py:174
  212.3 5.0 %collective-permute-done.29.refs_1_ = bf16[64,2048]{1,0:T(8,128)(2,1)S(1)} collective-permute-done((bf16[64,2048]{1,0:T(8,128)(2,1)}, bf16[64,2048]{1,0:T(8,128)(2,1)S(1)}, u32[]{:S(2)}, u32[]{:S(2)}) %collective-permute-start.29) | collective-permute-done | bytes 262176 | tf_op jit(solution)/shard_map/ppermute | solution.py:174
  217.3 3.9 %shard_map.95 = bf16[512,2048]{1,0:T(8,128)(2,1)} custom-call(s32[5]{0:T(128)S(1)} %stack.38.starts, bf16[512,2048]{1,0:T(8,128)(2,1)} %a.1, bf16[256,2048]{1,0:T(8,128)(2,1)S(1)} %bitcast.70, bf16[64,2048]{1,0:T(8,128)(2,1)S(1)} %collective-permute-done.29.refs_1_, bf16[64,2048]{1,0:T(8,128)(2,1)S(1)} %collective-permute-done.30.refs_2_, ...), custom_call_target="tpu_custom_call" | custom-call | tf_op jit(solution)/shard_map/pallas_call | solution.py:123
  (105 shorter events, 16.2 us)
Async XLA Ops:
  0.6 13.4 %copy-start = (bf16[512,2048]{1,0:T(8,128)(2,1)S(1)}, bf16[512,2048]{1,0:T(8,128)(2,1)}, u32[]{:S(2)}) copy-start(bf16[512,2048]{1,0:T(8,128)(2,1)} %a.1) | copy-start | bytes 6291460
  0.6 11.9 %copy-start.8 = (s32[512]{0:T(512)S(1)}, s32[512]{0:T(512)}, u32[]{:S(2)}) copy-start(s32[512]{0:T(512)} %param.21) | copy-start | bytes 6148
  0.7 13.3 %copy-start.6 = (bf16[32,16,16]{0,2,1:T(8,128)(2,1)S(1)}, bf16[32,16,16]{0,2,1:T(8,128)(2,1)}, u32[]{:S(2)}) copy-start(bf16[32,16,16]{0,2,1:T(8,128)(2,1)} %param.20) | copy-start | bytes 49156
  3.6 50.0 %collective-permute-start.12 = (bf16[64,2048]{1,0:T(8,128)(2,1)}, bf16[64,2048]{1,0:T(8,128)(2,1)}, u32[]{:S(2)}, u32[]{:S(2)}) collective-permute-start(bf16[64,2048]{1,0:T(8,128)(2,1)} %get-tuple-element.406), channel_id=1, source_target_pairs={{0,8},{1,9},{2,10},{3,11},{4,12},{5,13},{6,14},{7,15},{8,0},{9,1},... | collective-permute-start | bytes 786440 | tf_op jit(solution)/shard_map/ppermute | solution.py:174
  7.6 46.0 %collective-permute-start.13 = (bf16[64,2048]{1,0:T(8,128)(2,1)}, bf16[64,2048]{1,0:T(8,128)(2,1)}, u32[]{:S(2)}, u32[]{:S(2)}) collective-permute-start(bf16[64,2048]{1,0:T(8,128)(2,1)} %get-tuple-element.407), channel_id=1, source_target_pairs={{0,10},{1,11},{2,8},{3,9},{4,14},{5,15},{6,12},{7,13},{8,2},{9,3},... | collective-permute-start | bytes 786440 | tf_op jit(solution)/shard_map/ppermute | solution.py:174
  8.9 44.7 %collective-permute-start.14 = (bf16[64,2048]{1,0:T(8,128)(2,1)}, bf16[64,2048]{1,0:T(8,128)(2,1)}, u32[]{:S(2)}, u32[]{:S(2)}) collective-permute-start(bf16[64,2048]{1,0:T(8,128)(2,1)} %get-tuple-element.408), channel_id=1, source_target_pairs={{0,12},{1,13},{2,14},{3,15},{4,8},{5,9},{6,10},{7,11},{8,4},{9,5},... | collective-permute-start | bytes 786440 | tf_op jit(solution)/shard_map/ppermute | solution.py:174
  12.5 41.1 %collective-permute-start.15 = (bf16[64,2048]{1,0:T(8,128)(2,1)}, bf16[64,2048]{1,0:T(8,128)(2,1)}, u32[]{:S(2)}, u32[]{:S(2)}) collective-permute-start(bf16[64,2048]{1,0:T(8,128)(2,1)} %get-tuple-element.409), channel_id=1, source_target_pairs={{0,14},{1,15},{2,12},{3,13},{4,10},{5,11},{6,8},{7,9},{8,6},{9,7},... | collective-permute-start | bytes 786440 | tf_op jit(solution)/shard_map/ppermute | solution.py:174
  16.8 36.8 %all-to-all-start.2 = ((bf16[4,64,2048]{2,1,0:T(8,128)(2,1)}), bf16[4,64,2048]{2,1,0:T(8,128)(2,1)}, u32[]{:S(2)}, u32[]{:S(2)}) async-start(bf16[4,64,2048]{2,1,0:T(8,128)(2,1)} %bitcast), calls=%async_computation.2 | async-start | bytes 2097152 | tf_op jit(solution)/shard_map/cond/branch_1_fun/all_to_all | solution.py:191
  21.0 7.4 %copy-start.7 = (bf16[512,2048]{1,0:T(8,128)(2,1)S(1)}, bf16[512,2048]{1,0:T(8,128)(2,1)}, u32[]{:S(2)}) copy-start(bf16[512,2048]{1,0:T(8,128)(2,1)} %get-tuple-element.232) | copy-start | bytes 6291460 | tf_op jit(solution)/shard_map/cond
  53.6 8.4 %copy-start.1 = (bf16[512,512]{1,0:T(8,128)(2,1)}, bf16[512,512]{1,0:T(8,128)(2,1)S(1)}, u32[]{:S(2)}) copy-start(bf16[512,512]{1,0:T(8,128)(2,1)S(1)} %get-tuple-element.454) | copy-start | bytes 1572868
  53.6 8.4 %copy-start.3 = (bf16[512,512]{1,0:T(8,128)(2,1)}, bf16[512,512]{1,0:T(8,128)(2,1)S(1)}, u32[]{:S(2)}) copy-start(bf16[512,512]{1,0:T(8,128)(2,1)S(1)} %get-tuple-element.399) | copy-start | bytes 1572868
  53.6 49.4 %collective-permute-start.16 = (bf16[64,2048]{1,0:T(8,128)(2,1)}, bf16[64,2048]{1,0:T(8,128)(2,1)S(1)}, u32[]{:S(2)}, u32[]{:S(2)}) collective-permute-start(bf16[64,2048]{1,0:T(8,128)(2,1)} %get-tuple-element.423), channel_id=1, source_target_pairs={{0,8},{1,9},{2,10},{3,11},{4,12},{5,13},{6,14},{7,15},{8,0},{9,1},... | collective-permute-start | bytes 786440 | tf_op jit(solution)/shard_map/ppermute | solution.py:174
  57.3 45.8 %collective-permute-start.17 = (bf16[64,2048]{1,0:T(8,128)(2,1)}, bf16[64,2048]{1,0:T(8,128)(2,1)S(1)}, u32[]{:S(2)}, u32[]{:S(2)}) collective-permute-start(bf16[64,2048]{1,0:T(8,128)(2,1)} %get-tuple-element.424), channel_id=1, source_target_pairs={{0,10},{1,11},{2,8},{3,9},{4,14},{5,15},{6,12},{7,13},{8,2},{9,3},... | collective-permute-start | bytes 786440 | tf_op jit(solution)/shard_map/ppermute | solution.py:174
  57.6 45.4 %collective-permute-start.18 = (bf16[64,2048]{1,0:T(8,128)(2,1)}, bf16[64,2048]{1,0:T(8,128)(2,1)}, u32[]{:S(2)}, u32[]{:S(2)}) collective-permute-start(bf16[64,2048]{1,0:T(8,128)(2,1)} %get-tuple-element.425), channel_id=1, source_target_pairs={{0,12},{1,13},{2,14},{3,15},{4,8},{5,9},{6,10},{7,11},{8,4},{9,5},... | collective-permute-start | bytes 786440 | tf_op jit(solution)/shard_map/ppermute | solution.py:174
  61.1 42.0 %collective-permute-start.19 = (bf16[64,2048]{1,0:T(8,128)(2,1)}, bf16[64,2048]{1,0:T(8,128)(2,1)}, u32[]{:S(2)}, u32[]{:S(2)}) collective-permute-start(bf16[64,2048]{1,0:T(8,128)(2,1)} %get-tuple-element.426), channel_id=1, source_target_pairs={{0,14},{1,15},{2,12},{3,13},{4,10},{5,11},{6,8},{7,9},{8,6},{9,7},... | collective-permute-start | bytes 786440 | tf_op jit(solution)/shard_map/ppermute | solution.py:174
  65.6 4.5 %collective-permute-start = (bf16[256,2048]{1,0:T(8,128)(2,1)S(1)}, bf16[256,2048]{1,0:T(8,128)(2,1)}, u32[]{:S(2)}, u32[]{:S(2)}) collective-permute-start(bf16[256,2048]{1,0:T(8,128)(2,1)S(1)} %get-tuple-element.258), channel_id=1, source_target_pairs={{0,1},{1,0},{2,3},{3,2},{4,5},{5,4},{6,7},{7,6},{8,9},{9,8},{10,11... | collective-permute-start | bytes 3145736 | tf_op jit(solution)/shard_map/cond/branch_1_fun/ppermute | solution.py:177
  65.6 37.5 %all-to-all-start = ((bf16[4,64,2048]{2,1,0:T(8,128)(2,1)}), bf16[4,64,2048]{2,1,0:T(8,128)(2,1)}, u32[]{:S(2)}, u32[]{:S(2)}) async-start(bf16[4,64,2048]{2,1,0:T(8,128)(2,1)} %bitcast.6), calls=%async_computation | async-start | bytes 2097152 | tf_op jit(solution)/shard_map/cond/branch_1_fun/all_to_all | solution.py:191
  73.7 2.9 %collective-permute-start.1 = (bf16[256,2048]{1,0:T(8,128)(2,1)S(1)}, bf16[256,2048]{1,0:T(8,128)(2,1)S(1)}, u32[]{:S(2)}, u32[]{:S(2)}) collective-permute-start(bf16[256,2048]{1,0:T(8,128)(2,1)S(1)} %get-tuple-element.260), channel_id=1, source_target_pairs={{0,1},{1,0},{2,3},{3,2},{4,5},{5,4},{6,7},{7,6},{8,9},{9,8},{10,11... | collective-permute-start | bytes 3145736 | tf_op jit(solution)/shard_map/cond/branch_1_fun/ppermute | solution.py:177
  103.1 48.8 %collective-permute-start.20 = (bf16[64,2048]{1,0:T(8,128)(2,1)}, bf16[64,2048]{1,0:T(8,128)(2,1)}, u32[]{:S(2)}, u32[]{:S(2)}) collective-permute-start(bf16[64,2048]{1,0:T(8,128)(2,1)} %get-tuple-element.428), channel_id=1, source_target_pairs={{0,8},{1,9},{2,10},{3,11},{4,12},{5,13},{6,14},{7,15},{8,0},{9,1},... | collective-permute-start | bytes 786440 | tf_op jit(solution)/shard_map/ppermute | solution.py:174
  106.0 45.9 %collective-permute-start.21 = (bf16[64,2048]{1,0:T(8,128)(2,1)}, bf16[64,2048]{1,0:T(8,128)(2,1)}, u32[]{:S(2)}, u32[]{:S(2)}) collective-permute-start(bf16[64,2048]{1,0:T(8,128)(2,1)} %get-tuple-element.429), channel_id=1, source_target_pairs={{0,10},{1,11},{2,8},{3,9},{4,14},{5,15},{6,12},{7,13},{8,2},{9,3},... | collective-permute-start | bytes 786440 | tf_op jit(solution)/shard_map/ppermute | solution.py:174
  106.5 45.4 %collective-permute-start.22 = (bf16[64,2048]{1,0:T(8,128)(2,1)}, bf16[64,2048]{1,0:T(8,128)(2,1)}, u32[]{:S(2)}, u32[]{:S(2)}) collective-permute-start(bf16[64,2048]{1,0:T(8,128)(2,1)} %get-tuple-element.430), channel_id=1, source_target_pairs={{0,12},{1,13},{2,14},{3,15},{4,8},{5,9},{6,10},{7,11},{8,4},{9,5},... | collective-permute-start | bytes 786440 | tf_op jit(solution)/shard_map/ppermute | solution.py:174
  109.9 42.0 %collective-permute-start.23 = (bf16[64,2048]{1,0:T(8,128)(2,1)}, bf16[64,2048]{1,0:T(8,128)(2,1)}, u32[]{:S(2)}, u32[]{:S(2)}) collective-permute-start(bf16[64,2048]{1,0:T(8,128)(2,1)} %get-tuple-element.431), channel_id=1, source_target_pairs={{0,14},{1,15},{2,12},{3,13},{4,10},{5,11},{6,8},{7,9},{8,6},{9,7},... | collective-permute-start | bytes 786440 | tf_op jit(solution)/shard_map/ppermute | solution.py:174
  113.1 4.3 %collective-permute-start.10 = (bf16[256,2048]{1,0:T(8,128)(2,1)S(1)}, bf16[256,2048]{1,0:T(8,128)(2,1)S(1)}, u32[]{:S(2)}, u32[]{:S(2)}) collective-permute-start(bf16[256,2048]{1,0:T(8,128)(2,1)S(1)} %get-tuple-element.275), channel_id=1, source_target_pairs={{0,1},{1,0},{2,3},{3,2},{4,5},{5,4},{6,7},{7,6},{8,9},{9,8},{10,11... | collective-permute-start | bytes 3145736 | tf_op jit(solution)/shard_map/cond/branch_1_fun/ppermute | solution.py:177
  113.2 38.7 %all-to-all-start.1 = ((bf16[4,64,2048]{2,1,0:T(8,128)(2,1)}), bf16[4,64,2048]{2,1,0:T(8,128)(2,1)}, u32[]{:S(2)}, u32[]{:S(2)}) async-start(bf16[4,64,2048]{2,1,0:T(8,128)(2,1)} %bitcast.74), calls=%async_computation.1 | async-start | bytes 2097152 | tf_op jit(solution)/shard_map/cond/branch_1_fun/all_to_all | solution.py:191
  121.3 6.6 %collective-permute-start.11 = (bf16[256,2048]{1,0:T(8,128)(2,1)}, bf16[256,2048]{1,0:T(8,128)(2,1)}, u32[]{:S(2)}, u32[]{:S(2)}) collective-permute-start(bf16[256,2048]{1,0:T(8,128)(2,1)} %get-tuple-element.277), channel_id=1, source_target_pairs={{0,1},{1,0},{2,3},{3,2},{4,5},{5,4},{6,7},{7,6},{8,9},{9,8},{10,11... | collective-permute-start | bytes 3145736 | tf_op jit(solution)/shard_map/cond/branch_1_fun/ppermute | solution.py:177
  151.9 4.5 %copy-start.5 = (f32[32,16,16]{0,2,1:T(8,128)}, f32[32,16,16]{0,2,1:T(8,128)S(1)}, u32[]{:S(2)}) copy-start(f32[32,16,16]{0,2,1:T(8,128)S(1)} %get-tuple-element.613) | copy-start | bytes 98308
  151.9 28.6 %collective-permute-start.24 = (bf16[64,2048]{1,0:T(8,128)(2,1)}, bf16[64,2048]{1,0:T(8,128)(2,1)S(1)}, u32[]{:S(2)}, u32[]{:S(2)}) collective-permute-start(bf16[64,2048]{1,0:T(8,128)(2,1)} %get-tuple-element.459), channel_id=1, source_target_pairs={{0,12},{1,13},{2,14},{3,15},{4,8},{5,9},{6,10},{7,11},{8,4},{9,5},... | collective-permute-start | bytes 786440 | tf_op jit(solution)/shard_map/ppermute | solution.py:174
  154.0 26.6 %collective-permute-start.25 = (bf16[64,2048]{1,0:T(8,128)(2,1)}, bf16[64,2048]{1,0:T(8,128)(2,1)S(1)}, u32[]{:S(2)}, u32[]{:S(2)}) collective-permute-start(bf16[64,2048]{1,0:T(8,128)(2,1)} %get-tuple-element.460), channel_id=1, source_target_pairs={{0,14},{1,15},{2,12},{3,13},{4,10},{5,11},{6,8},{7,9},{8,6},{9,7},... | collective-permute-start | bytes 786440 | tf_op jit(solution)/shard_map/ppermute | solution.py:174
  161.1 14.8 %copy-start.2 = (bf16[512,512]{1,0:T(8,128)(2,1)S(1)}, bf16[512,512]{1,0:T(8,128)(2,1)}, u32[]{:S(2)}) copy-start(bf16[512,512]{1,0:T(8,128)(2,1)} %get-tuple-element.296.matrix) | copy-start | bytes 1572868 | tf_op jit(solution)/shard_map/cond
  161.2 1.6 collective-permute-start.2
  162.9 8.5 %collective-permute-start.3 = (bf16[4,32,512]{2,1,0:T(8,128)(2,1)S(1)}, bf16[4,32,512]{2,1,0:T(8,128)(2,1)S(1)}, u32[]{:S(2)}, u32[]{:S(2)}) collective-permute-start(bf16[4,32,512]{2,1,0:T(8,128)(2,1)S(1)} %slice_bitcast_fusion), channel_id=1, source_target_pairs={{0,2},{1,3},{2,0},{3,1},{4,6},{5,7},{6,4},{7,5},{8,10},{9,11},{10,... | collective-permute-start | bytes 393224 | tf_op jit(solution)/shard_map/cond/branch_1_fun/ppermute | solution.py:174
  171.5 9.0 %collective-permute-start.4 = (bf16[32,512]{1,0:T(8,128)(2,1)S(1)}, bf16[32,512]{1,0:T(8,128)(2,1)S(1)}, u32[]{:S(2)}, u32[]{:S(2)}) collective-permute-start(bf16[32,512]{1,0:T(8,128)(2,1)S(1)} %get-tuple-element.620), channel_id=1, source_target_pairs={{0,4},{1,5},{2,6},{3,7},{4,0},{5,1},{6,2},{7,3},{8,12},{9,13},{10,... | collective-permute-start | bytes 98312 | tf_op jit(solution)/shard_map/cond/branch_1_fun/ppermute | solution.py:174
  171.5 8.9 %collective-permute-start.5 = (bf16[32,512]{1,0:T(8,128)(2,1)S(1)}, bf16[32,512]{1,0:T(8,128)(2,1)S(1)}, u32[]{:S(2)}, u32[]{:S(2)}) collective-permute-start(bf16[32,512]{1,0:T(8,128)(2,1)S(1)} %get-tuple-element.622), channel_id=1, source_target_pairs={{0,8},{1,9},{2,10},{3,11},{4,12},{5,13},{6,14},{7,15},{8,0},{9,1},... | collective-permute-start | bytes 98312 | tf_op jit(solution)/shard_map/cond/branch_1_fun/ppermute | solution.py:174
  174.3 6.1 %collective-permute-start.6 = (bf16[32,512]{1,0:T(8,128)(2,1)S(1)}, bf16[32,512]{1,0:T(8,128)(2,1)S(1)}, u32[]{:S(2)}, u32[]{:S(2)}) collective-permute-start(bf16[32,512]{1,0:T(8,128)(2,1)S(1)} %get-tuple-element.621), channel_id=1, source_target_pairs={{0,12},{1,13},{2,14},{3,15},{4,8},{5,9},{6,10},{7,11},{8,4},{9,5},... | collective-permute-start | bytes 98312 | tf_op jit(solution)/shard_map/cond/branch_1_fun/ppermute | solution.py:174
  180.5 36.7 %all-to-all-start.3 = ((bf16[4,64,2048]{2,1,0:T(8,128)(2,1)}), bf16[4,64,2048]{2,1,0:T(8,128)(2,1)S(1)}, u32[]{:S(2)}, u32[]{:S(2)}) async-start(bf16[4,64,2048]{2,1,0:T(8,128)(2,1)} %bitcast.35), calls=%async_computation.3 | async-start | bytes 2097152 | tf_op jit(solution)/shard_map/all_to_all | solution.py:191
  184.1 21.0 %collective-permute-start.26 = (bf16[32,512]{1,0:T(8,128)(2,1)S(1)}, bf16[32,512]{1,0:T(8,128)(2,1)S(1)}, u32[]{:S(2)}, u32[]{:S(2)}) collective-permute-start(bf16[32,512]{1,0:T(8,128)(2,1)S(1)} %get-tuple-element.469), channel_id=1, source_target_pairs={{0,4},{1,5},{2,6},{3,7},{4,0},{5,1},{6,2},{7,3},{8,12},{9,13},{10,... | collective-permute-start | bytes 98312 | tf_op jit(solution)/shard_map/ppermute | solution.py:174
  186.0 19.0 %collective-permute-start.27 = (bf16[32,512]{1,0:T(8,128)(2,1)S(1)}, bf16[32,512]{1,0:T(8,128)(2,1)S(1)}, u32[]{:S(2)}, u32[]{:S(2)}) collective-permute-start(bf16[32,512]{1,0:T(8,128)(2,1)S(1)} %get-tuple-element.469), channel_id=1, source_target_pairs={{0,8},{1,9},{2,10},{3,11},{4,12},{5,13},{6,14},{7,15},{8,0},{9,1},... | collective-permute-start | bytes 98312 | tf_op jit(solution)/shard_map/ppermute | solution.py:174
  187.6 17.4 %collective-permute-start.28 = (bf16[32,512]{1,0:T(8,128)(2,1)S(1)}, bf16[32,512]{1,0:T(8,128)(2,1)S(1)}, u32[]{:S(2)}, u32[]{:S(2)}) collective-permute-start(bf16[32,512]{1,0:T(8,128)(2,1)S(1)} %get-tuple-element.469), channel_id=1, source_target_pairs={{0,12},{1,13},{2,14},{3,15},{4,8},{5,9},{6,10},{7,11},{8,4},{9,5},... | collective-permute-start | bytes 98312 | tf_op jit(solution)/shard_map/ppermute | solution.py:174
  188.5 23.7 %collective-permute-start.30 = (bf16[64,2048]{1,0:T(8,128)(2,1)}, bf16[64,2048]{1,0:T(8,128)(2,1)S(1)}, u32[]{:S(2)}, u32[]{:S(2)}) collective-permute-start(bf16[64,2048]{1,0:T(8,128)(2,1)} %get-tuple-element.465), channel_id=1, source_target_pairs={{0,10},{1,11},{2,8},{3,9},{4,14},{5,15},{6,12},{7,13},{8,2},{9,3},... | collective-permute-start | bytes 786440 | tf_op jit(solution)/shard_map/ppermute | solution.py:174
  205.0 12.2 %collective-permute-start.29 = (bf16[64,2048]{1,0:T(8,128)(2,1)}, bf16[64,2048]{1,0:T(8,128)(2,1)S(1)}, u32[]{:S(2)}, u32[]{:S(2)}) collective-permute-start(bf16[64,2048]{1,0:T(8,128)(2,1)} %get-tuple-element.464), channel_id=1, source_target_pairs={{0,8},{1,9},{2,10},{3,11},{4,12},{5,13},{6,14},{7,15},{8,0},{9,1},... | collective-permute-start | bytes 786440 | tf_op jit(solution)/shard_map/ppermute | solution.py:174
  205.2 5.0 %collective-permute-start.7 = (bf16[4,32,512]{2,1,0:T(8,128)(2,1)S(1)}, bf16[4,32,512]{2,1,0:T(8,128)(2,1)S(1)}, u32[]{:S(2)}, u32[]{:S(2)}) collective-permute-start(bf16[4,32,512]{2,1,0:T(8,128)(2,1)S(1)} %pad_maximum_fusion.refs_0_), channel_id=1, source_target_pairs={{0,2},{1,3},{2,0},{3,1},{4,6},{5,7},{6,4},{7,5},{8,10},{9,11},{10,... | collective-permute-start | bytes 393224 | tf_op jit(solution)/shard_map/cond/branch_1_fun/ppermute | solution.py:174
  206.8 3.5 %collective-permute-start.8 = (bf16[4,32,512]{2,1,0:T(8,128)(2,1)S(1)}, bf16[4,32,512]{2,1,0:T(8,128)(2,1)S(1)}, u32[]{:S(2)}, u32[]{:S(2)}) collective-permute-start(bf16[4,32,512]{2,1,0:T(8,128)(2,1)S(1)} %pad_maximum_fusion.refs_0_), channel_id=1, source_target_pairs={{0,1},{1,0},{2,3},{3,2},{4,5},{5,4},{6,7},{7,6},{8,9},{9,8},{10,11... | collective-permute-start | bytes 393224 | tf_op jit(solution)/shard_map/cond/branch_1_fun/ppermute | solution.py:177
  210.3 1.3 collective-permute-start.9
  212.2 8.9 %copy-start.4 = (f32[512,512]{1,0:T(8,128)}, f32[512,512]{1,0:T(8,128)S(1)}, u32[]{:S(2)}) copy-start(f32[512,512]{1,0:T(8,128)S(1)} %get-tuple-element.687) | copy-start | bytes 3145732

commit v4 on v3

--- a/solution.py
+++ b/solution.py
@@ -51,6 +51,31 @@
         out[at] = a[at] * slab[...]
 
 
+def last_kernel(place, a, slab, old, out):
+    out[...] = a[...] * slab[...]
+
+
+def place_last(place, a, slab, total):
+    rows, width = slab.shape
+    block = pl.BlockSpec((rows, width), lambda i, place: (place[0], 0))
+    return pl.pallas_call(
+        last_kernel,
+        grid_spec=pltpu.PrefetchScalarGridSpec(
+            num_scalar_prefetch=1,
+            grid=(1,),
+            in_specs=[
+                block,
+                pl.BlockSpec((rows, width), lambda i, place: (0, 0)),
+                pl.BlockSpec(memory_space=pl.ANY),
+            ],
+            out_specs=block,
+        ),
+        out_shape=jax.ShapeDtypeStruct(total.shape, BF16),
+        input_output_aliases={3: 0},
+        compiler_params=LIMIT,
+    )(place, a, slab, total)
+
+
 def cut_kernel(matrix, rows, *slabs):
     total = jnp.dot(matrix[...], rows[...], preferred_element_type=F32).astype(BF16)
     at = 0
@@ -65,23 +90,34 @@
     out[...] = jnp.dot(matrix[...], rows, preferred_element_type=F32).astype(BF16)
 
 
-def partial_kernel(order, right, *refs):
+def partial_kernel(slab, starts, order, right, side, *refs):
     *slabs, out, total = refs
 
     @pl.when(pl.program_id(0) == 0)
     def _():
         total[...] = jnp.zeros_like(total)
 
-    left = jnp.concatenate([s[...] for s in slabs], axis=0)
+    count = side.shape[0] // slab
+    if slab % 16 == 0:
+        rows = [side[pl.ds(pl.multiple_of(starts[k], slab), slab)] for k in range(count)]
+    else:
+        rows = [side[...]]
+    left = jnp.concatenate(rows + [s[...] for s in slabs], axis=0)
     total[...] += lax.dot_general(
         left, right[...], (((1,), (1,)), ((), ())), preferred_element_type=F32
     )
 
     @pl.when(pl.program_id(0) == pl.num_programs(0) - 1)
     def _():
-        out[...] = jnp.dot(
-            order[...], total[...].astype(BF16), preferred_element_type=F32
-        ).astype(BF16)
+        if slab % 16 == 0:
+            out[...] = total[...]
+        else:
+            out[...] = jnp.dot(
+                order[...].astype(F32),
+                total[...],
+                precision=lax.Precision.HIGHEST,
+                preferred_element_type=F32,
+            )
 
 
 def gradient_kernel(same, spread_out, *refs):
@@ -147,13 +183,6 @@
     )(position, *parts)
 
 
-def tree_sum(terms):
-    terms = [t.astype(F32) for t in terms]
-    while len(terms) > 1:
-        terms = [a + b for a, b in zip(terms[::2], terms[1::2])]
-    return terms[0].astype(BF16)
-
-
 def per_device(signal, gate_input, cotangent, block_factor, cross_factor, order_table):
     count = lax.axis_size("seq")
     block, width = signal.shape
@@ -173,8 +202,11 @@
     def chip(x, k):
         return lax.ppermute(x, "seq", [(s, s ^ (2 * k)) for s in range(count)])
 
+    def near(x, i):
+        return lax.ppermute(x, "seq", [(s, s ^ i) for s in range(count)])
+
     def sibling(x):
-        return lax.ppermute(x, "seq", [(s, s ^ 1) for s in range(count)])
+        return near(x, 1)
 
     cross_ks = list(range(far, chips))
     side_groups = [
@@ -200,8 +232,7 @@
 
     half = chips * share
 
-    def turn(slabs, matrix, side):
-        side = send_side(side)
+    def turn(slabs, matrix):
         keep, send = by_columns(functools.partial(split_kernel, share), slabs, [half, half], width, [core])
         other = sibling(send)
         own_out, other_out = by_columns(mix_kernel, [keep, other], [half, half], width, (), [matrix])
@@ -209,7 +240,7 @@
         sent = by_columns(
             functools.partial(join_kernel, share), [own_out, other_in], sizes, width, [core]
         )
-        return side, list(sent), keep, other
+        return list(sent), keep, other
 
     def after(x, earlier):
         return lax.optimization_barrier((x, earlier))
@@ -230,8 +261,7 @@
     at = jnp.arange(block, dtype=jnp.int32) % share
     same = at[:, None] == at[None, :]
 
-    def prepare(side, signal, block_factor, cross_factor, order_table, held, order, relative):
-        side = send_side(side)
+    def prepare(signal, block_factor, cross_factor, order_table, held, order, relative):
         one_hot = hot(order_table, block)
         permuted = jnp.dot(one_hot, signal, preferred_element_type=F32).astype(BF16)
         within = jnp.tile(jnp.arange(slab, dtype=jnp.int32), chips)
@@ -248,20 +278,28 @@
             near.astype(BF16).reshape(block, count), spread_out.T, preferred_element_type=F32
         )
         cross = jnp.where(same, cross, 0.0).astype(BF16)
-        return side, list(mixed), permuted, home, cross, cross.T, chosen, spread_out, rows(relative)
-
-    side, mixed, permuted, home_factor, cross, cross_t, chosen, spread_out, reorder = phase(
-        prepare, side, later[2], block_factor, cross_factor, order_table, held, order, relative
-    )
-
+        return list(mixed), permuted, home, cross, cross.T, chosen, spread_out, rows(relative)
+
+    mixed, permuted, home_factor, cross, cross_t, chosen, spread_out, reorder = phase(
+        prepare, later[2], block_factor, cross_factor, order_table, held, order, relative
+    )
+
+    got = send_cross({far: mixed[1]})
+    side, mixed = after(side, mixed)
+    side = phase(send_side, side)
     mixed, grads, side = lax.optimization_barrier((mixed, grads, side))
     grads = [side] + [grads[k] for k in cross_ks]
-    got = send_cross(dict(zip(cross_ks, mixed[1:])))
-    side, back, *grad_rows = phase(turn, grads, cross_t, mixed[0])
+    got.update(send_cross(dict(zip(cross_ks[1:], mixed[2:]))))
+
+    def turn_beside(slabs, matrix, side):
+        return send_side(side), *turn(slabs, matrix)
+
+    side, back, *grad_rows = phase(turn_beside, grads, cross_t, mixed[0])
     back, got, side = lax.optimization_barrier((back, got, side))
     mixed = [side] + [got[k] for k in cross_ks]
 
     got = send_cross(dict(zip(cross_ks, back[1:])))
+
     def cross_gradient(rows, same, chosen, spread_out):
         products = by_columns(
             gradient_kernel,
@@ -280,7 +318,8 @@
         ) / math.sqrt(width)
 
     def turn_and_gradient(slabs, matrix, side, grad_rows, *rest):
-        side, sent, *mixed_rows = turn(slabs, matrix, side)
+        side = send_side(side)
+        sent, *mixed_rows = turn(slabs, matrix)
         return side, sent, cross_gradient(grad_rows + mixed_rows, *rest)
 
     side, gated, grad_cross = phase(
@@ -290,57 +329,84 @@
     backs = [side] + [got[k] for k in cross_ks]
 
     gateds = dict(zip(cross_ks, gated[1:]))
-    first, second = cross_ks[far // 2 :], cross_ks[: far // 2]
+    first, last = cross_ks[::2], cross_ks[1::2]
     arrived = send_cross({k: gateds[k] for k in first})
-
-    def home(backs, permuted, home_factor, reorder):
+    gated_side = send_side(gated[0])
+
+    def add(kept, received):
+        return sum((x.astype(F32) for x in received), kept)
+
+    def home(backs, permuted, reorder, starts):
         terms = by_columns(
-            partial_kernel,
+            functools.partial(partial_kernel, slab),
             [permuted] + backs,
             [(block, block)],
             width,
+            scalars=[starts],
             whole=[reorder],
             scratch=[pltpu.VMEM((block, block), F32)],
+            dtype=F32,
         )[0]
-        terms = terms.reshape(chips, 2, share, block)
-        mine = lambda i: lax.dynamic_index_in_dim(terms, jnp.bitwise_xor(e, i), 1, keepdims=False)
-        terms = tree_sum([mine(0), sibling(mine(1))]).reshape(far, 2, share, block)
-        terms = tree_sum([terms[:, 0], chip(terms[:, 1], 1)])
-        own = tree_sum([terms[0]] + [chip(terms[k], 2 * k) for k in range(1, far)])
-        grad_signal = by_columns(whole_kernel, backs, [block], width, (), [home_factor])[0]
-        return own, grad_signal
-
-    own, grad_signal = phase(home, backs, permuted, home_factor, reorder)
-    (side, rest), arrived, own = lax.optimization_barrier(
-        ((gated[0], {k: gateds[k] for k in second}), arrived, own)
-    )
-    arrived.update(send_cross({k: rest[k] for k in second[far // 4 :]}))
-    side = send_side(side)
+        terms = terms.reshape(far, 2, 2, share, block)
+        mine = lambda i: lax.dynamic_index_in_dim(
+            terms[:, i // 2], jnp.bitwise_xor(e, i % 2), 1, keepdims=False
+        )
+        terms = add(mine(0), [near(mine(i).astype(BF16), i) for i in (1, 2, 3)])
+        own = add(terms[0], [chip(terms[k].astype(BF16), 2 * k) for k in range(1, far)])
+        return own.astype(BF16)
+
+    own = phase(home, backs, permuted, reorder, relative[:far] * slab)
+    rest, own, arrived = lax.optimization_barrier(
+        ({k: gateds[k] for k in last}, own, arrived)
+    )
     got = [own] + [chip(own, 2 * k) for k in range(1, far)]
-    rest, got = after({k: rest[k] for k in second[: far // 4]}, got)
-    arrived.update(send_cross(rest))
-
-    def all_rows(got, position):
-        near = jnp.stack(got)
-        parts = [near, chip(near, 1)]
-        parts += [sibling(x) for x in parts]
-        return in_order(position, parts, 1.0 / math.sqrt(count * width)).reshape(block, block)
-
-    k = (every % far) * 2 + every // far % 2
-    position = jnp.bitwise_xor(h, k) * 2 + jnp.bitwise_xor(e, every // chips)
-    grad_block = phase(all_rows, got, position.astype(jnp.int32))
-    arrived, side, grad_block = lax.optimization_barrier((arrived, side, grad_block))
-    starts = [side_start] + [jnp.bitwise_xor(h, k) * slab for k in cross_ks]
-    slabs = [side] + [arrived[k] for k in cross_ks]
-    if slab % 16 == 0:
-        grad_gate = by_columns(
-            place_kernel, [cotangent] + slabs, [block], width, [jnp.stack(starts).astype(jnp.int32)]
-        )[0]
-    else:
-        grad_gate = jnp.zeros_like(cotangent)
+    rest, got = after(rest, got)
+    late = send_cross(rest)
+
+    dynamic = slab % 16 == 0
+    starts = {k: jnp.bitwise_xor(h, k) * slab for k in cross_ks}
+
+    def place(total, starts, slabs):
         for start, x in zip(starts, slabs):
             rows = lax.dynamic_slice_in_dim(cotangent, start, x.shape[0], 0) * x
-            grad_gate = lax.dynamic_update_slice_in_dim(grad_gate, rows, start, 0)
+            total = lax.dynamic_update_slice_in_dim(total, rows, start, 0)
+        return total
+
+    def finish(got, position, backs, home_factor, cotangent, starts, slabs):
+        first = jnp.stack(got)
+        rows = in_order(
+            position,
+            [first] + [near(first, i) for i in (1, 2, 3)],
+            1.0 / math.sqrt(count * width),
+        )
+        grad_signal = by_columns(whole_kernel, backs, [block], width, (), [home_factor])[0]
+        if dynamic:
+            grad_gate = by_columns(
+                place_kernel, [cotangent] + slabs, [block], width, [jnp.stack(starts)]
+            )[0]
+        else:
+            grad_gate = place(jnp.zeros_like(cotangent), starts, slabs)
+        return rows.reshape(block, block), grad_signal, grad_gate
+
+    k = every % far * 2 + every // far // 2
+    position = jnp.bitwise_xor(h, k) * 2 + jnp.bitwise_xor(e, every // far % 2)
+    grad_block, grad_signal, grad_gate = phase(
+        finish,
+        got,
+        position.astype(jnp.int32),
+        backs,
+        home_factor,
+        cotangent,
+        [side_start.astype(jnp.int32)] + [starts[k].astype(jnp.int32) for k in first],
+        [gated_side] + [arrived[k] for k in first],
+    )
+    late, grad_gate = after(late, grad_gate)
+    if dynamic:
+        for k in last:
+            at = jnp.bitwise_xor(h, k).reshape(1).astype(jnp.int32)
+            grad_gate = place_last(at, cotangent, late[k], grad_gate)
+    else:
+        grad_gate = place(grad_gate, [starts[k] for k in last], [late[k] for k in last])
     return (grad_signal, grad_gate, grad_block, grad_cross)
 
 

time: 222 us -> 218 us (0.982)
  waiting for transfers between devices: 97.9 us -> 66.5 us
  blocking collectives: 0 us -> 23.7 us
  local copies, waits for them, and re-layouts: 3.85 us -> 8.62 us
  Pallas kernels: 42 us -> 39.5 us
    all_to_all x4 -> x3, waiting for transfers between devices: 62.2 us -> 34 us  [send_side(): lax.all_to_all(x, 'seq', split_axis=0, concat_axis=0, tiled=True, axis_in...]
    all_to_all x0 -> x1, blocking collectives: none -> 23.7 us  [send_side(): lax.all_to_all(x, 'seq', split_axis=0, concat_axis=0, tiled=True, axis_in...]
    ppermute x24 -> x22, waiting for transfers between devices: 30.6 us -> 10.6 us  [chip(): return lax.ppermute(x, 'seq', [(s, s ^ 2 * k) for s in range(count)])]
    ppermute x7 -> x10, waiting for transfers between devices: 5.13 us -> 21.9 us  [near(): return lax.ppermute(x, 'seq', [(s, s ^ i) for s in range(count)])]
    ppermute x7 -> x10, starting transfers between devices: 1.21 us -> 5.33 us  [near(): return lax.ppermute(x, 'seq', [(s, s ^ i) for s in range(count)])]
    all_to_all x4 -> x3, starting transfers between devices: 16.3 us -> 12.8 us  [send_side(): lax.all_to_all(x, 'seq', split_axis=0, concat_axis=0, tiled=True, axis_in...]
    unnamed x14 -> x22, local copies, waits for them, and re-layouts: 0.03 us -> 2.93 us
    pallas_call x11, Pallas kernels: 41.3 us -> 38.9 us  [by_columns(): pl.pallas_call(kernel, grid=(width // columns,), in_specs=[pl.BlockSpec(m...]
  transfers between devices with their start and end apart: 35 -> 35, of which waited for: 10 -> 11; matrix products, arithmetic and copies ran while one was open for 7% -> 9% of each run, Pallas kernels for 17% -> 18%
where the time goes in v4:
time: 218 us; the launch traced here: 217 us
  waiting for transfers between devices  66.5 us (31%)
  starting transfers between devices  59.4 us (27%)
  Pallas kernels  39.5 us (18%)
  blocking collectives  23.7 us (11%)
  matrix products  9.66 us (4%)
  local copies, waits for them, and re-layouts  8.62 us (4%)
  other arithmetic  7.67 us (4%)
    ppermute x22, starting transfers between devices, chip(): return lax.ppermute(x, 'seq', [(s, s ^ 2 * k) for s in range(count)])  41.2 us
    pallas_call x11, Pallas kernels, by_columns(): pl.pallas_call(kernel, grid=(width // columns,), in_specs=[pl.BlockSpec(m...  38.9 us
    all_to_all x3, waiting for transfers between devices, send_side(): lax.all_to_all(x, 'seq', split_axis=0, concat_axis=0, tiled=True, axis_in...  34 us
    all_to_all x1, blocking collectives, send_side(): lax.all_to_all(x, 'seq', split_axis=0, concat_axis=0, tiled=True, axis_in...  23.7 us
    ppermute x10, waiting for transfers between devices, near(): return lax.ppermute(x, 'seq', [(s, s ^ i) for s in range(count)])  21.9 us
    all_to_all x3, starting transfers between devices, send_side(): lax.all_to_all(x, 'seq', split_axis=0, concat_axis=0, tiled=True, axis_in...  12.8 us
    ppermute x22, waiting for transfers between devices, chip(): return lax.ppermute(x, 'seq', [(s, s ^ 2 * k) for s in range(count)])  10.6 us
    ppermute x10, starting transfers between devices, near(): return lax.ppermute(x, 'seq', [(s, s ^ i) for s in range(count)])  5.33 us
  transfers between devices with their start and end apart: 35, of which 11 were waited for; matrix products, arithmetic and copies ran while one was open for 9% of the time, Pallas kernels for 18%

profile of v4, /device:TPU:0, one launch (start us, length us, event | category | flops | bytes accessed | tf_op | source)
XLA Modules:
  0.0 217.0 jit_solution(18116594004354372738)
XLA Ops:
  0.7 2.7 %dynamic-slice_multiply_fusion.1 = (bf16[64,2048]{1,0:T(8,128)(2,1)}, bf16[64,2048]{1,0:T(8,128)(2,1)}, bf16[64,2048]{1,0:T(8,128)(2,1)}, bf16[64,2048]{1,0:T(8,128)(2,1)}) fusion(bf16[512,2048]{1,0:T(8,128)(2,1)} %param.19, s32[]{:T(128)S(6)} %select_n.112, bf16[512,2048]{1,0:T(8,128)(2,1)} %a.3, s32[]{:T(128)S(6)} %select_n.111, s32[]{:T(128)S(6)} %select_n.110, ...), kind=kLoop, calls=%fused_computation.63 | loop fusion | flops 2097152 | bytes 3145744 | tf_op jit(solution)/shard_map/mul | solution.py:248
  3.4 4.0 %collective-permute-start.13 = (bf16[64,2048]{1,0:T(8,128)(2,1)}, bf16[64,2048]{1,0:T(8,128)(2,1)}, u32[]{:S(2)}, u32[]{:S(2)}) collective-permute-start(bf16[64,2048]{1,0:T(8,128)(2,1)} %get-tuple-element.391), channel_id=1, source_target_pairs={{0,8},{1,9},{2,10},{3,11},{4,12},{5,13},{6,14},{7,15},{8,0},{9,1},... | collective-permute-start | bytes 786440 | tf_op jit(solution)/shard_map/ppermute | solution.py:203
  8.8 3.6 %collective-permute-start.15 = (bf16[64,2048]{1,0:T(8,128)(2,1)}, bf16[64,2048]{1,0:T(8,128)(2,1)}, u32[]{:S(2)}, u32[]{:S(2)}) collective-permute-start(bf16[64,2048]{1,0:T(8,128)(2,1)} %get-tuple-element.393), channel_id=1, source_target_pairs={{0,12},{1,13},{2,14},{3,15},{4,8},{5,9},{6,10},{7,11},{8,4},{9,5},... | collective-permute-start | bytes 786440 | tf_op jit(solution)/shard_map/ppermute | solution.py:203
  13.9 18.6 %conditional.6 = (bf16[256,2048]{1,0:T(8,128)(2,1)}, bf16[64,2048]{1,0:T(8,128)(2,1)}, bf16[64,2048]{1,0:T(8,128)(2,1)}, bf16[64,2048]{1,0:T(8,128)(2,1)}, bf16[...) conditional(s32[]{:T(128)} %bitcast.30, () %tuple.69, ...), branch_computations={%region_0.1_spmd, %region_1.2_spmd} | conditional | flops 1622943616 | bytes 8788276 | solution.py:200
  14.1 1.6 convolution_convert_fusion.2.matrix
  15.8 4.2 %convolution_convert_fusion.rows = bf16[512,2048]{1,0:T(8,128)(2,1)} fusion(bf16[512,2048]{1,0:T(8,128)(2,1)} %get-tuple-element.205, s32[512]{0:T(512)S(1)} %get-tuple-element.204), kind=kOutput, calls=%fused_computation | convolution fusion | flops 1075052544 | bytes 4196352 | tf_op jit(solution)/shard_map/cond/branch_1_fun/dot_general | solution.py:266
  20.0 4.4 %branch_1_fun.12 = (bf16[256,2048]{1,0:T(8,128)(2,1)}, bf16[64,2048]{1,0:T(8,128)(2,1)}, bf16[64,2048]{1,0:T(8,128)(2,1)}, bf16[64,2048]{1,0:T(8,128)(2,1)}, bf16[64,2048]{1,0:T(8,128)(2,1)}) custom-call(bf16[512,512]{1,0:T(8,128)(2,1)S(1)} %convolution_convert_fusion.2.matrix, bf16[512,2048]{1,0:T(8,128)(2,1)} %convolution_convert_fusion.rows), custom_call_target="tpu_custom_call" | custom-call | tf_op jit(solution)/shard_map/cond/branch_1_fun/pallas_call | solution.py:159
  26.9 2.0 fusion
  28.9 1.9 copy.54
  33.5 2.6 %dynamic-slice_multiply_fusion = bf16[256,2048]{1,0:T(8,128)(2,1)} fusion(bf16[512,2048]{1,0:T(8,128)(2,1)} %param.19, s32[]{:T(128)S(6)} %select_n.114, bf16[512,2048]{1,0:T(8,128)(2,1)S(1)} %copy-done), kind=kLoop, calls=%fused_computation.61 | loop fusion | flops 2097152 | bytes 3145732 | tf_op jit(solution)/shard_map/mul | solution.py:250
  36.1 23.7 %conditional.7 = (bf16[256,2048]{1,0:T(8,128)(2,1)S(1)}) conditional(s32[]{:T(128)} %bitcast.30, () %tuple.72, bf16[256,2048]{1,0:T(8,128)(2,1)} %dynamic-slice_multiply_fusion), branch_computations={%region_2.3_spmd, %region_3.4_spmd} | conditional | bytes 2097160 | solution.py:200
  36.1 23.7 %all_to_all.38 = bf16[4,64,2048]{2,1,0:T(8,128)(2,1)S(1)} all-to-all(bf16[4,64,2048]{2,1,0:T(8,128)(2,1)} %bitcast.87), channel_id=1, replica_groups={{0,2,4,6},{1,3,5,7},{8,10,12,14},{9,11,13,15},{16,18,20,22},{17,19,21,2..., dimensions={0} | all-to-all | bytes 2097152 | tf_op jit(solution)/shard_map/cond/branch_1_fun/all_to_all | solution.py:223
  59.8 2.9 %collective-permute-start.18 = (bf16[64,2048]{1,0:T(8,128)(2,1)}, bf16[64,2048]{1,0:T(8,128)(2,1)}, u32[]{:S(2)}, u32[]{:S(2)}) collective-permute-start(bf16[64,2048]{1,0:T(8,128)(2,1)} %get-tuple-element.408), channel_id=1, source_target_pairs={{0,10},{1,11},{2,8},{3,9},{4,14},{5,15},{6,12},{7,13},{8,2},{9,3},... | collective-permute-start | bytes 786440 | tf_op jit(solution)/shard_map/ppermute | solution.py:203
  63.7 3.8 %collective-permute-start.20 = (bf16[64,2048]{1,0:T(8,128)(2,1)}, bf16[64,2048]{1,0:T(8,128)(2,1)}, u32[]{:S(2)}, u32[]{:S(2)}) collective-permute-start(bf16[64,2048]{1,0:T(8,128)(2,1)} %get-tuple-element.410), channel_id=1, source_target_pairs={{0,14},{1,15},{2,12},{3,13},{4,10},{5,11},{6,8},{7,9},{8,6},{9,7},... | collective-permute-start | bytes 786440 | tf_op jit(solution)/shard_map/ppermute | solution.py:203
  67.5 30.9 %conditional.8 = (bf16[256,2048]{1,0:T(8,128)(2,1)}, bf16[256,2048]{1,0:T(8,128)(2,1)}, bf16[64,2048]{1,0:T(8,128)(2,1)}, bf16[64,2048]{1,0:T(8,128)(2,1)}, bf16...) conditional(s32[]{:T(128)} %bitcast.30, () %tuple.67, ...), branch_computations={%region_4.5_spmd, %region_5.6_spmd} | conditional | bytes 12583088 | solution.py:200
  67.5 3.5 %branch_1_fun.13 = (bf16[256,2048]{1,0:T(8,128)(2,1)}, bf16[256,2048]{1,0:T(8,128)(2,1)S(1)}) custom-call(s32[1]{0:T(128)} %get-tuple-element.216.core, bf16[256,2048]{1,0:T(8,128)(2,1)S(1)} %get-tuple-element.218.refs_0_, bf16[64,2048]{1,0:T(8,128)(2,1)} %get-tuple-element.219.refs_1_, bf16[64,2048]{1,0:T(8,128)(2,1)} %get-tuple-element.220.refs_2_, ...), custom_call_target="tpu_custom_call" | custom-call | tf_op jit(solution)/shard_map/cond/branch_1_fun/pallas_call | solution.py:159
  71.0 4.3 %all-to-all-start.1 = ((bf16[4,64,2048]{2,1,0:T(8,128)(2,1)}), bf16[4,64,2048]{2,1,0:T(8,128)(2,1)}, u32[]{:S(2)}, u32[]{:S(2)}) async-start(bf16[4,64,2048]{2,1,0:T(8,128)(2,1)} %bitcast.5), calls=%async_computation.1 | async-start | bytes 2097152 | tf_op jit(solution)/shard_map/cond/branch_1_fun/all_to_all | solution.py:223
  76.6 3.5 %branch_1_fun.14 = (bf16[256,2048]{1,0:T(8,128)(2,1)S(1)}, bf16[256,2048]{1,0:T(8,128)(2,1)S(1)}) custom-call(bf16[512,512]{1,0:T(8,128)(2,1)S(1)} %copy.19.matrix, bf16[256,2048]{1,0:T(8,128)(2,1)} %get-tuple-element.622.own, bf16[256,2048]{1,0:T(8,128)(2,1)} %collective-permute-done.other), custom_call_target="tpu_custom_call" | custom-call | tf_op jit(solution)/shard_map/cond/branch_1_fun/pallas_call | solution.py:159
  80.7 2.3 %collective-permute-done.1.other = bf16[256,2048]{1,0:T(8,128)(2,1)S(1)} collective-permute-done((bf16[256,2048]{1,0:T(8,128)(2,1)S(1)}, bf16[256,2048]{1,0:T(8,128)(2,1)S(1)}, u32[]{:S(2)}, u32[]{:S(2)}) %collective-permute-start.1) | collective-permute-done | bytes 1048608 | tf_op jit(solution)/shard_map/cond/branch_1_fun/ppermute | solution.py:206
  83.0 2.0 branch_1_fun.15
  84.9 13.5 %all-to-all-done.1 = bf16[4,64,2048]{2,1,0:T(8,128)(2,1)} async-done(((bf16[4,64,2048]{2,1,0:T(8,128)(2,1)}), bf16[4,64,2048]{2,1,0:T(8,128)(2,1)}, u32[]{:S(2)}, u32[]{:S(2)}) %all-to-all-start.1) | async-done | bytes 1048608 | tf_op jit(solution)/shard_map/cond/branch_1_fun/all_to_all | solution.py:223
  98.5 3.6 %collective-permute-start.21 = (bf16[64,2048]{1,0:T(8,128)(2,1)}, bf16[64,2048]{1,0:T(8,128)(2,1)}, u32[]{:S(2)}, u32[]{:S(2)}) collective-permute-start(bf16[64,2048]{1,0:T(8,128)(2,1)} %get-tuple-element.412), channel_id=1, source_target_pairs={{0,8},{1,9},{2,10},{3,11},{4,12},{5,13},{6,14},{7,15},{8,0},{9,1},... | collective-permute-start | bytes 786440 | tf_op jit(solution)/shard_map/ppermute | solution.py:203
  102.4 3.5 %collective-permute-start.23 = (bf16[64,2048]{1,0:T(8,128)(2,1)}, bf16[64,2048]{1,0:T(8,128)(2,1)}, u32[]{:S(2)}, u32[]{:S(2)}) collective-permute-start(bf16[64,2048]{1,0:T(8,128)(2,1)} %get-tuple-element.414), channel_id=1, source_target_pairs={{0,12},{1,13},{2,14},{3,15},{4,8},{5,9},{6,10},{7,11},{8,4},{9,5},... | collective-permute-start | bytes 786440 | tf_op jit(solution)/shard_map/ppermute | solution.py:203
  106.8 41.4 %conditional.9 = (bf16[256,2048]{1,0:T(8,128)(2,1)}, bf16[256,2048]{1,0:T(8,128)(2,1)}, bf16[64,2048]{1,0:T(8,128)(2,1)}, bf16[64,2048]{1,0:T(8,128)(2,1)}, bf16...) conditional(s32[]{:T(128)} %bitcast.30, () %tuple.76, ...), branch_computations={%region_6.7_spmd, %region_7.8_spmd} | conditional | flops 1843200 | bytes 12518056 | solution.py:200
  106.8 2.5 %branch_1_fun.16 = (bf16[256,2048]{1,0:T(8,128)(2,1)S(1)}, bf16[256,2048]{1,0:T(8,128)(2,1)S(1)}) custom-call(s32[1]{0:T(128)} %get-tuple-element.233.core, bf16[256,2048]{1,0:T(8,128)(2,1)} %get-tuple-element.235.refs_0_, bf16[64,2048]{1,0:T(8,128)(2,1)} %get-tuple-element.236.refs_1_, bf16[64,2048]{1,0:T(8,128)(2,1)} %get-tuple-element.237.refs_2_, ...), custom_call_target="tpu_custom_call" | custom-call | tf_op jit(solution)/shard_map/cond/branch_1_fun/pallas_call | solution.py:159
  109.3 4.3 %all-to-all-start.2 = ((bf16[4,64,2048]{2,1,0:T(8,128)(2,1)}), bf16[4,64,2048]{2,1,0:T(8,128)(2,1)}, u32[]{:S(2)}, u32[]{:S(2)}) async-start(bf16[4,64,2048]{2,1,0:T(8,128)(2,1)} %bitcast.7), calls=%async_computation.2 | async-start | bytes 2097152 | tf_op jit(solution)/shard_map/cond/branch_1_fun/all_to_all | solution.py:223
  113.6 3.9 %branch_1_fun.17 = (bf16[256,2048]{1,0:T(8,128)(2,1)S(1)}, bf16[256,2048]{1,0:T(8,128)(2,1)}) custom-call(bf16[512,512]{1,0:T(8,128)(2,1)} %get-tuple-element.234.matrix, bf16[256,2048]{1,0:T(8,128)(2,1)S(1)} %get-tuple-element.240.own.refs_2_, bf16[256,2048]{1,0:T(8,128)(2,1)S(1)} %collective-permute-done.11.other.refs_3_), custom_call_target="tpu_custom_call" | custom-call | tf_op jit(solution)/shard_map/cond/branch_1_fun/pallas_call | solution.py:159
  118.2 4.8 %branch_1_fun.19 = f32[512,16]{1,0:T(8,128)S(1)} custom-call(bf16[512,512]{1,0:T(8,128)(2,1)S(1)} %convert_element_type.70.same, bf16[512,16]{1,0:T(8,128)(2,1)} %get-tuple-element.250.spread_out, bf16[256,2048]{1,0:T(8,128)(2,1)} %get-tuple-element.251.refs_0_, bf16[256,2048]{1,0:T(8,128)(2,1)} %get-tuple-element.252.refs_1_, ...), custom_call_target="tpu_custom_call" | custom-call | tf_op jit(solution)/shard_map/cond/branch_1_fun/pallas_call | solution.py:159
  124.1 3.6 %branch_1_fun.18 = (bf16[256,2048]{1,0:T(8,128)(2,1)}, bf16[64,2048]{1,0:T(8,128)(2,1)}, bf16[64,2048]{1,0:T(8,128)(2,1)}, bf16[64,2048]{1,0:T(8,128)(2,1)}, bf16[64,2048]{1,0:T(8,128)(2,1)}) custom-call(s32[1]{0:T(128)} %get-tuple-element.233.core, bf16[256,2048]{1,0:T(8,128)(2,1)S(1)} %get-tuple-element.242.own, ...), custom_call_target="tpu_custom_call" | custom-call | tf_op jit(solution)/shard_map/cond/branch_1_fun/pallas_call | solution.py:159
  127.8 20.5 %all-to-all-done.2 = bf16[4,64,2048]{2,1,0:T(8,128)(2,1)} async-done(((bf16[4,64,2048]{2,1,0:T(8,128)(2,1)}), bf16[4,64,2048]{2,1,0:T(8,128)(2,1)}, u32[]{:S(2)}, u32[]{:S(2)}) %all-to-all-start.2) | async-done | bytes 1048608 | tf_op jit(solution)/shard_map/cond/branch_1_fun/all_to_all | solution.py:223
  148.3 4.3 %all-to-all-start.3 = ((bf16[4,64,2048]{2,1,0:T(8,128)(2,1)}), bf16[4,64,2048]{2,1,0:T(8,128)(2,1)}, u32[]{:S(2)}, u32[]{:S(2)}) async-start(bf16[4,64,2048]{2,1,0:T(8,128)(2,1)} %bitcast.32), calls=%async_computation.3 | async-start | bytes 2097152 | tf_op jit(solution)/shard_map/all_to_all | solution.py:223
  152.6 2.7 %collective-permute-start.25 = (bf16[64,2048]{1,0:T(8,128)(2,1)}, bf16[64,2048]{1,0:T(8,128)(2,1)}, u32[]{:S(2)}, u32[]{:S(2)}) collective-permute-start(bf16[64,2048]{1,0:T(8,128)(2,1)} %get-tuple-element.442), channel_id=1, source_target_pairs={{0,8},{1,9},{2,10},{3,11},{4,12},{5,13},{6,14},{7,15},{8,0},{9,1},... | collective-permute-start | bytes 786440 | tf_op jit(solution)/shard_map/ppermute | solution.py:203
  155.2 1.7 collective-permute-start.26
  156.9 25.8 %conditional.10 = (bf16[32,512]{1,0:T(8,128)(2,1)S(1)}) conditional(s32[]{:T(128)} %bitcast.30, () %tuple.79, (s32[8]{0:T(128)S(1)}, bf16[512,512]{1,0:T(8,128)(2,1)}, bf16[512,2048]{1,0:T(8,128)(2,1)}, bf16[256,2048]{1,0:T(8,128)(2,1)}, bf16[64,2048]{1,0:T(8,128)(2,1)}, /*index=5*/bf16[64,2048]{1,0:T(8,128)(2,1)}, bf16[64,2048]{1,0:T(8,128)(2,1)}, ...), branch_computations={%region_8.9_spmd, %region_9.10_spmd} | conditional | flops 573451 | bytes 5767544 | solution.py:200
  156.9 4.5 %branch_1_fun.20 = f32[512,512]{1,0:T(8,128)S(1)} custom-call(s32[4]{0:T(128)S(1)} %slice_multiply_fusion.starts, bf16[512,512]{1,0:T(8,128)(2,1)} %get-tuple-element.255.order, bf16[512,2048]{1,0:T(8,128)(2,1)} %get-tuple-element.256.right, bf16[256,2048]{1,0:T(8,128)(2,1)} %get-tuple-element.257.side, bf16[64,2048]{1,0:T(8,128)(2,1)} %get-tuple-element.258.refs_0_, ...), custom_call_target="tpu_custom_call" | custom-call | tf_op jit(solution)/shard_map/cond/branch_1_fun/pallas_call | solution.py:159
  161.5 1.5 collective-permute-start.6
  163.9 6.7 %collective-permute-done.6 = bf16[4,32,512]{2,1,0:T(8,128)(2,1)S(1)} collective-permute-done((bf16[4,32,512]{2,1,0:T(8,128)(2,1)S(1)}, bf16[4,32,512]{2,1,0:T(8,128)(2,1)S(1)}, u32[]{:S(2)}, u32[]{:S(2)}) %collective-permute-start.6) | collective-permute-done | bytes 131104 | tf_op jit(solution)/shard_map/cond/branch_1_fun/ppermute | solution.py:206
  170.5 1.6 collective-permute-done.7
  172.2 3.5 %collective-permute-start.10 = (bf16[32,512]{1,0:T(8,128)(2,1)S(1)}, bf16[32,512]{1,0:T(8,128)(2,1)S(1)}, u32[]{:S(2)}, u32[]{:S(2)}) collective-permute-start(bf16[32,512]{1,0:T(8,128)(2,1)S(1)} %get-tuple-element.576), channel_id=1, source_target_pairs={{0,12},{1,13},{2,14},{3,15},{4,8},{5,9},{6,10},{7,11},{8,4},{9,5},... | collective-permute-start | bytes 98312 | tf_op jit(solution)/shard_map/cond/branch_1_fun/ppermute | solution.py:203
  176.7 4.7 %collective-permute-done.10 = bf16[32,512]{1,0:T(8,128)(2,1)S(1)} collective-permute-done((bf16[32,512]{1,0:T(8,128)(2,1)S(1)}, bf16[32,512]{1,0:T(8,128)(2,1)S(1)}, u32[]{:S(2)}, u32[]{:S(2)}) %collective-permute-start.10) | collective-permute-done | bytes 32800 | tf_op jit(solution)/shard_map/cond/branch_1_fun/ppermute | solution.py:203
  182.8 3.2 %collective-permute-start.28 = (bf16[32,512]{1,0:T(8,128)(2,1)S(1)}, bf16[32,512]{1,0:T(8,128)(2,1)S(1)}, u32[]{:S(2)}, u32[]{:S(2)}) collective-permute-start(bf16[32,512]{1,0:T(8,128)(2,1)S(1)} %get-tuple-element.645), channel_id=1, source_target_pairs={{0,8},{1,9},{2,10},{3,11},{4,12},{5,13},{6,14},{7,15},{8,0},{9,1},... | collective-permute-start | bytes 98312 | tf_op jit(solution)/shard_map/ppermute | solution.py:203
  188.3 3.5 %collective-permute-done.29 = bf16[32,512]{1,0:T(8,128)(2,1)S(1)} collective-permute-done((bf16[32,512]{1,0:T(8,128)(2,1)S(1)}, bf16[32,512]{1,0:T(8,128)(2,1)S(1)}, u32[]{:S(2)}, u32[]{:S(2)}) %collective-permute-start.29) | collective-permute-done | bytes 32800 | tf_op jit(solution)/shard_map/ppermute | solution.py:203
  191.8 2.0 collective-permute-start.31
  193.8 20.1 %conditional.11 = (f32[512,512]{1,0:T(8,128)S(1)}, bf16[512,2048]{1,0:T(8,128)(2,1)S(1)}, bf16[512,2048]{1,0:T(8,128)(2,1)S(1)}) conditional(s32[]{:T(128)} %bitcast.30, () %tuple.66, (s32[]{:T(128)}, s32[16]{0:T(128)S(1)}, s32[16]{0:T(128)S(1)}, s32[16]{0:T(128)S(1)}, pred[16]{0:T(512)(128)(4,1)S(1)}, /*index=5*/s32[16]{0:T(128)S(1)}, ...), branch_computations={%region_10.11_spmd, %region_11.12_spmd} | conditional | flops 197158 | bytes 5242912 | solution.py:200
  195.9 2.5 %branch_1_fun.23 = bf16[512,2048]{1,0:T(8,128)(2,1)S(1)} custom-call(s32[3]{0:T(128)S(1)} %pad_add_fusion.starts, bf16[512,2048]{1,0:T(8,128)(2,1)S(1)} %get-tuple-element.286.a, bf16[256,2048]{1,0:T(8,128)(2,1)} %bitcast.29.refs_0_, bf16[64,2048]{1,0:T(8,128)(2,1)} %get-tuple-element.288.refs_1_, bf16[64,2048]{1,0:T(8,128)(2,1)} %get-tuple-element.289.refs_2_), custom_call_target="tpu_custom_call" | custom-call | tf_op jit(solution)/shard_map/cond/branch_1_fun/pallas_call | solution.py:159
  198.5 3.5 %branch_1_fun.22 = bf16[512,2048]{1,0:T(8,128)(2,1)S(1)} custom-call(bf16[512,512]{1,0:T(8,128)(2,1)S(1)} %copy-done.4, bf16[256,2048]{1,0:T(8,128)(2,1)} %get-tuple-element.278.refs_0_, bf16[64,2048]{1,0:T(8,128)(2,1)} %get-tuple-element.279.refs_1_, bf16[64,2048]{1,0:T(8,128)(2,1)} %get-tuple-element.280.refs_2_, ...), custom_call_target="tpu_custom_call" | custom-call | tf_op jit(solution)/shard_map/cond/branch_1_fun/pallas_call | solution.py:159
  202.0 9.0 %collective-permute-done.3.refs_2_ = bf16[4,32,512]{2,1,0:T(8,128)(2,1)S(1)} collective-permute-done((bf16[4,32,512]{2,1,0:T(8,128)(2,1)S(1)}, bf16[4,32,512]{2,1,0:T(8,128)(2,1)S(1)}, u32[]{:S(2)}, u32[]{:S(2)}) %collective-permute-start.3) | collective-permute-done | bytes 131104 | tf_op jit(solution)/shard_map/cond/branch_1_fun/ppermute | solution.py:206
  211.1 2.3 %collective-permute-done.4.refs_3_ = bf16[4,32,512]{2,1,0:T(8,128)(2,1)S(1)} collective-permute-done((bf16[4,32,512]{2,1,0:T(8,128)(2,1)S(1)}, bf16[4,32,512]{2,1,0:T(8,128)(2,1)S(1)}, u32[]{:S(2)}, u32[]{:S(2)}) %collective-permute-start.4) | collective-permute-done | bytes 131104 | tf_op jit(solution)/shard_map/cond/branch_1_fun/ppermute | solution.py:206
  (118 shorter events, 24.4 us)
Async XLA Ops:
  0.6 12.0 %copy-start.11 = (s32[512]{0:T(512)S(1)}, s32[512]{0:T(512)}, u32[]{:S(2)}) copy-start(s32[512]{0:T(512)} %param.23) | copy-start | bytes 6148
  0.6 13.3 %copy-start.8 = (bf16[32,16,16]{0,2,1:T(8,128)(2,1)S(1)}, bf16[32,16,16]{0,2,1:T(8,128)(2,1)}, u32[]{:S(2)}) copy-start(bf16[32,16,16]{0,2,1:T(8,128)(2,1)} %param.22) | copy-start | bytes 49156
  3.4 56.4 %collective-permute-start.13 = (bf16[64,2048]{1,0:T(8,128)(2,1)}, bf16[64,2048]{1,0:T(8,128)(2,1)}, u32[]{:S(2)}, u32[]{:S(2)}) collective-permute-start(bf16[64,2048]{1,0:T(8,128)(2,1)} %get-tuple-element.391), channel_id=1, source_target_pairs={{0,8},{1,9},{2,10},{3,11},{4,12},{5,13},{6,14},{7,15},{8,0},{9,1},... | collective-permute-start | bytes 786440 | tf_op jit(solution)/shard_map/ppermute | solution.py:203
  7.5 52.3 %collective-permute-start.14 = (bf16[64,2048]{1,0:T(8,128)(2,1)}, bf16[64,2048]{1,0:T(8,128)(2,1)}, u32[]{:S(2)}, u32[]{:S(2)}) collective-permute-start(bf16[64,2048]{1,0:T(8,128)(2,1)} %get-tuple-element.392), channel_id=1, source_target_pairs={{0,10},{1,11},{2,8},{3,9},{4,14},{5,15},{6,12},{7,13},{8,2},{9,3},... | collective-permute-start | bytes 786440 | tf_op jit(solution)/shard_map/ppermute | solution.py:203
  8.8 51.0 %collective-permute-start.15 = (bf16[64,2048]{1,0:T(8,128)(2,1)}, bf16[64,2048]{1,0:T(8,128)(2,1)}, u32[]{:S(2)}, u32[]{:S(2)}) collective-permute-start(bf16[64,2048]{1,0:T(8,128)(2,1)} %get-tuple-element.393), channel_id=1, source_target_pairs={{0,12},{1,13},{2,14},{3,15},{4,8},{5,9},{6,10},{7,11},{8,4},{9,5},... | collective-permute-start | bytes 786440 | tf_op jit(solution)/shard_map/ppermute | solution.py:203
  12.4 47.4 %collective-permute-start.16 = (bf16[64,2048]{1,0:T(8,128)(2,1)}, bf16[64,2048]{1,0:T(8,128)(2,1)}, u32[]{:S(2)}, u32[]{:S(2)}) collective-permute-start(bf16[64,2048]{1,0:T(8,128)(2,1)} %get-tuple-element.394), channel_id=1, source_target_pairs={{0,14},{1,15},{2,12},{3,13},{4,10},{5,11},{6,8},{7,9},{8,6},{9,7},... | collective-permute-start | bytes 786440 | tf_op jit(solution)/shard_map/ppermute | solution.py:203
  12.6 1.3 copy-start.9
  13.9 19.6 %copy-start = (bf16[512,2048]{1,0:T(8,128)(2,1)S(1)}, bf16[512,2048]{1,0:T(8,128)(2,1)}, u32[]{:S(2)}) copy-start(bf16[512,2048]{1,0:T(8,128)(2,1)} %a.3) | copy-start | bytes 6291460
  32.5 35.0 %copy-start.3 = (bf16[512,512]{1,0:T(8,128)(2,1)}, bf16[512,512]{1,0:T(8,128)(2,1)S(1)}, u32[]{:S(2)}) copy-start(bf16[512,512]{1,0:T(8,128)(2,1)S(1)} %get-tuple-element.451) | copy-start | bytes 1572868
  32.5 65.9 %collective-permute-start.17 = (bf16[64,2048]{1,0:T(8,128)(2,1)}, bf16[64,2048]{1,0:T(8,128)(2,1)}, u32[]{:S(2)}, u32[]{:S(2)}) collective-permute-start(bf16[64,2048]{1,0:T(8,128)(2,1)} %get-tuple-element.383), channel_id=1, source_target_pairs={{0,8},{1,9},{2,10},{3,11},{4,12},{5,13},{6,14},{7,15},{8,0},{9,1},... | collective-permute-start | bytes 786440 | tf_op jit(solution)/shard_map/ppermute | solution.py:203
  59.8 38.6 %collective-permute-start.18 = (bf16[64,2048]{1,0:T(8,128)(2,1)}, bf16[64,2048]{1,0:T(8,128)(2,1)}, u32[]{:S(2)}, u32[]{:S(2)}) collective-permute-start(bf16[64,2048]{1,0:T(8,128)(2,1)} %get-tuple-element.408), channel_id=1, source_target_pairs={{0,10},{1,11},{2,8},{3,9},{4,14},{5,15},{6,12},{7,13},{8,2},{9,3},... | collective-permute-start | bytes 786440 | tf_op jit(solution)/shard_map/ppermute | solution.py:203
  62.7 35.7 %collective-permute-start.19 = (bf16[64,2048]{1,0:T(8,128)(2,1)}, bf16[64,2048]{1,0:T(8,128)(2,1)}, u32[]{:S(2)}, u32[]{:S(2)}) collective-permute-start(bf16[64,2048]{1,0:T(8,128)(2,1)} %get-tuple-element.409), channel_id=1, source_target_pairs={{0,12},{1,13},{2,14},{3,15},{4,8},{5,9},{6,10},{7,11},{8,4},{9,5},... | collective-permute-start | bytes 786440 | tf_op jit(solution)/shard_map/ppermute | solution.py:203
  63.7 34.7 %collective-permute-start.20 = (bf16[64,2048]{1,0:T(8,128)(2,1)}, bf16[64,2048]{1,0:T(8,128)(2,1)}, u32[]{:S(2)}, u32[]{:S(2)}) collective-permute-start(bf16[64,2048]{1,0:T(8,128)(2,1)} %get-tuple-element.410), channel_id=1, source_target_pairs={{0,14},{1,15},{2,12},{3,13},{4,10},{5,11},{6,8},{7,9},{8,6},{9,7},... | collective-permute-start | bytes 786440 | tf_op jit(solution)/shard_map/ppermute | solution.py:203
  71.0 5.5 %collective-permute-start = (bf16[256,2048]{1,0:T(8,128)(2,1)S(1)}, bf16[256,2048]{1,0:T(8,128)(2,1)}, u32[]{:S(2)}, u32[]{:S(2)}) collective-permute-start(bf16[256,2048]{1,0:T(8,128)(2,1)S(1)} %get-tuple-element.224), channel_id=1, source_target_pairs={{0,1},{1,0},{2,3},{3,2},{4,5},{5,4},{6,7},{7,6},{8,9},{9,8},{10,11... | collective-permute-start | bytes 3145736 | tf_op jit(solution)/shard_map/cond/branch_1_fun/ppermute | solution.py:206
  71.0 27.4 %all-to-all-start.1 = ((bf16[4,64,2048]{2,1,0:T(8,128)(2,1)}), bf16[4,64,2048]{2,1,0:T(8,128)(2,1)}, u32[]{:S(2)}, u32[]{:S(2)}) async-start(bf16[4,64,2048]{2,1,0:T(8,128)(2,1)} %bitcast.5), calls=%async_computation.1 | async-start | bytes 2097152 | tf_op jit(solution)/shard_map/cond/branch_1_fun/all_to_all | solution.py:223
  80.1 2.9 %collective-permute-start.1 = (bf16[256,2048]{1,0:T(8,128)(2,1)S(1)}, bf16[256,2048]{1,0:T(8,128)(2,1)S(1)}, u32[]{:S(2)}, u32[]{:S(2)}) collective-permute-start(bf16[256,2048]{1,0:T(8,128)(2,1)S(1)} %get-tuple-element.226), channel_id=1, source_target_pairs={{0,1},{1,0},{2,3},{3,2},{4,5},{5,4},{6,7},{7,6},{8,9},{9,8},{10,11... | collective-permute-start | bytes 3145736 | tf_op jit(solution)/shard_map/cond/branch_1_fun/ppermute | solution.py:206
  98.5 49.8 %collective-permute-start.21 = (bf16[64,2048]{1,0:T(8,128)(2,1)}, bf16[64,2048]{1,0:T(8,128)(2,1)}, u32[]{:S(2)}, u32[]{:S(2)}) collective-permute-start(bf16[64,2048]{1,0:T(8,128)(2,1)} %get-tuple-element.412), channel_id=1, source_target_pairs={{0,8},{1,9},{2,10},{3,11},{4,12},{5,13},{6,14},{7,15},{8,0},{9,1},... | collective-permute-start | bytes 786440 | tf_op jit(solution)/shard_map/ppermute | solution.py:203
  102.1 46.2 %collective-permute-start.22 = (bf16[64,2048]{1,0:T(8,128)(2,1)}, bf16[64,2048]{1,0:T(8,128)(2,1)}, u32[]{:S(2)}, u32[]{:S(2)}) collective-permute-start(bf16[64,2048]{1,0:T(8,128)(2,1)} %get-tuple-element.413), channel_id=1, source_target_pairs={{0,10},{1,11},{2,8},{3,9},{4,14},{5,15},{6,12},{7,13},{8,2},{9,3},... | collective-permute-start | bytes 786440 | tf_op jit(solution)/shard_map/ppermute | solution.py:203
  102.4 45.9 %collective-permute-start.23 = (bf16[64,2048]{1,0:T(8,128)(2,1)}, bf16[64,2048]{1,0:T(8,128)(2,1)}, u32[]{:S(2)}, u32[]{:S(2)}) collective-permute-start(bf16[64,2048]{1,0:T(8,128)(2,1)} %get-tuple-element.414), channel_id=1, source_target_pairs={{0,12},{1,13},{2,14},{3,15},{4,8},{5,9},{6,10},{7,11},{8,4},{9,5},... | collective-permute-start | bytes 786440 | tf_op jit(solution)/shard_map/ppermute | solution.py:203
  105.9 42.3 %collective-permute-start.24 = (bf16[64,2048]{1,0:T(8,128)(2,1)}, bf16[64,2048]{1,0:T(8,128)(2,1)}, u32[]{:S(2)}, u32[]{:S(2)}) collective-permute-start(bf16[64,2048]{1,0:T(8,128)(2,1)} %get-tuple-element.415), channel_id=1, source_target_pairs={{0,14},{1,15},{2,12},{3,13},{4,10},{5,11},{6,8},{7,9},{8,6},{9,7},... | collective-permute-start | bytes 786440 | tf_op jit(solution)/shard_map/ppermute | solution.py:203
  109.3 4.3 %collective-permute-start.11 = (bf16[256,2048]{1,0:T(8,128)(2,1)S(1)}, bf16[256,2048]{1,0:T(8,128)(2,1)S(1)}, u32[]{:S(2)}, u32[]{:S(2)}) collective-permute-start(bf16[256,2048]{1,0:T(8,128)(2,1)S(1)} %get-tuple-element.241), channel_id=1, source_target_pairs={{0,1},{1,0},{2,3},{3,2},{4,5},{5,4},{6,7},{7,6},{8,9},{9,8},{10,11... | collective-permute-start | bytes 3145736 | tf_op jit(solution)/shard_map/cond/branch_1_fun/ppermute | solution.py:206
  109.3 38.9 %all-to-all-start.2 = ((bf16[4,64,2048]{2,1,0:T(8,128)(2,1)}), bf16[4,64,2048]{2,1,0:T(8,128)(2,1)}, u32[]{:S(2)}, u32[]{:S(2)}) async-start(bf16[4,64,2048]{2,1,0:T(8,128)(2,1)} %bitcast.7), calls=%async_computation.2 | async-start | bytes 2097152 | tf_op jit(solution)/shard_map/cond/branch_1_fun/all_to_all | solution.py:223
  117.5 6.6 %collective-permute-start.12 = (bf16[256,2048]{1,0:T(8,128)(2,1)}, bf16[256,2048]{1,0:T(8,128)(2,1)}, u32[]{:S(2)}, u32[]{:S(2)}) collective-permute-start(bf16[256,2048]{1,0:T(8,128)(2,1)} %get-tuple-element.243), channel_id=1, source_target_pairs={{0,1},{1,0},{2,3},{3,2},{4,5},{5,4},{6,7},{7,6},{8,9},{9,8},{10,11... | collective-permute-start | bytes 3145736 | tf_op jit(solution)/shard_map/cond/branch_1_fun/ppermute | solution.py:206
  148.2 8.7 %copy-start.7 = (f32[32,16,16]{0,2,1:T(8,128)}, f32[32,16,16]{0,2,1:T(8,128)S(1)}, u32[]{:S(2)}) copy-start(f32[32,16,16]{0,2,1:T(8,128)S(1)} %get-tuple-element.558) | copy-start | bytes 98308
  148.2 8.7 %copy-start.10 = (s32[8]{0:T(128)S(1)}, s32[8]{0:T(128)}, u32[]{:S(2)}) copy-start(s32[8]{0:T(128)} %copy-done.9) | copy-start | bytes 100
  148.3 45.5 %all-to-all-start.3 = ((bf16[4,64,2048]{2,1,0:T(8,128)(2,1)}), bf16[4,64,2048]{2,1,0:T(8,128)(2,1)}, u32[]{:S(2)}, u32[]{:S(2)}) async-start(bf16[4,64,2048]{2,1,0:T(8,128)(2,1)} %bitcast.32), calls=%async_computation.3 | async-start | bytes 2097152 | tf_op jit(solution)/shard_map/all_to_all | solution.py:223
  152.6 30.2 %collective-permute-start.25 = (bf16[64,2048]{1,0:T(8,128)(2,1)}, bf16[64,2048]{1,0:T(8,128)(2,1)}, u32[]{:S(2)}, u32[]{:S(2)}) collective-permute-start(bf16[64,2048]{1,0:T(8,128)(2,1)} %get-tuple-element.442), channel_id=1, source_target_pairs={{0,8},{1,9},{2,10},{3,11},{4,12},{5,13},{6,14},{7,15},{8,0},{9,1},... | collective-permute-start | bytes 786440 | tf_op jit(solution)/shard_map/ppermute | solution.py:203
  155.2 27.5 %collective-permute-start.26 = (bf16[64,2048]{1,0:T(8,128)(2,1)}, bf16[64,2048]{1,0:T(8,128)(2,1)}, u32[]{:S(2)}, u32[]{:S(2)}) collective-permute-start(bf16[64,2048]{1,0:T(8,128)(2,1)} %get-tuple-element.443), channel_id=1, source_target_pairs={{0,12},{1,13},{2,14},{3,15},{4,8},{5,9},{6,10},{7,11},{8,4},{9,5},... | collective-permute-start | bytes 786440 | tf_op jit(solution)/shard_map/ppermute | solution.py:203
  156.9 36.9 %copy-start.1 = (bf16[512,2048]{1,0:T(8,128)(2,1)S(1)}, bf16[512,2048]{1,0:T(8,128)(2,1)}, u32[]{:S(2)}) copy-start(bf16[512,2048]{1,0:T(8,128)(2,1)} %a.3) | copy-start | bytes 6291460
  161.5 9.0 %collective-permute-start.6 = (bf16[4,32,512]{2,1,0:T(8,128)(2,1)S(1)}, bf16[4,32,512]{2,1,0:T(8,128)(2,1)S(1)}, u32[]{:S(2)}, u32[]{:S(2)}) collective-permute-start(bf16[4,32,512]{2,1,0:T(8,128)(2,1)S(1)} %get-tuple-element.573), channel_id=1, source_target_pairs={{0,2},{1,3},{2,0},{3,1},{4,6},{5,7},{6,4},{7,5},{8,10},{9,11},{10,... | collective-permute-start | bytes 393224 | tf_op jit(solution)/shard_map/cond/branch_1_fun/ppermute | solution.py:206
  163.1 9.1 %collective-permute-start.7 = (bf16[4,32,512]{2,1,0:T(8,128)(2,1)S(1)}, bf16[4,32,512]{2,1,0:T(8,128)(2,1)S(1)}, u32[]{:S(2)}, u32[]{:S(2)}) collective-permute-start(bf16[4,32,512]{2,1,0:T(8,128)(2,1)S(1)} %get-tuple-element.574), channel_id=1, source_target_pairs={{0,3},{1,2},{2,1},{3,0},{4,7},{5,6},{6,5},{7,4},{8,11},{9,10},{10,... | collective-permute-start | bytes 393224 | tf_op jit(solution)/shard_map/cond/branch_1_fun/ppermute | solution.py:206
  163.1 9.0 %collective-permute-start.5 = (bf16[4,32,512]{2,1,0:T(8,128)(2,1)S(1)}, bf16[4,32,512]{2,1,0:T(8,128)(2,1)S(1)}, u32[]{:S(2)}, u32[]{:S(2)}) collective-permute-start(bf16[4,32,512]{2,1,0:T(8,128)(2,1)S(1)} %fusion.17), channel_id=1, source_target_pairs={{0,1},{1,0},{2,3},{3,2},{4,5},{5,4},{6,7},{7,6},{8,9},{9,8},{10,11... | collective-permute-start | bytes 393224 | tf_op jit(solution)/shard_map/cond/branch_1_fun/ppermute | solution.py:206
  172.2 9.2 %collective-permute-start.10 = (bf16[32,512]{1,0:T(8,128)(2,1)S(1)}, bf16[32,512]{1,0:T(8,128)(2,1)S(1)}, u32[]{:S(2)}, u32[]{:S(2)}) collective-permute-start(bf16[32,512]{1,0:T(8,128)(2,1)S(1)} %get-tuple-element.576), channel_id=1, source_target_pairs={{0,12},{1,13},{2,14},{3,15},{4,8},{5,9},{6,10},{7,11},{8,4},{9,5},... | collective-permute-start | bytes 98312 | tf_op jit(solution)/shard_map/cond/branch_1_fun/ppermute | solution.py:203
  175.8 5.6 %collective-permute-start.8 = (bf16[32,512]{1,0:T(8,128)(2,1)S(1)}, bf16[32,512]{1,0:T(8,128)(2,1)S(1)}, u32[]{:S(2)}, u32[]{:S(2)}) collective-permute-start(bf16[32,512]{1,0:T(8,128)(2,1)S(1)} %get-tuple-element.575), channel_id=1, source_target_pairs={{0,4},{1,5},{2,6},{3,7},{4,0},{5,1},{6,2},{7,3},{8,12},{9,13},{10,... | collective-permute-start | bytes 98312 | tf_op jit(solution)/shard_map/cond/branch_1_fun/ppermute | solution.py:203
  175.8 6.9 %collective-permute-start.9 = (bf16[32,512]{1,0:T(8,128)(2,1)S(1)}, bf16[32,512]{1,0:T(8,128)(2,1)S(1)}, u32[]{:S(2)}, u32[]{:S(2)}) collective-permute-start(bf16[32,512]{1,0:T(8,128)(2,1)S(1)} %get-tuple-element.577), channel_id=1, source_target_pairs={{0,8},{1,9},{2,10},{3,11},{4,12},{5,13},{6,14},{7,15},{8,0},{9,1},... | collective-permute-start | bytes 98312 | tf_op jit(solution)/shard_map/cond/branch_1_fun/ppermute | solution.py:203
  182.8 4.5 %collective-permute-start.27 = (bf16[32,512]{1,0:T(8,128)(2,1)S(1)}, bf16[32,512]{1,0:T(8,128)(2,1)S(1)}, u32[]{:S(2)}, u32[]{:S(2)}) collective-permute-start(bf16[32,512]{1,0:T(8,128)(2,1)S(1)} %get-tuple-element.645), channel_id=1, source_target_pairs={{0,4},{1,5},{2,6},{3,7},{4,0},{5,1},{6,2},{7,3},{8,12},{9,13},{10,... | collective-permute-start | bytes 98312 | tf_op jit(solution)/shard_map/ppermute | solution.py:203
  182.8 5.4 %collective-permute-start.28 = (bf16[32,512]{1,0:T(8,128)(2,1)S(1)}, bf16[32,512]{1,0:T(8,128)(2,1)S(1)}, u32[]{:S(2)}, u32[]{:S(2)}) collective-permute-start(bf16[32,512]{1,0:T(8,128)(2,1)S(1)} %get-tuple-element.645), channel_id=1, source_target_pairs={{0,8},{1,9},{2,10},{3,11},{4,12},{5,13},{6,14},{7,15},{8,0},{9,1},... | collective-permute-start | bytes 98312 | tf_op jit(solution)/shard_map/ppermute | solution.py:203
  186.0 5.7 %collective-permute-start.29 = (bf16[32,512]{1,0:T(8,128)(2,1)S(1)}, bf16[32,512]{1,0:T(8,128)(2,1)S(1)}, u32[]{:S(2)}, u32[]{:S(2)}) collective-permute-start(bf16[32,512]{1,0:T(8,128)(2,1)S(1)} %get-tuple-element.645), channel_id=1, source_target_pairs={{0,12},{1,13},{2,14},{3,15},{4,8},{5,9},{6,10},{7,11},{8,4},{9,5},... | collective-permute-start | bytes 98312 | tf_op jit(solution)/shard_map/ppermute | solution.py:203
  191.8 22.3 %collective-permute-start.30 = (bf16[64,2048]{1,0:T(8,128)(2,1)}, bf16[64,2048]{1,0:T(8,128)(2,1)S(1)}, u32[]{:S(2)}, u32[]{:S(2)}) collective-permute-start(bf16[64,2048]{1,0:T(8,128)(2,1)} %get-tuple-element.456), channel_id=1, source_target_pairs={{0,10},{1,11},{2,8},{3,9},{4,14},{5,15},{6,12},{7,13},{8,2},{9,3},... | collective-permute-start | bytes 786440 | tf_op jit(solution)/shard_map/ppermute | solution.py:203
  191.8 22.2 %collective-permute-start.31 = (bf16[64,2048]{1,0:T(8,128)(2,1)}, bf16[64,2048]{1,0:T(8,128)(2,1)S(1)}, u32[]{:S(2)}, u32[]{:S(2)}) collective-permute-start(bf16[64,2048]{1,0:T(8,128)(2,1)} %get-tuple-element.457), channel_id=1, source_target_pairs={{0,14},{1,15},{2,12},{3,13},{4,10},{5,11},{6,8},{7,9},{8,6},{9,7},... | collective-permute-start | bytes 786440 | tf_op jit(solution)/shard_map/ppermute | solution.py:203
  193.9 8.1 %collective-permute-start.2 = (bf16[4,32,512]{2,1,0:T(8,128)(2,1)S(1)}, bf16[4,32,512]{2,1,0:T(8,128)(2,1)S(1)}, u32[]{:S(2)}, u32[]{:S(2)}) collective-permute-start(bf16[4,32,512]{2,1,0:T(8,128)(2,1)S(1)} %pad_maximum_fusion.refs_0_), channel_id=1, source_target_pairs={{0,1},{1,0},{2,3},{3,2},{4,5},{5,4},{6,7},{7,6},{8,9},{9,8},{10,11... | collective-permute-start | bytes 393224 | tf_op jit(solution)/shard_map/cond/branch_1_fun/ppermute | solution.py:206
  194.0 17.1 %collective-permute-start.3 = (bf16[4,32,512]{2,1,0:T(8,128)(2,1)S(1)}, bf16[4,32,512]{2,1,0:T(8,128)(2,1)S(1)}, u32[]{:S(2)}, u32[]{:S(2)}) collective-permute-start(bf16[4,32,512]{2,1,0:T(8,128)(2,1)S(1)} %pad_maximum_fusion.refs_0_), channel_id=1, source_target_pairs={{0,2},{1,3},{2,0},{3,1},{4,6},{5,7},{6,4},{7,5},{8,10},{9,11},{10,... | collective-permute-start | bytes 393224 | tf_op jit(solution)/shard_map/cond/branch_1_fun/ppermute | solution.py:206
  195.1 18.3 %collective-permute-start.4 = (bf16[4,32,512]{2,1,0:T(8,128)(2,1)S(1)}, bf16[4,32,512]{2,1,0:T(8,128)(2,1)S(1)}, u32[]{:S(2)}, u32[]{:S(2)}) collective-permute-start(bf16[4,32,512]{2,1,0:T(8,128)(2,1)S(1)} %pad_maximum_fusion.refs_0_), channel_id=1, source_target_pairs={{0,3},{1,2},{2,1},{3,0},{4,7},{5,6},{6,5},{7,4},{8,11},{9,10},{10,... | collective-permute-start | bytes 393224 | tf_op jit(solution)/shard_map/cond/branch_1_fun/ppermute | solution.py:206
  195.9 2.5 %copy-start.4 = (bf16[512,512]{1,0:T(8,128)(2,1)S(1)}, bf16[512,512]{1,0:T(8,128)(2,1)}, u32[]{:S(2)}) copy-start(bf16[512,512]{1,0:T(8,128)(2,1)} %get-tuple-element.277.matrix) | copy-start | bytes 1572868 | tf_op jit(solution)/shard_map/cond
  214.0 1.3 copy-start.5
  214.0 1.6 copy-start.6
  215.7 1.3 copy-start.2

commit v5 on v4

--- a/solution.py
+++ b/solution.py
@@ -331,12 +331,12 @@
     gateds = dict(zip(cross_ks, gated[1:]))
     first, last = cross_ks[::2], cross_ks[1::2]
     arrived = send_cross({k: gateds[k] for k in first})
-    gated_side = send_side(gated[0])
 
     def add(kept, received):
         return sum((x.astype(F32) for x in received), kept)
 
-    def home(backs, permuted, reorder, starts):
+    def home(side, backs, permuted, reorder, starts):
+        side = send_side(side)
         terms = by_columns(
             functools.partial(partial_kernel, slab),
             [permuted] + backs,
@@ -352,15 +352,20 @@
             terms[:, i // 2], jnp.bitwise_xor(e, i % 2), 1, keepdims=False
         )
         terms = add(mine(0), [near(mine(i).astype(BF16), i) for i in (1, 2, 3)])
-        own = add(terms[0], [chip(terms[k].astype(BF16), 2 * k) for k in range(1, far)])
-        return own.astype(BF16)
-
-    own = phase(home, backs, permuted, reorder, relative[:far] * slab)
+        terms = terms.astype(BF16)
+        got = [terms] + [chip(terms, 2 * k) for k in range(1, far)]
+        got = [
+            jnp.stack([g[k ^ j] for j in range(far)]).astype(F32) if k else g.astype(F32)
+            for k, g in enumerate(got)
+        ]
+        while len(got) > 1:
+            got = [x + y for x, y in zip(got[::2], got[1::2])]
+        return got[0].astype(BF16), side
+
+    own, gated_side = phase(home, gated[0], backs, permuted, reorder, relative[:far] * slab)
     rest, own, arrived = lax.optimization_barrier(
         ({k: gateds[k] for k in last}, own, arrived)
     )
-    got = [own] + [chip(own, 2 * k) for k in range(1, far)]
-    rest, got = after(rest, got)
     late = send_cross(rest)
 
     dynamic = slab % 16 == 0
@@ -373,10 +378,9 @@
         return total
 
     def finish(got, position, backs, home_factor, cotangent, starts, slabs):
-        first = jnp.stack(got)
         rows = in_order(
             position,
-            [first] + [near(first, i) for i in (1, 2, 3)],
+            [got] + [near(got, i) for i in (1, 2, 3)],
             1.0 / math.sqrt(count * width),
         )
         grad_signal = by_columns(whole_kernel, backs, [block], width, (), [home_factor])[0]
@@ -392,7 +396,7 @@
     position = jnp.bitwise_xor(h, k) * 2 + jnp.bitwise_xor(e, every // far % 2)
     grad_block, grad_signal, grad_gate = phase(
         finish,
-        got,
+        own,
         position.astype(jnp.int32),
         backs,
         home_factor,

time: 218 us -> 216 us (level)
    ppermute x10, waiting for transfers between devices: 21.9 us -> 19.3 us  [near(): return lax.ppermute(x, 'seq', [(s, s ^ i) for s in range(count)])]
    ppermute x22 -> x19, starting transfers between devices: 41.2 us -> 40.5 us  [chip(): return lax.ppermute(x, 'seq', [(s, s ^ 2 * k) for s in range(count)])]
    ppermute x22 -> x19, waiting for transfers between devices: 10.6 us -> 10.9 us  [chip(): return lax.ppermute(x, 'seq', [(s, s ^ 2 * k) for s in range(count)])]
  transfers between devices with their start and end apart: 35 -> 32, of which waited for: 11 -> 10; matrix products, arithmetic and copies ran while one was open for 9% -> 10% of each run, Pallas kernels for 18% -> 18%
where the time goes in v5:
time: 216 us; the launch traced here: 215 us
  waiting for transfers between devices  64.5 us (30%)
  starting transfers between devices  58.7 us (27%)
  Pallas kernels  39.4 us (18%)
  blocking collectives  22.4 us (10%)
  other arithmetic  9.71 us (4%)
  matrix products  9.56 us (4%)
  local copies, waits for them, and re-layouts  8.64 us (4%)
    ppermute x19, starting transfers between devices, chip(): return lax.ppermute(x, 'seq', [(s, s ^ 2 * k) for s in range(count)])  40.5 us
    pallas_call x11, Pallas kernels, by_columns(): pl.pallas_call(kernel, grid=(width // columns,), in_specs=[pl.BlockSpec(m...  38.7 us
    all_to_all x3, waiting for transfers between devices, send_side(): lax.all_to_all(x, 'seq', split_axis=0, concat_axis=0, tiled=True, axis_in...  34.3 us
    all_to_all x1, blocking collectives, send_side(): lax.all_to_all(x, 'seq', split_axis=0, concat_axis=0, tiled=True, axis_in...  22.4 us
    ppermute x10, waiting for transfers between devices, near(): return lax.ppermute(x, 'seq', [(s, s ^ i) for s in range(count)])  19.3 us
    all_to_all x3, starting transfers between devices, send_side(): lax.all_to_all(x, 'seq', split_axis=0, concat_axis=0, tiled=True, axis_in...  12.9 us
    ppermute x19, waiting for transfers between devices, chip(): return lax.ppermute(x, 'seq', [(s, s ^ 2 * k) for s in range(count)])  10.9 us
    ppermute x10, starting transfers between devices, near(): return lax.ppermute(x, 'seq', [(s, s ^ i) for s in range(count)])  5.35 us
  transfers between devices with their start and end apart: 32, of which 10 were waited for; matrix products, arithmetic and copies ran while one was open for 10% of the time, Pallas kernels for 18%

profile of v5, /device:TPU:0, one launch (start us, length us, event | category | flops | bytes accessed | tf_op | source)
XLA Modules:
  0.0 214.7 jit_solution(9501911153455456688)
XLA Ops:
  0.7 2.7 %dynamic-slice_multiply_fusion.1 = (bf16[64,2048]{1,0:T(8,128)(2,1)}, bf16[64,2048]{1,0:T(8,128)(2,1)}, bf16[64,2048]{1,0:T(8,128)(2,1)}, bf16[64,2048]{1,0:T(8,128)(2,1)}) fusion(bf16[512,2048]{1,0:T(8,128)(2,1)} %param.19, s32[]{:T(128)S(6)} %select_n.112, bf16[512,2048]{1,0:T(8,128)(2,1)} %a.3, s32[]{:T(128)S(6)} %select_n.111, s32[]{:T(128)S(6)} %select_n.110, ...), kind=kLoop, calls=%fused_computation.56 | loop fusion | flops 2097152 | bytes 3145744 | tf_op jit(solution)/shard_map/mul | solution.py:248
  3.4 4.0 %collective-permute-start.13 = (bf16[64,2048]{1,0:T(8,128)(2,1)}, bf16[64,2048]{1,0:T(8,128)(2,1)}, u32[]{:S(2)}, u32[]{:S(2)}) collective-permute-start(bf16[64,2048]{1,0:T(8,128)(2,1)} %get-tuple-element.377), channel_id=1, source_target_pairs={{0,8},{1,9},{2,10},{3,11},{4,12},{5,13},{6,14},{7,15},{8,0},{9,1},... | collective-permute-start | bytes 786440 | tf_op jit(solution)/shard_map/ppermute | solution.py:203
  8.7 3.6 %collective-permute-start.15 = (bf16[64,2048]{1,0:T(8,128)(2,1)}, bf16[64,2048]{1,0:T(8,128)(2,1)}, u32[]{:S(2)}, u32[]{:S(2)}) collective-permute-start(bf16[64,2048]{1,0:T(8,128)(2,1)} %get-tuple-element.379), channel_id=1, source_target_pairs={{0,12},{1,13},{2,14},{3,15},{4,8},{5,9},{6,10},{7,11},{8,4},{9,5},... | collective-permute-start | bytes 786440 | tf_op jit(solution)/shard_map/ppermute | solution.py:203
  14.4 19.3 %conditional.6 = (bf16[256,2048]{1,0:T(8,128)(2,1)}, bf16[64,2048]{1,0:T(8,128)(2,1)}, bf16[64,2048]{1,0:T(8,128)(2,1)}, bf16[64,2048]{1,0:T(8,128)(2,1)}, bf16[...) conditional(s32[]{:T(128)} %bitcast.23, () %tuple.70, ...), branch_computations={%region_0.1_spmd, %region_1.2_spmd} | conditional | flops 1622943616 | bytes 8788276 | solution.py:200
  15.4 1.5 convolution_convert_fusion.2.matrix
  16.9 4.2 %convolution_convert_fusion.rows = bf16[512,2048]{1,0:T(8,128)(2,1)} fusion(bf16[512,2048]{1,0:T(8,128)(2,1)} %get-tuple-element.197, s32[512]{0:T(512)S(1)} %get-tuple-element.196), kind=kOutput, calls=%fused_computation | convolution fusion | flops 1075052544 | bytes 4196352 | tf_op jit(solution)/shard_map/cond/branch_1_fun/dot_general | solution.py:266
  21.2 4.4 %branch_1_fun.12 = (bf16[256,2048]{1,0:T(8,128)(2,1)}, bf16[64,2048]{1,0:T(8,128)(2,1)}, bf16[64,2048]{1,0:T(8,128)(2,1)}, bf16[64,2048]{1,0:T(8,128)(2,1)}, bf16[64,2048]{1,0:T(8,128)(2,1)}) custom-call(bf16[512,512]{1,0:T(8,128)(2,1)S(1)} %convolution_convert_fusion.2.matrix, bf16[512,2048]{1,0:T(8,128)(2,1)} %convolution_convert_fusion.rows), custom_call_target="tpu_custom_call" | custom-call | tf_op jit(solution)/shard_map/cond/branch_1_fun/pallas_call | solution.py:159
  28.0 2.0 fusion
  30.1 1.9 copy.54
  34.7 2.6 %dynamic-slice_multiply_fusion = bf16[256,2048]{1,0:T(8,128)(2,1)} fusion(bf16[512,2048]{1,0:T(8,128)(2,1)} %param.19, s32[]{:T(128)S(6)} %select_n.114, bf16[512,2048]{1,0:T(8,128)(2,1)S(1)} %copy-done), kind=kLoop, calls=%fused_computation.54 | loop fusion | flops 2097152 | bytes 3145732 | tf_op jit(solution)/shard_map/mul | solution.py:250
  37.2 22.4 %conditional.7 = (bf16[256,2048]{1,0:T(8,128)(2,1)S(1)}) conditional(s32[]{:T(128)} %bitcast.23, () %tuple.73, bf16[256,2048]{1,0:T(8,128)(2,1)} %dynamic-slice_multiply_fusion), branch_computations={%region_2.3_spmd, %region_3.4_spmd} | conditional | bytes 2097160 | solution.py:200
  37.2 22.4 %all_to_all.36 = bf16[4,64,2048]{2,1,0:T(8,128)(2,1)S(1)} all-to-all(bf16[4,64,2048]{2,1,0:T(8,128)(2,1)} %bitcast.68), channel_id=1, replica_groups={{0,2,4,6},{1,3,5,7},{8,10,12,14},{9,11,13,15},{16,18,20,22},{17,19,21,2..., dimensions={0} | all-to-all | bytes 2097152 | tf_op jit(solution)/shard_map/cond/branch_1_fun/all_to_all | solution.py:223
  59.7 3.0 %collective-permute-start.18 = (bf16[64,2048]{1,0:T(8,128)(2,1)}, bf16[64,2048]{1,0:T(8,128)(2,1)}, u32[]{:S(2)}, u32[]{:S(2)}) collective-permute-start(bf16[64,2048]{1,0:T(8,128)(2,1)} %get-tuple-element.394), channel_id=1, source_target_pairs={{0,10},{1,11},{2,8},{3,9},{4,14},{5,15},{6,12},{7,13},{8,2},{9,3},... | collective-permute-start | bytes 786440 | tf_op jit(solution)/shard_map/ppermute | solution.py:203
  62.7 1.5 collective-permute-start.19
  64.3 3.2 %collective-permute-start.20 = (bf16[64,2048]{1,0:T(8,128)(2,1)}, bf16[64,2048]{1,0:T(8,128)(2,1)}, u32[]{:S(2)}, u32[]{:S(2)}) collective-permute-start(bf16[64,2048]{1,0:T(8,128)(2,1)} %get-tuple-element.396), channel_id=1, source_target_pairs={{0,14},{1,15},{2,12},{3,13},{4,10},{5,11},{6,8},{7,9},{8,6},{9,7},... | collective-permute-start | bytes 786440 | tf_op jit(solution)/shard_map/ppermute | solution.py:203
  67.5 31.2 %conditional.8 = (bf16[256,2048]{1,0:T(8,128)(2,1)}, bf16[256,2048]{1,0:T(8,128)(2,1)}, bf16[64,2048]{1,0:T(8,128)(2,1)}, bf16[64,2048]{1,0:T(8,128)(2,1)}, bf16...) conditional(s32[]{:T(128)} %bitcast.23, () %tuple.68, ...), branch_computations={%region_4.5_spmd, %region_5.6_spmd} | conditional | bytes 12583088 | solution.py:200
  67.5 3.5 %branch_1_fun.13 = (bf16[256,2048]{1,0:T(8,128)(2,1)}, bf16[256,2048]{1,0:T(8,128)(2,1)S(1)}) custom-call(s32[1]{0:T(128)} %get-tuple-element.208.core, bf16[256,2048]{1,0:T(8,128)(2,1)S(1)} %get-tuple-element.210.refs_0_, bf16[64,2048]{1,0:T(8,128)(2,1)} %get-tuple-element.211.refs_1_, bf16[64,2048]{1,0:T(8,128)(2,1)} %get-tuple-element.212.refs_2_, ...), custom_call_target="tpu_custom_call" | custom-call | tf_op jit(solution)/shard_map/cond/branch_1_fun/pallas_call | solution.py:159
  71.0 4.2 %all-to-all-start.1 = ((bf16[4,64,2048]{2,1,0:T(8,128)(2,1)}), bf16[4,64,2048]{2,1,0:T(8,128)(2,1)}, u32[]{:S(2)}, u32[]{:S(2)}) async-start(bf16[4,64,2048]{2,1,0:T(8,128)(2,1)} %bitcast.5), calls=%async_computation.1 | async-start | bytes 2097152 | tf_op jit(solution)/shard_map/cond/branch_1_fun/all_to_all | solution.py:223
  76.5 3.5 %branch_1_fun.14 = (bf16[256,2048]{1,0:T(8,128)(2,1)S(1)}, bf16[256,2048]{1,0:T(8,128)(2,1)S(1)}) custom-call(bf16[512,512]{1,0:T(8,128)(2,1)S(1)} %copy.19.matrix, bf16[256,2048]{1,0:T(8,128)(2,1)} %get-tuple-element.609.own, bf16[256,2048]{1,0:T(8,128)(2,1)} %collective-permute-done.other), custom_call_target="tpu_custom_call" | custom-call | tf_op jit(solution)/shard_map/cond/branch_1_fun/pallas_call | solution.py:159
  80.6 2.3 %collective-permute-done.1.other = bf16[256,2048]{1,0:T(8,128)(2,1)S(1)} collective-permute-done((bf16[256,2048]{1,0:T(8,128)(2,1)S(1)}, bf16[256,2048]{1,0:T(8,128)(2,1)S(1)}, u32[]{:S(2)}, u32[]{:S(2)}) %collective-permute-start.1) | collective-permute-done | bytes 1048608 | tf_op jit(solution)/shard_map/cond/branch_1_fun/ppermute | solution.py:206
  82.9 2.0 branch_1_fun.15
  84.9 13.8 %all-to-all-done.1 = bf16[4,64,2048]{2,1,0:T(8,128)(2,1)} async-done(((bf16[4,64,2048]{2,1,0:T(8,128)(2,1)}), bf16[4,64,2048]{2,1,0:T(8,128)(2,1)}, u32[]{:S(2)}, u32[]{:S(2)}) %all-to-all-start.1) | async-done | bytes 1048608 | tf_op jit(solution)/shard_map/cond/branch_1_fun/all_to_all | solution.py:223
  98.7 3.3 %collective-permute-start.21 = (bf16[64,2048]{1,0:T(8,128)(2,1)}, bf16[64,2048]{1,0:T(8,128)(2,1)}, u32[]{:S(2)}, u32[]{:S(2)}) collective-permute-start(bf16[64,2048]{1,0:T(8,128)(2,1)} %get-tuple-element.398), channel_id=1, source_target_pairs={{0,8},{1,9},{2,10},{3,11},{4,12},{5,13},{6,14},{7,15},{8,0},{9,1},... | collective-permute-start | bytes 786440 | tf_op jit(solution)/shard_map/ppermute | solution.py:203
  102.6 3.3 %collective-permute-start.23 = (bf16[64,2048]{1,0:T(8,128)(2,1)}, bf16[64,2048]{1,0:T(8,128)(2,1)}, u32[]{:S(2)}, u32[]{:S(2)}) collective-permute-start(bf16[64,2048]{1,0:T(8,128)(2,1)} %get-tuple-element.400), channel_id=1, source_target_pairs={{0,12},{1,13},{2,14},{3,15},{4,8},{5,9},{6,10},{7,11},{8,4},{9,5},... | collective-permute-start | bytes 786440 | tf_op jit(solution)/shard_map/ppermute | solution.py:203
  106.8 41.4 %conditional.9 = (bf16[256,2048]{1,0:T(8,128)(2,1)}, bf16[256,2048]{1,0:T(8,128)(2,1)}, bf16[64,2048]{1,0:T(8,128)(2,1)}, bf16[64,2048]{1,0:T(8,128)(2,1)}, bf16...) conditional(s32[]{:T(128)} %bitcast.23, () %tuple.77, ...), branch_computations={%region_6.7_spmd, %region_7.8_spmd} | conditional | flops 1843200 | bytes 12518056 | solution.py:200
  106.8 2.5 %branch_1_fun.16 = (bf16[256,2048]{1,0:T(8,128)(2,1)S(1)}, bf16[256,2048]{1,0:T(8,128)(2,1)S(1)}) custom-call(s32[1]{0:T(128)} %get-tuple-element.225.core, bf16[256,2048]{1,0:T(8,128)(2,1)} %get-tuple-element.227.refs_0_, bf16[64,2048]{1,0:T(8,128)(2,1)} %get-tuple-element.228.refs_1_, bf16[64,2048]{1,0:T(8,128)(2,1)} %get-tuple-element.229.refs_2_, ...), custom_call_target="tpu_custom_call" | custom-call | tf_op jit(solution)/shard_map/cond/branch_1_fun/pallas_call | solution.py:159
  109.3 4.3 %all-to-all-start.3 = ((bf16[4,64,2048]{2,1,0:T(8,128)(2,1)}), bf16[4,64,2048]{2,1,0:T(8,128)(2,1)}, u32[]{:S(2)}, u32[]{:S(2)}) async-start(bf16[4,64,2048]{2,1,0:T(8,128)(2,1)} %bitcast.7), calls=%async_computation.3 | async-start | bytes 2097152 | tf_op jit(solution)/shard_map/cond/branch_1_fun/all_to_all | solution.py:223
  113.6 3.9 %branch_1_fun.17 = (bf16[256,2048]{1,0:T(8,128)(2,1)S(1)}, bf16[256,2048]{1,0:T(8,128)(2,1)}) custom-call(bf16[512,512]{1,0:T(8,128)(2,1)} %get-tuple-element.226.matrix, bf16[256,2048]{1,0:T(8,128)(2,1)S(1)} %get-tuple-element.232.own.refs_2_, bf16[256,2048]{1,0:T(8,128)(2,1)S(1)} %collective-permute-done.11.other.refs_3_), custom_call_target="tpu_custom_call" | custom-call | tf_op jit(solution)/shard_map/cond/branch_1_fun/pallas_call | solution.py:159
  118.1 4.8 %branch_1_fun.19 = f32[512,16]{1,0:T(8,128)S(1)} custom-call(bf16[512,512]{1,0:T(8,128)(2,1)S(1)} %convert_element_type.65.same, bf16[512,16]{1,0:T(8,128)(2,1)} %get-tuple-element.242.spread_out, bf16[256,2048]{1,0:T(8,128)(2,1)} %get-tuple-element.243.refs_0_, bf16[256,2048]{1,0:T(8,128)(2,1)} %get-tuple-element.244.refs_1_, ...), custom_call_target="tpu_custom_call" | custom-call | tf_op jit(solution)/shard_map/cond/branch_1_fun/pallas_call | solution.py:159
  124.1 3.6 %branch_1_fun.18 = (bf16[256,2048]{1,0:T(8,128)(2,1)}, bf16[64,2048]{1,0:T(8,128)(2,1)}, bf16[64,2048]{1,0:T(8,128)(2,1)}, bf16[64,2048]{1,0:T(8,128)(2,1)}, bf16[64,2048]{1,0:T(8,128)(2,1)}) custom-call(s32[1]{0:T(128)} %get-tuple-element.225.core, bf16[256,2048]{1,0:T(8,128)(2,1)S(1)} %get-tuple-element.234.own, ...), custom_call_target="tpu_custom_call" | custom-call | tf_op jit(solution)/shard_map/cond/branch_1_fun/pallas_call | solution.py:159
  127.7 20.5 %all-to-all-done.3 = bf16[4,64,2048]{2,1,0:T(8,128)(2,1)} async-done(((bf16[4,64,2048]{2,1,0:T(8,128)(2,1)}), bf16[4,64,2048]{2,1,0:T(8,128)(2,1)}, u32[]{:S(2)}, u32[]{:S(2)}) %all-to-all-start.3) | async-done | bytes 1048608 | tf_op jit(solution)/shard_map/cond/branch_1_fun/all_to_all | solution.py:223
  148.3 2.6 %collective-permute-start.25 = (bf16[64,2048]{1,0:T(8,128)(2,1)}, bf16[64,2048]{1,0:T(8,128)(2,1)}, u32[]{:S(2)}, u32[]{:S(2)}) collective-permute-start(bf16[64,2048]{1,0:T(8,128)(2,1)} %get-tuple-element.430), channel_id=1, source_target_pairs={{0,8},{1,9},{2,10},{3,11},{4,12},{5,13},{6,14},{7,15},{8,0},{9,1},... | collective-permute-start | bytes 786440 | tf_op jit(solution)/shard_map/ppermute | solution.py:203
  151.6 35.9 %conditional.10 = (bf16[4,32,512]{2,1,0:T(8,128)(2,1)S(1)}, bf16[256,2048]{1,0:T(8,128)(2,1)}) conditional(s32[]{:T(128)} %bitcast.23, () %tuple.80, (s32[8]{0:T(128)}, bf16[512,512]{1,0:T(8,128)(2,1)}, bf16[512,2048]{1,0:T(8,128)(2,1)}, bf16[256,2048]{1,0:T(8,128)(2,1)}, bf16[64,2048]{1,0:T(8,128)(2,1)}, /*index=5*/bf16[64,2048]{1,0:T(8,128)(2,1)}, ...), branch_computations={%region_8.9_spmd, %region_9.10_spmd} | conditional | flops 1441803 | bytes 10879392 | solution.py:200
  151.6 4.4 %all-to-all-start.2 = ((bf16[4,64,2048]{2,1,0:T(8,128)(2,1)}), bf16[4,64,2048]{2,1,0:T(8,128)(2,1)}, u32[]{:S(2)}, u32[]{:S(2)}) async-start(bf16[4,64,2048]{2,1,0:T(8,128)(2,1)} %bitcast.17), calls=%async_computation.2 | async-start | bytes 2097152 | tf_op jit(solution)/shard_map/cond/branch_1_fun/all_to_all | solution.py:223
  156.6 4.4 %branch_1_fun.20 = f32[512,512]{1,0:T(8,128)S(1)} custom-call(s32[4]{0:T(128)S(1)} %slice_multiply_fusion.starts, bf16[512,512]{1,0:T(8,128)(2,1)} %get-tuple-element.247.order, bf16[512,2048]{1,0:T(8,128)(2,1)} %get-tuple-element.248.right, bf16[256,2048]{1,0:T(8,128)(2,1)} %get-tuple-element.249.side, bf16[64,2048]{1,0:T(8,128)(2,1)} %get-tuple-element.250.refs_0_, ...), custom_call_target="tpu_custom_call" | custom-call | tf_op jit(solution)/shard_map/cond/branch_1_fun/pallas_call | solution.py:159
  161.1 2.0 collective-permute-start.6
  163.4 3.9 %collective-permute-done.6 = bf16[4,32,512]{2,1,0:T(8,128)(2,1)S(1)} collective-permute-done((bf16[4,32,512]{2,1,0:T(8,128)(2,1)S(1)}, bf16[4,32,512]{2,1,0:T(8,128)(2,1)S(1)}, u32[]{:S(2)}, u32[]{:S(2)}) %collective-permute-start.6) | collective-permute-done | bytes 131104 | tf_op jit(solution)/shard_map/cond/branch_1_fun/ppermute | solution.py:206
  167.3 1.7 collective-permute-done.7
  169.1 5.6 %collective-permute-start.10 = (bf16[4,32,512]{2,1,0:T(8,128)(2,1)S(1)}, bf16[4,32,512]{2,1,0:T(8,128)(2,1)S(1)}, u32[]{:S(2)}, u32[]{:S(2)}) collective-permute-start(bf16[4,32,512]{2,1,0:T(8,128)(2,1)S(1)} %fusion.17), channel_id=1, source_target_pairs={{0,12},{1,13},{2,14},{3,15},{4,8},{5,9},{6,10},{7,11},{8,4},{9,5},... | collective-permute-start | bytes 393224 | tf_op jit(solution)/shard_map/cond/branch_1_fun/ppermute | solution.py:203
  174.7 1.8 collective-permute-start.9
  177.8 7.4 %collective-permute-done.8 = bf16[4,32,512]{2,1,0:T(8,128)(2,1)S(1)} collective-permute-done((bf16[4,32,512]{2,1,0:T(8,128)(2,1)S(1)}, bf16[4,32,512]{2,1,0:T(8,128)(2,1)S(1)}, u32[]{:S(2)}, u32[]{:S(2)}) %collective-permute-start.8) | collective-permute-done | bytes 131104 | tf_op jit(solution)/shard_map/cond/branch_1_fun/ppermute | solution.py:203
  185.1 2.3 %collective-permute-done.9 = bf16[4,32,512]{2,1,0:T(8,128)(2,1)S(1)} collective-permute-done((bf16[4,32,512]{2,1,0:T(8,128)(2,1)S(1)}, bf16[4,32,512]{2,1,0:T(8,128)(2,1)S(1)}, u32[]{:S(2)}, u32[]{:S(2)}) %collective-permute-start.9) | collective-permute-done | bytes 131104 | tf_op jit(solution)/shard_map/cond/branch_1_fun/ppermute | solution.py:203
  188.2 3.3 %collective-permute-start.28 = (bf16[64,2048]{1,0:T(8,128)(2,1)}, bf16[64,2048]{1,0:T(8,128)(2,1)S(1)}, u32[]{:S(2)}, u32[]{:S(2)}) collective-permute-start(bf16[64,2048]{1,0:T(8,128)(2,1)} %get-tuple-element.439), channel_id=1, source_target_pairs={{0,14},{1,15},{2,12},{3,13},{4,10},{5,11},{6,8},{7,9},{8,6},{9,7},... | collective-permute-start | bytes 786440 | tf_op jit(solution)/shard_map/ppermute | solution.py:203
  191.6 20.1 %conditional.11 = (f32[512,512]{1,0:T(8,128)S(1)}, bf16[512,2048]{1,0:T(8,128)(2,1)S(1)}, bf16[512,2048]{1,0:T(8,128)(2,1)S(1)}) conditional(s32[]{:T(128)} %bitcast.23, () %tuple.67, (s32[]{:T(128)}, s32[16]{0:T(128)S(1)}, s32[16]{0:T(128)S(1)}, s32[16]{0:T(128)S(1)}, pred[16]{0:T(512)(128)(4,1)S(1)}, /*index=5*/s32[16]{0:T(128)S(1)}, ...), branch_computations={%region_10.11_spmd, %region_11.12_spmd} | conditional | flops 550 | bytes 5242912 | solution.py:200
  193.6 2.5 %branch_1_fun.23 = bf16[512,2048]{1,0:T(8,128)(2,1)S(1)} custom-call(s32[3]{0:T(128)S(1)} %pad_add_fusion.starts, bf16[512,2048]{1,0:T(8,128)(2,1)S(1)} %get-tuple-element.276.a, bf16[256,2048]{1,0:T(8,128)(2,1)} %get-tuple-element.277.refs_0_, bf16[64,2048]{1,0:T(8,128)(2,1)} %get-tuple-element.278.refs_1_, bf16[64,2048]{1,0:T(8,128)(2,1)} %get-tuple-element.279.refs_2_), custom_call_target="tpu_custom_call" | custom-call | tf_op jit(solution)/shard_map/cond/branch_1_fun/pallas_call | solution.py:159
  196.2 3.5 %branch_1_fun.22 = bf16[512,2048]{1,0:T(8,128)(2,1)S(1)} custom-call(bf16[512,512]{1,0:T(8,128)(2,1)S(1)} %copy-done.4, bf16[256,2048]{1,0:T(8,128)(2,1)} %get-tuple-element.268.refs_0_, bf16[64,2048]{1,0:T(8,128)(2,1)} %get-tuple-element.269.refs_1_, bf16[64,2048]{1,0:T(8,128)(2,1)} %get-tuple-element.270.refs_2_, ...), custom_call_target="tpu_custom_call" | custom-call | tf_op jit(solution)/shard_map/cond/branch_1_fun/pallas_call | solution.py:159
  199.7 9.4 %collective-permute-done.3.refs_2_ = bf16[4,32,512]{2,1,0:T(8,128)(2,1)S(1)} collective-permute-done((bf16[4,32,512]{2,1,0:T(8,128)(2,1)S(1)}, bf16[4,32,512]{2,1,0:T(8,128)(2,1)S(1)}, u32[]{:S(2)}, u32[]{:S(2)}) %collective-permute-start.3) | collective-permute-done | bytes 131104 | tf_op jit(solution)/shard_map/cond/branch_1_fun/ppermute | solution.py:206
  209.2 1.9 collective-permute-done.4.refs_3_
  (109 shorter events, 23.3 us)
Async XLA Ops:
  0.6 12.5 %copy-start.9 = (s32[512]{0:T(512)S(1)}, s32[512]{0:T(512)}, u32[]{:S(2)}) copy-start(s32[512]{0:T(512)} %param.23) | copy-start | bytes 6148
  0.6 13.8 %copy-start.8 = (bf16[32,16,16]{0,2,1:T(8,128)(2,1)S(1)}, bf16[32,16,16]{0,2,1:T(8,128)(2,1)}, u32[]{:S(2)}) copy-start(bf16[32,16,16]{0,2,1:T(8,128)(2,1)} %param.22) | copy-start | bytes 49156
  3.4 56.2 %collective-permute-start.13 = (bf16[64,2048]{1,0:T(8,128)(2,1)}, bf16[64,2048]{1,0:T(8,128)(2,1)}, u32[]{:S(2)}, u32[]{:S(2)}) collective-permute-start(bf16[64,2048]{1,0:T(8,128)(2,1)} %get-tuple-element.377), channel_id=1, source_target_pairs={{0,8},{1,9},{2,10},{3,11},{4,12},{5,13},{6,14},{7,15},{8,0},{9,1},... | collective-permute-start | bytes 786440 | tf_op jit(solution)/shard_map/ppermute | solution.py:203
  7.4 52.2 %collective-permute-start.14 = (bf16[64,2048]{1,0:T(8,128)(2,1)}, bf16[64,2048]{1,0:T(8,128)(2,1)}, u32[]{:S(2)}, u32[]{:S(2)}) collective-permute-start(bf16[64,2048]{1,0:T(8,128)(2,1)} %get-tuple-element.378), channel_id=1, source_target_pairs={{0,10},{1,11},{2,8},{3,9},{4,14},{5,15},{6,12},{7,13},{8,2},{9,3},... | collective-permute-start | bytes 786440 | tf_op jit(solution)/shard_map/ppermute | solution.py:203
  8.7 50.9 %collective-permute-start.15 = (bf16[64,2048]{1,0:T(8,128)(2,1)}, bf16[64,2048]{1,0:T(8,128)(2,1)}, u32[]{:S(2)}, u32[]{:S(2)}) collective-permute-start(bf16[64,2048]{1,0:T(8,128)(2,1)} %get-tuple-element.379), channel_id=1, source_target_pairs={{0,12},{1,13},{2,14},{3,15},{4,8},{5,9},{6,10},{7,11},{8,4},{9,5},... | collective-permute-start | bytes 786440 | tf_op jit(solution)/shard_map/ppermute | solution.py:203
  12.3 47.3 %collective-permute-start.16 = (bf16[64,2048]{1,0:T(8,128)(2,1)}, bf16[64,2048]{1,0:T(8,128)(2,1)}, u32[]{:S(2)}, u32[]{:S(2)}) collective-permute-start(bf16[64,2048]{1,0:T(8,128)(2,1)} %get-tuple-element.380), channel_id=1, source_target_pairs={{0,14},{1,15},{2,12},{3,13},{4,10},{5,11},{6,8},{7,9},{8,6},{9,7},... | collective-permute-start | bytes 786440 | tf_op jit(solution)/shard_map/ppermute | solution.py:203
  14.4 20.2 %copy-start = (bf16[512,2048]{1,0:T(8,128)(2,1)S(1)}, bf16[512,2048]{1,0:T(8,128)(2,1)}, u32[]{:S(2)}) copy-start(bf16[512,2048]{1,0:T(8,128)(2,1)} %a.3) | copy-start | bytes 6291460
  33.7 33.8 %copy-start.3 = (bf16[512,512]{1,0:T(8,128)(2,1)}, bf16[512,512]{1,0:T(8,128)(2,1)S(1)}, u32[]{:S(2)}) copy-start(bf16[512,512]{1,0:T(8,128)(2,1)S(1)} %get-tuple-element.433) | copy-start | bytes 1572868
  33.7 65.0 %collective-permute-start.17 = (bf16[64,2048]{1,0:T(8,128)(2,1)}, bf16[64,2048]{1,0:T(8,128)(2,1)}, u32[]{:S(2)}, u32[]{:S(2)}) collective-permute-start(bf16[64,2048]{1,0:T(8,128)(2,1)} %get-tuple-element.369), channel_id=1, source_target_pairs={{0,8},{1,9},{2,10},{3,11},{4,12},{5,13},{6,14},{7,15},{8,0},{9,1},... | collective-permute-start | bytes 786440 | tf_op jit(solution)/shard_map/ppermute | solution.py:203
  59.7 39.0 %collective-permute-start.18 = (bf16[64,2048]{1,0:T(8,128)(2,1)}, bf16[64,2048]{1,0:T(8,128)(2,1)}, u32[]{:S(2)}, u32[]{:S(2)}) collective-permute-start(bf16[64,2048]{1,0:T(8,128)(2,1)} %get-tuple-element.394), channel_id=1, source_target_pairs={{0,10},{1,11},{2,8},{3,9},{4,14},{5,15},{6,12},{7,13},{8,2},{9,3},... | collective-permute-start | bytes 786440 | tf_op jit(solution)/shard_map/ppermute | solution.py:203
  62.7 36.0 %collective-permute-start.19 = (bf16[64,2048]{1,0:T(8,128)(2,1)}, bf16[64,2048]{1,0:T(8,128)(2,1)}, u32[]{:S(2)}, u32[]{:S(2)}) collective-permute-start(bf16[64,2048]{1,0:T(8,128)(2,1)} %get-tuple-element.395), channel_id=1, source_target_pairs={{0,12},{1,13},{2,14},{3,15},{4,8},{5,9},{6,10},{7,11},{8,4},{9,5},... | collective-permute-start | bytes 786440 | tf_op jit(solution)/shard_map/ppermute | solution.py:203
  64.3 34.4 %collective-permute-start.20 = (bf16[64,2048]{1,0:T(8,128)(2,1)}, bf16[64,2048]{1,0:T(8,128)(2,1)}, u32[]{:S(2)}, u32[]{:S(2)}) collective-permute-start(bf16[64,2048]{1,0:T(8,128)(2,1)} %get-tuple-element.396), channel_id=1, source_target_pairs={{0,14},{1,15},{2,12},{3,13},{4,10},{5,11},{6,8},{7,9},{8,6},{9,7},... | collective-permute-start | bytes 786440 | tf_op jit(solution)/shard_map/ppermute | solution.py:203
  71.0 5.5 %collective-permute-start = (bf16[256,2048]{1,0:T(8,128)(2,1)S(1)}, bf16[256,2048]{1,0:T(8,128)(2,1)}, u32[]{:S(2)}, u32[]{:S(2)}) collective-permute-start(bf16[256,2048]{1,0:T(8,128)(2,1)S(1)} %get-tuple-element.216), channel_id=1, source_target_pairs={{0,1},{1,0},{2,3},{3,2},{4,5},{5,4},{6,7},{7,6},{8,9},{9,8},{10,11... | collective-permute-start | bytes 3145736 | tf_op jit(solution)/shard_map/cond/branch_1_fun/ppermute | solution.py:206
  71.0 27.7 %all-to-all-start.1 = ((bf16[4,64,2048]{2,1,0:T(8,128)(2,1)}), bf16[4,64,2048]{2,1,0:T(8,128)(2,1)}, u32[]{:S(2)}, u32[]{:S(2)}) async-start(bf16[4,64,2048]{2,1,0:T(8,128)(2,1)} %bitcast.5), calls=%async_computation.1 | async-start | bytes 2097152 | tf_op jit(solution)/shard_map/cond/branch_1_fun/all_to_all | solution.py:223
  80.1 2.9 %collective-permute-start.1 = (bf16[256,2048]{1,0:T(8,128)(2,1)S(1)}, bf16[256,2048]{1,0:T(8,128)(2,1)S(1)}, u32[]{:S(2)}, u32[]{:S(2)}) collective-permute-start(bf16[256,2048]{1,0:T(8,128)(2,1)S(1)} %get-tuple-element.218), channel_id=1, source_target_pairs={{0,1},{1,0},{2,3},{3,2},{4,5},{5,4},{6,7},{7,6},{8,9},{9,8},{10,11... | collective-permute-start | bytes 3145736 | tf_op jit(solution)/shard_map/cond/branch_1_fun/ppermute | solution.py:206
  98.7 49.5 %collective-permute-start.21 = (bf16[64,2048]{1,0:T(8,128)(2,1)}, bf16[64,2048]{1,0:T(8,128)(2,1)}, u32[]{:S(2)}, u32[]{:S(2)}) collective-permute-start(bf16[64,2048]{1,0:T(8,128)(2,1)} %get-tuple-element.398), channel_id=1, source_target_pairs={{0,8},{1,9},{2,10},{3,11},{4,12},{5,13},{6,14},{7,15},{8,0},{9,1},... | collective-permute-start | bytes 786440 | tf_op jit(solution)/shard_map/ppermute | solution.py:203
  102.1 46.2 %collective-permute-start.22 = (bf16[64,2048]{1,0:T(8,128)(2,1)}, bf16[64,2048]{1,0:T(8,128)(2,1)}, u32[]{:S(2)}, u32[]{:S(2)}) collective-permute-start(bf16[64,2048]{1,0:T(8,128)(2,1)} %get-tuple-element.399), channel_id=1, source_target_pairs={{0,10},{1,11},{2,8},{3,9},{4,14},{5,15},{6,12},{7,13},{8,2},{9,3},... | collective-permute-start | bytes 786440 | tf_op jit(solution)/shard_map/ppermute | solution.py:203
  102.6 45.6 %collective-permute-start.23 = (bf16[64,2048]{1,0:T(8,128)(2,1)}, bf16[64,2048]{1,0:T(8,128)(2,1)}, u32[]{:S(2)}, u32[]{:S(2)}) collective-permute-start(bf16[64,2048]{1,0:T(8,128)(2,1)} %get-tuple-element.400), channel_id=1, source_target_pairs={{0,12},{1,13},{2,14},{3,15},{4,8},{5,9},{6,10},{7,11},{8,4},{9,5},... | collective-permute-start | bytes 786440 | tf_op jit(solution)/shard_map/ppermute | solution.py:203
  105.9 42.3 %collective-permute-start.24 = (bf16[64,2048]{1,0:T(8,128)(2,1)}, bf16[64,2048]{1,0:T(8,128)(2,1)}, u32[]{:S(2)}, u32[]{:S(2)}) collective-permute-start(bf16[64,2048]{1,0:T(8,128)(2,1)} %get-tuple-element.401), channel_id=1, source_target_pairs={{0,14},{1,15},{2,12},{3,13},{4,10},{5,11},{6,8},{7,9},{8,6},{9,7},... | collective-permute-start | bytes 786440 | tf_op jit(solution)/shard_map/ppermute | solution.py:203
  109.3 4.3 %collective-permute-start.11 = (bf16[256,2048]{1,0:T(8,128)(2,1)S(1)}, bf16[256,2048]{1,0:T(8,128)(2,1)S(1)}, u32[]{:S(2)}, u32[]{:S(2)}) collective-permute-start(bf16[256,2048]{1,0:T(8,128)(2,1)S(1)} %get-tuple-element.233), channel_id=1, source_target_pairs={{0,1},{1,0},{2,3},{3,2},{4,5},{5,4},{6,7},{7,6},{8,9},{9,8},{10,11... | collective-permute-start | bytes 3145736 | tf_op jit(solution)/shard_map/cond/branch_1_fun/ppermute | solution.py:206
  109.3 38.9 %all-to-all-start.3 = ((bf16[4,64,2048]{2,1,0:T(8,128)(2,1)}), bf16[4,64,2048]{2,1,0:T(8,128)(2,1)}, u32[]{:S(2)}, u32[]{:S(2)}) async-start(bf16[4,64,2048]{2,1,0:T(8,128)(2,1)} %bitcast.7), calls=%async_computation.3 | async-start | bytes 2097152 | tf_op jit(solution)/shard_map/cond/branch_1_fun/all_to_all | solution.py:223
  117.5 6.6 %collective-permute-start.12 = (bf16[256,2048]{1,0:T(8,128)(2,1)}, bf16[256,2048]{1,0:T(8,128)(2,1)}, u32[]{:S(2)}, u32[]{:S(2)}) collective-permute-start(bf16[256,2048]{1,0:T(8,128)(2,1)} %get-tuple-element.235), channel_id=1, source_target_pairs={{0,1},{1,0},{2,3},{3,2},{4,5},{5,4},{6,7},{7,6},{8,9},{9,8},{10,11... | collective-permute-start | bytes 3145736 | tf_op jit(solution)/shard_map/cond/branch_1_fun/ppermute | solution.py:206
  148.2 3.3 %copy-start.7 = (f32[32,16,16]{0,2,1:T(8,128)}, f32[32,16,16]{0,2,1:T(8,128)S(1)}, u32[]{:S(2)}) copy-start(f32[32,16,16]{0,2,1:T(8,128)S(1)} %get-tuple-element.540) | copy-start | bytes 98308
  148.3 39.2 %collective-permute-start.25 = (bf16[64,2048]{1,0:T(8,128)(2,1)}, bf16[64,2048]{1,0:T(8,128)(2,1)}, u32[]{:S(2)}, u32[]{:S(2)}) collective-permute-start(bf16[64,2048]{1,0:T(8,128)(2,1)} %get-tuple-element.430), channel_id=1, source_target_pairs={{0,8},{1,9},{2,10},{3,11},{4,12},{5,13},{6,14},{7,15},{8,0},{9,1},... | collective-permute-start | bytes 786440 | tf_op jit(solution)/shard_map/ppermute | solution.py:203
  150.9 36.6 %collective-permute-start.26 = (bf16[64,2048]{1,0:T(8,128)(2,1)}, bf16[64,2048]{1,0:T(8,128)(2,1)}, u32[]{:S(2)}, u32[]{:S(2)}) collective-permute-start(bf16[64,2048]{1,0:T(8,128)(2,1)} %get-tuple-element.431), channel_id=1, source_target_pairs={{0,12},{1,13},{2,14},{3,15},{4,8},{5,9},{6,10},{7,11},{8,4},{9,5},... | collective-permute-start | bytes 786440 | tf_op jit(solution)/shard_map/ppermute | solution.py:203
  151.5 40.0 %copy-start.1 = (bf16[512,2048]{1,0:T(8,128)(2,1)S(1)}, bf16[512,2048]{1,0:T(8,128)(2,1)}, u32[]{:S(2)}) copy-start(bf16[512,2048]{1,0:T(8,128)(2,1)} %a.3) | copy-start | bytes 6291460
  151.6 35.9 %all-to-all-start.2 = ((bf16[4,64,2048]{2,1,0:T(8,128)(2,1)}), bf16[4,64,2048]{2,1,0:T(8,128)(2,1)}, u32[]{:S(2)}, u32[]{:S(2)}) async-start(bf16[4,64,2048]{2,1,0:T(8,128)(2,1)} %bitcast.17), calls=%async_computation.2 | async-start | bytes 2097152 | tf_op jit(solution)/shard_map/cond/branch_1_fun/all_to_all | solution.py:223
  161.1 6.3 %collective-permute-start.6 = (bf16[4,32,512]{2,1,0:T(8,128)(2,1)S(1)}, bf16[4,32,512]{2,1,0:T(8,128)(2,1)S(1)}, u32[]{:S(2)}, u32[]{:S(2)}) collective-permute-start(bf16[4,32,512]{2,1,0:T(8,128)(2,1)S(1)} %get-tuple-element.552), channel_id=1, source_target_pairs={{0,2},{1,3},{2,0},{3,1},{4,6},{5,7},{6,4},{7,5},{8,10},{9,11},{10,... | collective-permute-start | bytes 393224 | tf_op jit(solution)/shard_map/cond/branch_1_fun/ppermute | solution.py:206
  163.1 6.0 %collective-permute-start.7 = (bf16[4,32,512]{2,1,0:T(8,128)(2,1)S(1)}, bf16[4,32,512]{2,1,0:T(8,128)(2,1)S(1)}, u32[]{:S(2)}, u32[]{:S(2)}) collective-permute-start(bf16[4,32,512]{2,1,0:T(8,128)(2,1)S(1)} %get-tuple-element.553), channel_id=1, source_target_pairs={{0,3},{1,2},{2,1},{3,0},{4,7},{5,6},{6,5},{7,4},{8,11},{9,10},{10,... | collective-permute-start | bytes 393224 | tf_op jit(solution)/shard_map/cond/branch_1_fun/ppermute | solution.py:206
  163.2 5.9 %collective-permute-start.5 = (bf16[4,32,512]{2,1,0:T(8,128)(2,1)S(1)}, bf16[4,32,512]{2,1,0:T(8,128)(2,1)S(1)}, u32[]{:S(2)}, u32[]{:S(2)}) collective-permute-start(bf16[4,32,512]{2,1,0:T(8,128)(2,1)S(1)} %fusion.18), channel_id=1, source_target_pairs={{0,1},{1,0},{2,3},{3,2},{4,5},{5,4},{6,7},{7,6},{8,9},{9,8},{10,11... | collective-permute-start | bytes 393224 | tf_op jit(solution)/shard_map/cond/branch_1_fun/ppermute | solution.py:206
  169.1 8.6 %collective-permute-start.10 = (bf16[4,32,512]{2,1,0:T(8,128)(2,1)S(1)}, bf16[4,32,512]{2,1,0:T(8,128)(2,1)S(1)}, u32[]{:S(2)}, u32[]{:S(2)}) collective-permute-start(bf16[4,32,512]{2,1,0:T(8,128)(2,1)S(1)} %fusion.17), channel_id=1, source_target_pairs={{0,12},{1,13},{2,14},{3,15},{4,8},{5,9},{6,10},{7,11},{8,4},{9,5},... | collective-permute-start | bytes 393224 | tf_op jit(solution)/shard_map/cond/branch_1_fun/ppermute | solution.py:203
  174.7 12.7 %collective-permute-start.9 = (bf16[4,32,512]{2,1,0:T(8,128)(2,1)S(1)}, bf16[4,32,512]{2,1,0:T(8,128)(2,1)S(1)}, u32[]{:S(2)}, u32[]{:S(2)}) collective-permute-start(bf16[4,32,512]{2,1,0:T(8,128)(2,1)S(1)} %fusion.17), channel_id=1, source_target_pairs={{0,8},{1,9},{2,10},{3,11},{4,12},{5,13},{6,14},{7,15},{8,0},{9,1},... | collective-permute-start | bytes 393224 | tf_op jit(solution)/shard_map/cond/branch_1_fun/ppermute | solution.py:203
  176.5 8.6 %collective-permute-start.8 = (bf16[4,32,512]{2,1,0:T(8,128)(2,1)S(1)}, bf16[4,32,512]{2,1,0:T(8,128)(2,1)S(1)}, u32[]{:S(2)}, u32[]{:S(2)}) collective-permute-start(bf16[4,32,512]{2,1,0:T(8,128)(2,1)S(1)} %fusion.17), channel_id=1, source_target_pairs={{0,4},{1,5},{2,6},{3,7},{4,0},{5,1},{6,2},{7,3},{8,12},{9,13},{10,... | collective-permute-start | bytes 393224 | tf_op jit(solution)/shard_map/cond/branch_1_fun/ppermute | solution.py:203
  187.5 24.2 %collective-permute-start.27 = (bf16[64,2048]{1,0:T(8,128)(2,1)}, bf16[64,2048]{1,0:T(8,128)(2,1)S(1)}, u32[]{:S(2)}, u32[]{:S(2)}) collective-permute-start(bf16[64,2048]{1,0:T(8,128)(2,1)} %get-tuple-element.438), channel_id=1, source_target_pairs={{0,10},{1,11},{2,8},{3,9},{4,14},{5,15},{6,12},{7,13},{8,2},{9,3},... | collective-permute-start | bytes 786440 | tf_op jit(solution)/shard_map/ppermute | solution.py:203
  188.2 23.5 %collective-permute-start.28 = (bf16[64,2048]{1,0:T(8,128)(2,1)}, bf16[64,2048]{1,0:T(8,128)(2,1)S(1)}, u32[]{:S(2)}, u32[]{:S(2)}) collective-permute-start(bf16[64,2048]{1,0:T(8,128)(2,1)} %get-tuple-element.439), channel_id=1, source_target_pairs={{0,14},{1,15},{2,12},{3,13},{4,10},{5,11},{6,8},{7,9},{8,6},{9,7},... | collective-permute-start | bytes 786440 | tf_op jit(solution)/shard_map/ppermute | solution.py:203
  191.6 8.1 %collective-permute-start.2 = (bf16[4,32,512]{2,1,0:T(8,128)(2,1)S(1)}, bf16[4,32,512]{2,1,0:T(8,128)(2,1)S(1)}, u32[]{:S(2)}, u32[]{:S(2)}) collective-permute-start(bf16[4,32,512]{2,1,0:T(8,128)(2,1)S(1)} %get-tuple-element.266.refs_0_), channel_id=1, source_target_pairs={{0,1},{1,0},{2,3},{3,2},{4,5},{5,4},{6,7},{7,6},{8,9},{9,8},{10,11... | collective-permute-start | bytes 393224 | tf_op jit(solution)/shard_map/cond/branch_1_fun/ppermute | solution.py:206
  191.7 17.5 %collective-permute-start.3 = (bf16[4,32,512]{2,1,0:T(8,128)(2,1)S(1)}, bf16[4,32,512]{2,1,0:T(8,128)(2,1)S(1)}, u32[]{:S(2)}, u32[]{:S(2)}) collective-permute-start(bf16[4,32,512]{2,1,0:T(8,128)(2,1)S(1)} %get-tuple-element.266.refs_0_), channel_id=1, source_target_pairs={{0,2},{1,3},{2,0},{3,1},{4,6},{5,7},{6,4},{7,5},{8,10},{9,11},{10,... | collective-permute-start | bytes 393224 | tf_op jit(solution)/shard_map/cond/branch_1_fun/ppermute | solution.py:206
  192.8 18.2 %collective-permute-start.4 = (bf16[4,32,512]{2,1,0:T(8,128)(2,1)S(1)}, bf16[4,32,512]{2,1,0:T(8,128)(2,1)S(1)}, u32[]{:S(2)}, u32[]{:S(2)}) collective-permute-start(bf16[4,32,512]{2,1,0:T(8,128)(2,1)S(1)} %get-tuple-element.266.refs_0_), channel_id=1, source_target_pairs={{0,3},{1,2},{2,1},{3,0},{4,7},{5,6},{6,5},{7,4},{8,11},{9,10},{10,... | collective-permute-start | bytes 393224 | tf_op jit(solution)/shard_map/cond/branch_1_fun/ppermute | solution.py:206
  193.6 2.5 %copy-start.4 = (bf16[512,512]{1,0:T(8,128)(2,1)S(1)}, bf16[512,512]{1,0:T(8,128)(2,1)}, u32[]{:S(2)}) copy-start(bf16[512,512]{1,0:T(8,128)(2,1)} %get-tuple-element.267.matrix) | copy-start | bytes 1572868 | tf_op jit(solution)/shard_map/cond
  211.7 1.3 copy-start.5
  211.7 1.6 copy-start.6
  213.4 1.3 copy-start.2

commit v6 on v5

--- a/solution.py
+++ b/solution.py
@@ -70,7 +70,7 @@
             ],
             out_specs=block,
         ),
-        out_shape=jax.ShapeDtypeStruct(total.shape, BF16),
+        out_shape=pltpu.HBM(total.shape, BF16),
         input_output_aliases={3: 0},
         compiler_params=LIMIT,
     )(place, a, slab, total)
@@ -152,7 +152,7 @@
             at += 1
 
 
-def by_columns(kernel, ins, outs, width, scalars=(), whole=(), scratch=(), dtype=BF16):
+def by_columns(kernel, ins, outs, width, scalars=(), whole=(), scratch=(), dtype=BF16, result=False):
     columns = min(COLUMNS, width)
     block = lambda rows: pl.BlockSpec((rows, columns), lambda i: (0, i))
     full = lambda shape: pl.BlockSpec(shape, lambda i: (0, 0))
@@ -164,7 +164,10 @@
         + [block(x.shape[0]) for x in ins],
         out_specs=[block(n) if isinstance(n, int) else full(n) for n in outs],
         out_shape=[
-            jax.ShapeDtypeStruct((n, width) if isinstance(n, int) else n, dtype) for n in outs
+            (pltpu.HBM if result else jax.ShapeDtypeStruct)(
+                (n, width) if isinstance(n, int) else n, dtype
+            )
+            for n in outs
         ],
         scratch_shapes=list(scratch),
         compiler_params=LIMIT,
@@ -329,7 +332,7 @@
     backs = [side] + [got[k] for k in cross_ks]
 
     gateds = dict(zip(cross_ks, gated[1:]))
-    first, last = cross_ks[::2], cross_ks[1::2]
+    first, last = cross_ks[::2][::-1], cross_ks[1::2][::-1]
     arrived = send_cross({k: gateds[k] for k in first})
 
     def add(kept, received):
@@ -383,10 +386,17 @@
             [got] + [near(got, i) for i in (1, 2, 3)],
             1.0 / math.sqrt(count * width),
         )
-        grad_signal = by_columns(whole_kernel, backs, [block], width, (), [home_factor])[0]
+        grad_signal = by_columns(
+            whole_kernel, backs, [block], width, (), [home_factor], result=True
+        )[0]
         if dynamic:
             grad_gate = by_columns(
-                place_kernel, [cotangent] + slabs, [block], width, [jnp.stack(starts)]
+                place_kernel,
+                [cotangent] + slabs,
+                [block],
+                width,
+                [jnp.stack(starts)],
+                result=True,
             )[0]
         else:
             grad_gate = place(jnp.zeros_like(cotangent), starts, slabs)

time: 216 us -> 215 us (level)
  Pallas kernels: 39.4 us -> 43.2 us
  waiting for transfers between devices: 64.5 us -> 61.1 us
  other arithmetic: 9.71 us -> 6.7 us
    unnamed x18 -> x16, local copies, waits for them, and re-layouts: 2.92 us -> 0.23 us
    pallas_call x11, Pallas kernels: 38.7 us -> 41 us  [by_columns(): pl.pallas_call(kernel, grid=(width // columns,), in_specs=[pl.BlockSpec(m...]
    ppermute x10, waiting for transfers between devices: 19.3 us -> 17 us  [near(): return lax.ppermute(x, 'seq', [(s, s ^ i) for s in range(count)])]
  transfers between devices with their start and end apart: 32 -> 32, of which waited for: 10 -> 9; matrix products, arithmetic and copies ran while one was open for 10% -> 9% of each run, Pallas kernels for 18% -> 20%
where the time goes in v6:
time: 215 us; the launch traced here: 213 us
  waiting for transfers between devices  61.1 us (28%)
  starting transfers between devices  59.4 us (28%)
  Pallas kernels  43.2 us (20%)
  blocking collectives  24.5 us (11%)
  matrix products  9.67 us (4%)
  local copies, waits for them, and re-layouts  6.73 us (3%)
  other arithmetic  6.7 us (3%)
    ppermute x19, starting transfers between devices, chip(): return lax.ppermute(x, 'seq', [(s, s ^ 2 * k) for s in range(count)])  41.2 us
    pallas_call x11, Pallas kernels, by_columns(): pl.pallas_call(kernel, grid=(width // columns,), in_specs=[pl.BlockSpec(m...  41 us
    all_to_all x3, waiting for transfers between devices, send_side(): lax.all_to_all(x, 'seq', split_axis=0, concat_axis=0, tiled=True, axis_in...  33.2 us
    all_to_all x1, blocking collectives, send_side(): lax.all_to_all(x, 'seq', split_axis=0, concat_axis=0, tiled=True, axis_in...  24.5 us
    ppermute x10, waiting for transfers between devices, near(): return lax.ppermute(x, 'seq', [(s, s ^ i) for s in range(count)])  17 us
    all_to_all x3, starting transfers between devices, send_side(): lax.all_to_all(x, 'seq', split_axis=0, concat_axis=0, tiled=True, axis_in...  12.9 us
    ppermute x19, waiting for transfers between devices, chip(): return lax.ppermute(x, 'seq', [(s, s ^ 2 * k) for s in range(count)])  10.8 us
    ppermute x10, starting transfers between devices, near(): return lax.ppermute(x, 'seq', [(s, s ^ i) for s in range(count)])  5.33 us
  transfers between devices with their start and end apart: 32, of which 9 were waited for; matrix products, arithmetic and copies ran while one was open for 9% of the time, Pallas kernels for 20%

profile of v6, /device:TPU:0, one launch (start us, length us, event | category | flops | bytes accessed | tf_op | source)
XLA Modules:
  0.0 213.2 jit_solution(12152570044444279827)
XLA Ops:
  0.7 2.7 %dynamic-slice_multiply_fusion.1 = (bf16[64,2048]{1,0:T(8,128)(2,1)}, bf16[64,2048]{1,0:T(8,128)(2,1)}, bf16[64,2048]{1,0:T(8,128)(2,1)}, bf16[64,2048]{1,0:T(8,128)(2,1)}) fusion(bf16[512,2048]{1,0:T(8,128)(2,1)} %param.19, s32[]{:T(128)S(6)} %select_n.112, bf16[512,2048]{1,0:T(8,128)(2,1)} %a.3, s32[]{:T(128)S(6)} %select_n.111, s32[]{:T(128)S(6)} %select_n.110, ...), kind=kLoop, calls=%fused_computation.56 | loop fusion | flops 2097152 | bytes 3145744 | tf_op jit(solution)/shard_map/mul | solution.py:251
  3.4 4.0 %collective-permute-start.13 = (bf16[64,2048]{1,0:T(8,128)(2,1)}, bf16[64,2048]{1,0:T(8,128)(2,1)}, u32[]{:S(2)}, u32[]{:S(2)}) collective-permute-start(bf16[64,2048]{1,0:T(8,128)(2,1)} %get-tuple-element.377), channel_id=1, source_target_pairs={{0,8},{1,9},{2,10},{3,11},{4,12},{5,13},{6,14},{7,15},{8,0},{9,1},... | collective-permute-start | bytes 786440 | tf_op jit(solution)/shard_map/ppermute | solution.py:206
  8.7 3.6 %collective-permute-start.15 = (bf16[64,2048]{1,0:T(8,128)(2,1)}, bf16[64,2048]{1,0:T(8,128)(2,1)}, u32[]{:S(2)}, u32[]{:S(2)}) collective-permute-start(bf16[64,2048]{1,0:T(8,128)(2,1)} %get-tuple-element.379), channel_id=1, source_target_pairs={{0,12},{1,13},{2,14},{3,15},{4,8},{5,9},{6,10},{7,11},{8,4},{9,5},... | collective-permute-start | bytes 786440 | tf_op jit(solution)/shard_map/ppermute | solution.py:206
  13.9 18.6 %conditional.6 = (bf16[256,2048]{1,0:T(8,128)(2,1)}, bf16[64,2048]{1,0:T(8,128)(2,1)}, bf16[64,2048]{1,0:T(8,128)(2,1)}, bf16[64,2048]{1,0:T(8,128)(2,1)}, bf16[...) conditional(s32[]{:T(128)} %bitcast.23, () %tuple.70, ...), branch_computations={%region_0.1_spmd, %region_1.2_spmd} | conditional | flops 1622943616 | bytes 8788276 | solution.py:203
  14.1 1.6 convolution_convert_fusion.2.matrix
  15.8 4.2 %convolution_convert_fusion.rows = bf16[512,2048]{1,0:T(8,128)(2,1)} fusion(bf16[512,2048]{1,0:T(8,128)(2,1)} %get-tuple-element.197, s32[512]{0:T(512)S(1)} %get-tuple-element.196), kind=kOutput, calls=%fused_computation | convolution fusion | flops 1075052544 | bytes 4196352 | tf_op jit(solution)/shard_map/cond/branch_1_fun/dot_general | solution.py:269
  20.0 4.4 %branch_1_fun.12 = (bf16[256,2048]{1,0:T(8,128)(2,1)}, bf16[64,2048]{1,0:T(8,128)(2,1)}, bf16[64,2048]{1,0:T(8,128)(2,1)}, bf16[64,2048]{1,0:T(8,128)(2,1)}, bf16[64,2048]{1,0:T(8,128)(2,1)}) custom-call(bf16[512,512]{1,0:T(8,128)(2,1)S(1)} %convolution_convert_fusion.2.matrix, bf16[512,2048]{1,0:T(8,128)(2,1)} %convolution_convert_fusion.rows), custom_call_target="tpu_custom_call" | custom-call | tf_op jit(solution)/shard_map/cond/branch_1_fun/pallas_call | solution.py:159
  25.2 1.4 broadcast_in_dim.2
  26.9 2.0 fusion
  28.9 1.9 copy.54
  33.4 1.6 dynamic-slice_multiply_fusion
  35.1 24.5 %conditional.7 = (bf16[256,2048]{1,0:T(8,128)(2,1)S(1)}) conditional(s32[]{:T(128)} %bitcast.23, () %tuple.73, bf16[256,2048]{1,0:T(8,128)(2,1)S(1)} %dynamic-slice_multiply_fusion), branch_computations={%region_2.3_spmd, %region_3.4_spmd} | conditional | bytes 2097160 | solution.py:203
  35.1 24.5 %all_to_all.36 = bf16[4,64,2048]{2,1,0:T(8,128)(2,1)S(1)} all-to-all(bf16[4,64,2048]{2,1,0:T(8,128)(2,1)S(1)} %bitcast.68), channel_id=1, replica_groups={{0,2,4,6},{1,3,5,7},{8,10,12,14},{9,11,13,15},{16,18,20,22},{17,19,21,2..., dimensions={0} | all-to-all | bytes 2097152 | tf_op jit(solution)/shard_map/cond/branch_1_fun/all_to_all | solution.py:226
  59.6 3.1 %collective-permute-start.18 = (bf16[64,2048]{1,0:T(8,128)(2,1)}, bf16[64,2048]{1,0:T(8,128)(2,1)S(1)}, u32[]{:S(2)}, u32[]{:S(2)}) collective-permute-start(bf16[64,2048]{1,0:T(8,128)(2,1)} %get-tuple-element.394), channel_id=1, source_target_pairs={{0,10},{1,11},{2,8},{3,9},{4,14},{5,15},{6,12},{7,13},{8,2},{9,3},... | collective-permute-start | bytes 786440 | tf_op jit(solution)/shard_map/ppermute | solution.py:206
  63.7 3.8 %collective-permute-start.20 = (bf16[64,2048]{1,0:T(8,128)(2,1)}, bf16[64,2048]{1,0:T(8,128)(2,1)}, u32[]{:S(2)}, u32[]{:S(2)}) collective-permute-start(bf16[64,2048]{1,0:T(8,128)(2,1)} %get-tuple-element.396), channel_id=1, source_target_pairs={{0,14},{1,15},{2,12},{3,13},{4,10},{5,11},{6,8},{7,9},{8,6},{9,7},... | collective-permute-start | bytes 786440 | tf_op jit(solution)/shard_map/ppermute | solution.py:206
  67.5 30.9 %conditional.8 = (bf16[256,2048]{1,0:T(8,128)(2,1)}, bf16[256,2048]{1,0:T(8,128)(2,1)}, bf16[64,2048]{1,0:T(8,128)(2,1)}, bf16[64,2048]{1,0:T(8,128)(2,1)}, bf16...) conditional(s32[]{:T(128)} %bitcast.23, () %tuple.68, ...), branch_computations={%region_4.5_spmd, %region_5.6_spmd} | conditional | bytes 12583088 | solution.py:203
  67.5 3.5 %branch_1_fun.13 = (bf16[256,2048]{1,0:T(8,128)(2,1)}, bf16[256,2048]{1,0:T(8,128)(2,1)S(1)}) custom-call(s32[1]{0:T(128)} %get-tuple-element.208.core, bf16[256,2048]{1,0:T(8,128)(2,1)S(1)} %get-tuple-element.210.refs_0_, bf16[64,2048]{1,0:T(8,128)(2,1)} %get-tuple-element.211.refs_1_, bf16[64,2048]{1,0:T(8,128)(2,1)} %get-tuple-element.212.refs_2_, ...), custom_call_target="tpu_custom_call" | custom-call | tf_op jit(solution)/shard_map/cond/branch_1_fun/pallas_call | solution.py:159
  71.0 4.2 %all-to-all-start.1 = ((bf16[4,64,2048]{2,1,0:T(8,128)(2,1)}), bf16[4,64,2048]{2,1,0:T(8,128)(2,1)}, u32[]{:S(2)}, u32[]{:S(2)}) async-start(bf16[4,64,2048]{2,1,0:T(8,128)(2,1)} %bitcast.5), calls=%async_computation.1 | async-start | bytes 2097152 | tf_op jit(solution)/shard_map/cond/branch_1_fun/all_to_all | solution.py:226
  76.5 3.5 %branch_1_fun.14 = (bf16[256,2048]{1,0:T(8,128)(2,1)S(1)}, bf16[256,2048]{1,0:T(8,128)(2,1)S(1)}) custom-call(bf16[512,512]{1,0:T(8,128)(2,1)S(1)} %copy.19.matrix, bf16[256,2048]{1,0:T(8,128)(2,1)} %get-tuple-element.609.own, bf16[256,2048]{1,0:T(8,128)(2,1)} %collective-permute-done.other), custom_call_target="tpu_custom_call" | custom-call | tf_op jit(solution)/shard_map/cond/branch_1_fun/pallas_call | solution.py:159
  80.6 2.3 %collective-permute-done.1.other = bf16[256,2048]{1,0:T(8,128)(2,1)S(1)} collective-permute-done((bf16[256,2048]{1,0:T(8,128)(2,1)S(1)}, bf16[256,2048]{1,0:T(8,128)(2,1)S(1)}, u32[]{:S(2)}, u32[]{:S(2)}) %collective-permute-start.1) | collective-permute-done | bytes 1048608 | tf_op jit(solution)/shard_map/cond/branch_1_fun/ppermute | solution.py:209
  82.9 2.0 branch_1_fun.15
  84.9 13.5 %all-to-all-done.1 = bf16[4,64,2048]{2,1,0:T(8,128)(2,1)} async-done(((bf16[4,64,2048]{2,1,0:T(8,128)(2,1)}), bf16[4,64,2048]{2,1,0:T(8,128)(2,1)}, u32[]{:S(2)}, u32[]{:S(2)}) %all-to-all-start.1) | async-done | bytes 1048608 | tf_op jit(solution)/shard_map/cond/branch_1_fun/all_to_all | solution.py:226
  98.4 3.6 %collective-permute-start.21 = (bf16[64,2048]{1,0:T(8,128)(2,1)}, bf16[64,2048]{1,0:T(8,128)(2,1)}, u32[]{:S(2)}, u32[]{:S(2)}) collective-permute-start(bf16[64,2048]{1,0:T(8,128)(2,1)} %get-tuple-element.398), channel_id=1, source_target_pairs={{0,8},{1,9},{2,10},{3,11},{4,12},{5,13},{6,14},{7,15},{8,0},{9,1},... | collective-permute-start | bytes 786440 | tf_op jit(solution)/shard_map/ppermute | solution.py:206
  102.4 3.5 %collective-permute-start.23 = (bf16[64,2048]{1,0:T(8,128)(2,1)}, bf16[64,2048]{1,0:T(8,128)(2,1)}, u32[]{:S(2)}, u32[]{:S(2)}) collective-permute-start(bf16[64,2048]{1,0:T(8,128)(2,1)} %get-tuple-element.400), channel_id=1, source_target_pairs={{0,12},{1,13},{2,14},{3,15},{4,8},{5,9},{6,10},{7,11},{8,4},{9,5},... | collective-permute-start | bytes 786440 | tf_op jit(solution)/shard_map/ppermute | solution.py:206
  106.8 41.4 %conditional.9 = (bf16[256,2048]{1,0:T(8,128)(2,1)}, bf16[256,2048]{1,0:T(8,128)(2,1)}, bf16[64,2048]{1,0:T(8,128)(2,1)}, bf16[64,2048]{1,0:T(8,128)(2,1)}, bf16...) conditional(s32[]{:T(128)} %bitcast.23, () %tuple.77, ...), branch_computations={%region_6.7_spmd, %region_7.8_spmd} | conditional | flops 1843200 | bytes 14615264 | solution.py:203
  107.6 2.5 %branch_1_fun.16 = (bf16[256,2048]{1,0:T(8,128)(2,1)S(1)}, bf16[256,2048]{1,0:T(8,128)(2,1)S(1)}) custom-call(s32[1]{0:T(128)} %get-tuple-element.225.core, bf16[256,2048]{1,0:T(8,128)(2,1)} %get-tuple-element.227.refs_0_, bf16[64,2048]{1,0:T(8,128)(2,1)} %copy-done.5, bf16[64,2048]{1,0:T(8,128)(2,1)} %copy-done.6, ...), custom_call_target="tpu_custom_call" | custom-call | tf_op jit(solution)/shard_map/cond/branch_1_fun/pallas_call | solution.py:159
  110.1 4.3 %all-to-all-start.3 = ((bf16[4,64,2048]{2,1,0:T(8,128)(2,1)}), bf16[4,64,2048]{2,1,0:T(8,128)(2,1)}, u32[]{:S(2)}, u32[]{:S(2)}) async-start(bf16[4,64,2048]{2,1,0:T(8,128)(2,1)} %bitcast.69), calls=%async_computation.3 | async-start | bytes 2097152 | tf_op jit(solution)/shard_map/cond/branch_1_fun/all_to_all | solution.py:226
  114.4 3.9 %branch_1_fun.17 = (bf16[256,2048]{1,0:T(8,128)(2,1)S(1)}, bf16[256,2048]{1,0:T(8,128)(2,1)}) custom-call(bf16[512,512]{1,0:T(8,128)(2,1)} %get-tuple-element.226.matrix, bf16[256,2048]{1,0:T(8,128)(2,1)S(1)} %get-tuple-element.232.own.refs_2_, bf16[256,2048]{1,0:T(8,128)(2,1)S(1)} %collective-permute-done.11.other.refs_3_), custom_call_target="tpu_custom_call" | custom-call | tf_op jit(solution)/shard_map/cond/branch_1_fun/pallas_call | solution.py:159
  118.9 4.8 %branch_1_fun.19 = f32[512,16]{1,0:T(8,128)S(1)} custom-call(bf16[512,512]{1,0:T(8,128)(2,1)S(1)} %convert_element_type.65.same, bf16[512,16]{1,0:T(8,128)(2,1)} %get-tuple-element.242.spread_out, bf16[256,2048]{1,0:T(8,128)(2,1)} %get-tuple-element.243.refs_0_, bf16[256,2048]{1,0:T(8,128)(2,1)} %get-tuple-element.244.refs_1_, ...), custom_call_target="tpu_custom_call" | custom-call | tf_op jit(solution)/shard_map/cond/branch_1_fun/pallas_call | solution.py:159
  124.9 3.6 %branch_1_fun.18 = (bf16[256,2048]{1,0:T(8,128)(2,1)}, bf16[64,2048]{1,0:T(8,128)(2,1)}, bf16[64,2048]{1,0:T(8,128)(2,1)}, bf16[64,2048]{1,0:T(8,128)(2,1)}, bf16[64,2048]{1,0:T(8,128)(2,1)}) custom-call(s32[1]{0:T(128)} %get-tuple-element.225.core, bf16[256,2048]{1,0:T(8,128)(2,1)S(1)} %get-tuple-element.234.own, ...), custom_call_target="tpu_custom_call" | custom-call | tf_op jit(solution)/shard_map/cond/branch_1_fun/pallas_call | solution.py:159
  128.5 19.7 %all-to-all-done.3 = bf16[4,64,2048]{2,1,0:T(8,128)(2,1)} async-done(((bf16[4,64,2048]{2,1,0:T(8,128)(2,1)}), bf16[4,64,2048]{2,1,0:T(8,128)(2,1)}, u32[]{:S(2)}, u32[]{:S(2)}) %all-to-all-start.3) | async-done | bytes 1048608 | tf_op jit(solution)/shard_map/cond/branch_1_fun/all_to_all | solution.py:226
  148.3 2.6 %collective-permute-start.25 = (bf16[64,2048]{1,0:T(8,128)(2,1)}, bf16[64,2048]{1,0:T(8,128)(2,1)}, u32[]{:S(2)}, u32[]{:S(2)}) collective-permute-start(bf16[64,2048]{1,0:T(8,128)(2,1)} %get-tuple-element.430), channel_id=1, source_target_pairs={{0,8},{1,9},{2,10},{3,11},{4,12},{5,13},{6,14},{7,15},{8,0},{9,1},... | collective-permute-start | bytes 786440 | tf_op jit(solution)/shard_map/ppermute | solution.py:206
  151.3 36.0 %conditional.10 = (bf16[4,32,512]{2,1,0:T(8,128)(2,1)S(1)}, bf16[256,2048]{1,0:T(8,128)(2,1)}) conditional(s32[]{:T(128)} %bitcast.23, () %tuple.80, (s32[8]{0:T(128)}, bf16[512,512]{1,0:T(8,128)(2,1)}, bf16[512,2048]{1,0:T(8,128)(2,1)}, bf16[256,2048]{1,0:T(8,128)(2,1)}, bf16[64,2048]{1,0:T(8,128)(2,1)}, /*index=5*/bf16[64,2048]{1,0:T(8,128)(2,1)}, ...), branch_computations={%region_8.9_spmd, %region_9.10_spmd} | conditional | flops 1441803 | bytes 10879548 | solution.py:203
  151.3 4.4 %all-to-all-start.2 = ((bf16[4,64,2048]{2,1,0:T(8,128)(2,1)}), bf16[4,64,2048]{2,1,0:T(8,128)(2,1)}, u32[]{:S(2)}, u32[]{:S(2)}) async-start(bf16[4,64,2048]{2,1,0:T(8,128)(2,1)} %bitcast.17), calls=%async_computation.2 | async-start | bytes 2097152 | tf_op jit(solution)/shard_map/cond/branch_1_fun/all_to_all | solution.py:226
  155.7 4.4 %branch_1_fun.20 = f32[512,512]{1,0:T(8,128)S(1)} custom-call(s32[4]{0:T(128)S(1)} %slice_multiply_fusion.starts, bf16[512,512]{1,0:T(8,128)(2,1)} %get-tuple-element.247.order, bf16[512,2048]{1,0:T(8,128)(2,1)} %get-tuple-element.248.right, bf16[256,2048]{1,0:T(8,128)(2,1)} %get-tuple-element.249.side, bf16[64,2048]{1,0:T(8,128)(2,1)} %get-tuple-element.250.refs_0_, ...), custom_call_target="tpu_custom_call" | custom-call | tf_op jit(solution)/shard_map/cond/branch_1_fun/pallas_call | solution.py:159
  160.2 2.0 collective-permute-start.6
  162.6 5.5 %collective-permute-done.6 = bf16[4,32,512]{2,1,0:T(8,128)(2,1)S(1)} collective-permute-done((bf16[4,32,512]{2,1,0:T(8,128)(2,1)S(1)}, bf16[4,32,512]{2,1,0:T(8,128)(2,1)S(1)}, u32[]{:S(2)}, u32[]{:S(2)}) %collective-permute-start.6) | collective-permute-done | bytes 131104 | tf_op jit(solution)/shard_map/cond/branch_1_fun/ppermute | solution.py:209
  168.3 6.4 %collective-permute-start.10 = (bf16[4,32,512]{2,1,0:T(8,128)(2,1)S(1)}, bf16[4,32,512]{2,1,0:T(8,128)(2,1)S(1)}, u32[]{:S(2)}, u32[]{:S(2)}) collective-permute-start(bf16[4,32,512]{2,1,0:T(8,128)(2,1)S(1)} %fusion.17), channel_id=1, source_target_pairs={{0,12},{1,13},{2,14},{3,15},{4,8},{5,9},{6,10},{7,11},{8,4},{9,5},... | collective-permute-start | bytes 393224 | tf_op jit(solution)/shard_map/cond/branch_1_fun/ppermute | solution.py:206
  174.7 1.6 collective-permute-start.9
  176.3 1.4 collective-permute-done.10
  177.8 7.8 %collective-permute-done.8 = bf16[4,32,512]{2,1,0:T(8,128)(2,1)S(1)} collective-permute-done((bf16[4,32,512]{2,1,0:T(8,128)(2,1)S(1)}, bf16[4,32,512]{2,1,0:T(8,128)(2,1)S(1)}, u32[]{:S(2)}, u32[]{:S(2)}) %collective-permute-start.8) | collective-permute-done | bytes 131104 | tf_op jit(solution)/shard_map/cond/branch_1_fun/ppermute | solution.py:206
  185.6 1.6 collective-permute-done.9
  187.3 1.5 collective-permute-start.27
  188.8 2.4 %collective-permute-start.28 = (bf16[64,2048]{1,0:T(8,128)(2,1)}, bf16[64,2048]{1,0:T(8,128)(2,1)S(1)}, u32[]{:S(2)}, u32[]{:S(2)}) collective-permute-start(bf16[64,2048]{1,0:T(8,128)(2,1)} %get-tuple-element.439), channel_id=1, source_target_pairs={{0,14},{1,15},{2,12},{3,13},{4,10},{5,11},{6,8},{7,9},{8,6},{9,7},... | collective-permute-start | bytes 786440 | tf_op jit(solution)/shard_map/ppermute | solution.py:206
  191.3 20.1 %conditional.11 = (f32[512,512]{1,0:T(8,128)S(1)}, bf16[512,2048]{1,0:T(8,128)(2,1)}, bf16[512,2048]{1,0:T(8,128)(2,1)}) conditional(s32[]{:T(128)} %bitcast.23, () %tuple.67, (s32[]{:T(128)}, s32[16]{0:T(128)S(1)}, s32[16]{0:T(128)S(1)}, s32[16]{0:T(128)S(1)}, pred[16]{0:T(512)(128)(4,1)S(1)}, /*index=5*/s32[16]{0:T(128)S(1)}, s32[16]{0:T(128)S(1)}, ...), branch_computations={%region_10.11_spmd, %region_11.12_spmd} | conditional | flops 550 | bytes 5242912 | solution.py:203
  193.3 3.8 %branch_1_fun.23 = bf16[512,2048]{1,0:T(8,128)(2,1)} custom-call(s32[3]{0:T(128)S(1)} %pad_add_fusion.starts, bf16[512,2048]{1,0:T(8,128)(2,1)S(1)} %get-tuple-element.276.a, bf16[256,2048]{1,0:T(8,128)(2,1)} %get-tuple-element.277.refs_0_, bf16[64,2048]{1,0:T(8,128)(2,1)} %get-tuple-element.278.refs_1_, bf16[64,2048]{1,0:T(8,128)(2,1)} %get-tuple-element.279.refs_2_), custom_call_target="tpu_custom_call" | custom-call | tf_op jit(solution)/shard_map/cond/branch_1_fun/pallas_call | solution.py:159
  197.1 4.5 %branch_1_fun.22 = bf16[512,2048]{1,0:T(8,128)(2,1)} custom-call(bf16[512,512]{1,0:T(8,128)(2,1)S(1)} %copy-done.3, bf16[256,2048]{1,0:T(8,128)(2,1)} %get-tuple-element.268.refs_0_, bf16[64,2048]{1,0:T(8,128)(2,1)} %get-tuple-element.269.refs_1_, bf16[64,2048]{1,0:T(8,128)(2,1)} %get-tuple-element.270.refs_2_, bf16[64,2048]{1,0:T(8,128)(2,1)} %get-tuple-element.271.refs_3_, ...), custom_call_target="tpu_custom_call" | custom-call | tf_op jit(solution)/shard_map/cond/branch_1_fun/pallas_call | solution.py:159
  201.7 9.0 %collective-permute-done.4.refs_3_ = bf16[4,32,512]{2,1,0:T(8,128)(2,1)S(1)} collective-permute-done((bf16[4,32,512]{2,1,0:T(8,128)(2,1)S(1)}, bf16[4,32,512]{2,1,0:T(8,128)(2,1)S(1)}, u32[]{:S(2)}, u32[]{:S(2)}) %collective-permute-start.4) | collective-permute-done | bytes 131104 | tf_op jit(solution)/shard_map/cond/branch_1_fun/ppermute | solution.py:209
  (113 shorter events, 18.2 us)
Async XLA Ops:
  0.6 12.0 %copy-start.11 = (s32[512]{0:T(512)S(1)}, s32[512]{0:T(512)}, u32[]{:S(2)}) copy-start(s32[512]{0:T(512)} %param.23) | copy-start | bytes 6148
  0.6 13.2 %copy-start.8 = (bf16[32,16,16]{0,2,1:T(8,128)(2,1)S(1)}, bf16[32,16,16]{0,2,1:T(8,128)(2,1)}, u32[]{:S(2)}) copy-start(bf16[32,16,16]{0,2,1:T(8,128)(2,1)} %param.22) | copy-start | bytes 49156
  3.4 56.2 %collective-permute-start.13 = (bf16[64,2048]{1,0:T(8,128)(2,1)}, bf16[64,2048]{1,0:T(8,128)(2,1)}, u32[]{:S(2)}, u32[]{:S(2)}) collective-permute-start(bf16[64,2048]{1,0:T(8,128)(2,1)} %get-tuple-element.377), channel_id=1, source_target_pairs={{0,8},{1,9},{2,10},{3,11},{4,12},{5,13},{6,14},{7,15},{8,0},{9,1},... | collective-permute-start | bytes 786440 | tf_op jit(solution)/shard_map/ppermute | solution.py:206
  7.4 52.1 %collective-permute-start.14 = (bf16[64,2048]{1,0:T(8,128)(2,1)}, bf16[64,2048]{1,0:T(8,128)(2,1)}, u32[]{:S(2)}, u32[]{:S(2)}) collective-permute-start(bf16[64,2048]{1,0:T(8,128)(2,1)} %get-tuple-element.378), channel_id=1, source_target_pairs={{0,10},{1,11},{2,8},{3,9},{4,14},{5,15},{6,12},{7,13},{8,2},{9,3},... | collective-permute-start | bytes 786440 | tf_op jit(solution)/shard_map/ppermute | solution.py:206
  8.7 50.8 %collective-permute-start.15 = (bf16[64,2048]{1,0:T(8,128)(2,1)}, bf16[64,2048]{1,0:T(8,128)(2,1)}, u32[]{:S(2)}, u32[]{:S(2)}) collective-permute-start(bf16[64,2048]{1,0:T(8,128)(2,1)} %get-tuple-element.379), channel_id=1, source_target_pairs={{0,12},{1,13},{2,14},{3,15},{4,8},{5,9},{6,10},{7,11},{8,4},{9,5},... | collective-permute-start | bytes 786440 | tf_op jit(solution)/shard_map/ppermute | solution.py:206
  12.3 47.3 %collective-permute-start.16 = (bf16[64,2048]{1,0:T(8,128)(2,1)}, bf16[64,2048]{1,0:T(8,128)(2,1)}, u32[]{:S(2)}, u32[]{:S(2)}) collective-permute-start(bf16[64,2048]{1,0:T(8,128)(2,1)} %get-tuple-element.380), channel_id=1, source_target_pairs={{0,14},{1,15},{2,12},{3,13},{4,10},{5,11},{6,8},{7,9},{8,6},{9,7},... | collective-permute-start | bytes 786440 | tf_op jit(solution)/shard_map/ppermute | solution.py:206
  12.6 1.3 copy-start.9
  13.9 19.6 %copy-start = (bf16[512,2048]{1,0:T(8,128)(2,1)S(1)}, bf16[512,2048]{1,0:T(8,128)(2,1)}, u32[]{:S(2)}) copy-start(bf16[512,2048]{1,0:T(8,128)(2,1)} %a.3) | copy-start | bytes 6291460
  32.5 2.6 %copy-start.2 = (bf16[512,512]{1,0:T(8,128)(2,1)}, bf16[512,512]{1,0:T(8,128)(2,1)S(1)}, u32[]{:S(2)}) copy-start(bf16[512,512]{1,0:T(8,128)(2,1)S(1)} %get-tuple-element.433) | copy-start | bytes 1572868
  32.5 65.9 %collective-permute-start.17 = (bf16[64,2048]{1,0:T(8,128)(2,1)}, bf16[64,2048]{1,0:T(8,128)(2,1)S(1)}, u32[]{:S(2)}, u32[]{:S(2)}) collective-permute-start(bf16[64,2048]{1,0:T(8,128)(2,1)} %get-tuple-element.369), channel_id=1, source_target_pairs={{0,8},{1,9},{2,10},{3,11},{4,12},{5,13},{6,14},{7,15},{8,0},{9,1},... | collective-permute-start | bytes 786440 | tf_op jit(solution)/shard_map/ppermute | solution.py:206
  59.6 38.8 %collective-permute-start.18 = (bf16[64,2048]{1,0:T(8,128)(2,1)}, bf16[64,2048]{1,0:T(8,128)(2,1)S(1)}, u32[]{:S(2)}, u32[]{:S(2)}) collective-permute-start(bf16[64,2048]{1,0:T(8,128)(2,1)} %get-tuple-element.394), channel_id=1, source_target_pairs={{0,10},{1,11},{2,8},{3,9},{4,14},{5,15},{6,12},{7,13},{8,2},{9,3},... | collective-permute-start | bytes 786440 | tf_op jit(solution)/shard_map/ppermute | solution.py:206
  62.7 35.7 %collective-permute-start.19 = (bf16[64,2048]{1,0:T(8,128)(2,1)}, bf16[64,2048]{1,0:T(8,128)(2,1)}, u32[]{:S(2)}, u32[]{:S(2)}) collective-permute-start(bf16[64,2048]{1,0:T(8,128)(2,1)} %get-tuple-element.395), channel_id=1, source_target_pairs={{0,12},{1,13},{2,14},{3,15},{4,8},{5,9},{6,10},{7,11},{8,4},{9,5},... | collective-permute-start | bytes 786440 | tf_op jit(solution)/shard_map/ppermute | solution.py:206
  63.7 34.7 %collective-permute-start.20 = (bf16[64,2048]{1,0:T(8,128)(2,1)}, bf16[64,2048]{1,0:T(8,128)(2,1)}, u32[]{:S(2)}, u32[]{:S(2)}) collective-permute-start(bf16[64,2048]{1,0:T(8,128)(2,1)} %get-tuple-element.396), channel_id=1, source_target_pairs={{0,14},{1,15},{2,12},{3,13},{4,10},{5,11},{6,8},{7,9},{8,6},{9,7},... | collective-permute-start | bytes 786440 | tf_op jit(solution)/shard_map/ppermute | solution.py:206
  71.0 5.5 %collective-permute-start = (bf16[256,2048]{1,0:T(8,128)(2,1)S(1)}, bf16[256,2048]{1,0:T(8,128)(2,1)}, u32[]{:S(2)}, u32[]{:S(2)}) collective-permute-start(bf16[256,2048]{1,0:T(8,128)(2,1)S(1)} %get-tuple-element.216), channel_id=1, source_target_pairs={{0,1},{1,0},{2,3},{3,2},{4,5},{5,4},{6,7},{7,6},{8,9},{9,8},{10,11... | collective-permute-start | bytes 3145736 | tf_op jit(solution)/shard_map/cond/branch_1_fun/ppermute | solution.py:209
  71.0 27.4 %all-to-all-start.1 = ((bf16[4,64,2048]{2,1,0:T(8,128)(2,1)}), bf16[4,64,2048]{2,1,0:T(8,128)(2,1)}, u32[]{:S(2)}, u32[]{:S(2)}) async-start(bf16[4,64,2048]{2,1,0:T(8,128)(2,1)} %bitcast.5), calls=%async_computation.1 | async-start | bytes 2097152 | tf_op jit(solution)/shard_map/cond/branch_1_fun/all_to_all | solution.py:226
  80.1 2.9 %collective-permute-start.1 = (bf16[256,2048]{1,0:T(8,128)(2,1)S(1)}, bf16[256,2048]{1,0:T(8,128)(2,1)S(1)}, u32[]{:S(2)}, u32[]{:S(2)}) collective-permute-start(bf16[256,2048]{1,0:T(8,128)(2,1)S(1)} %get-tuple-element.218), channel_id=1, source_target_pairs={{0,1},{1,0},{2,3},{3,2},{4,5},{5,4},{6,7},{7,6},{8,9},{9,8},{10,11... | collective-permute-start | bytes 3145736 | tf_op jit(solution)/shard_map/cond/branch_1_fun/ppermute | solution.py:209
  98.4 49.8 %collective-permute-start.21 = (bf16[64,2048]{1,0:T(8,128)(2,1)}, bf16[64,2048]{1,0:T(8,128)(2,1)}, u32[]{:S(2)}, u32[]{:S(2)}) collective-permute-start(bf16[64,2048]{1,0:T(8,128)(2,1)} %get-tuple-element.398), channel_id=1, source_target_pairs={{0,8},{1,9},{2,10},{3,11},{4,12},{5,13},{6,14},{7,15},{8,0},{9,1},... | collective-permute-start | bytes 786440 | tf_op jit(solution)/shard_map/ppermute | solution.py:206
  102.0 46.2 %collective-permute-start.22 = (bf16[64,2048]{1,0:T(8,128)(2,1)}, bf16[64,2048]{1,0:T(8,128)(2,1)}, u32[]{:S(2)}, u32[]{:S(2)}) collective-permute-start(bf16[64,2048]{1,0:T(8,128)(2,1)} %get-tuple-element.399), channel_id=1, source_target_pairs={{0,10},{1,11},{2,8},{3,9},{4,14},{5,15},{6,12},{7,13},{8,2},{9,3},... | collective-permute-start | bytes 786440 | tf_op jit(solution)/shard_map/ppermute | solution.py:206
  102.4 45.8 %collective-permute-start.23 = (bf16[64,2048]{1,0:T(8,128)(2,1)}, bf16[64,2048]{1,0:T(8,128)(2,1)}, u32[]{:S(2)}, u32[]{:S(2)}) collective-permute-start(bf16[64,2048]{1,0:T(8,128)(2,1)} %get-tuple-element.400), channel_id=1, source_target_pairs={{0,12},{1,13},{2,14},{3,15},{4,8},{5,9},{6,10},{7,11},{8,4},{9,5},... | collective-permute-start | bytes 786440 | tf_op jit(solution)/shard_map/ppermute | solution.py:206
  105.9 42.3 %collective-permute-start.24 = (bf16[64,2048]{1,0:T(8,128)(2,1)}, bf16[64,2048]{1,0:T(8,128)(2,1)}, u32[]{:S(2)}, u32[]{:S(2)}) collective-permute-start(bf16[64,2048]{1,0:T(8,128)(2,1)} %get-tuple-element.401), channel_id=1, source_target_pairs={{0,14},{1,15},{2,12},{3,13},{4,10},{5,11},{6,8},{7,9},{8,6},{9,7},... | collective-permute-start | bytes 786440 | tf_op jit(solution)/shard_map/ppermute | solution.py:206
  106.8 0.7 copy-start.5
  106.8 0.8 copy-start.6
  110.0 4.3 %collective-permute-start.11 = (bf16[256,2048]{1,0:T(8,128)(2,1)S(1)}, bf16[256,2048]{1,0:T(8,128)(2,1)S(1)}, u32[]{:S(2)}, u32[]{:S(2)}) collective-permute-start(bf16[256,2048]{1,0:T(8,128)(2,1)S(1)} %get-tuple-element.233), channel_id=1, source_target_pairs={{0,1},{1,0},{2,3},{3,2},{4,5},{5,4},{6,7},{7,6},{8,9},{9,8},{10,11... | collective-permute-start | bytes 3145736 | tf_op jit(solution)/shard_map/cond/branch_1_fun/ppermute | solution.py:209
  110.1 38.1 %all-to-all-start.3 = ((bf16[4,64,2048]{2,1,0:T(8,128)(2,1)}), bf16[4,64,2048]{2,1,0:T(8,128)(2,1)}, u32[]{:S(2)}, u32[]{:S(2)}) async-start(bf16[4,64,2048]{2,1,0:T(8,128)(2,1)} %bitcast.69), calls=%async_computation.3 | async-start | bytes 2097152 | tf_op jit(solution)/shard_map/cond/branch_1_fun/all_to_all | solution.py:226
  118.3 6.6 %collective-permute-start.12 = (bf16[256,2048]{1,0:T(8,128)(2,1)}, bf16[256,2048]{1,0:T(8,128)(2,1)}, u32[]{:S(2)}, u32[]{:S(2)}) collective-permute-start(bf16[256,2048]{1,0:T(8,128)(2,1)} %get-tuple-element.235), channel_id=1, source_target_pairs={{0,1},{1,0},{2,3},{3,2},{4,5},{5,4},{6,7},{7,6},{8,9},{9,8},{10,11... | collective-permute-start | bytes 3145736 | tf_op jit(solution)/shard_map/cond/branch_1_fun/ppermute | solution.py:209
  148.2 3.1 %copy-start.7 = (f32[32,16,16]{0,2,1:T(8,128)}, f32[32,16,16]{0,2,1:T(8,128)S(1)}, u32[]{:S(2)}) copy-start(f32[32,16,16]{0,2,1:T(8,128)S(1)} %get-tuple-element.540) | copy-start | bytes 98308
  148.3 39.0 %collective-permute-start.25 = (bf16[64,2048]{1,0:T(8,128)(2,1)}, bf16[64,2048]{1,0:T(8,128)(2,1)}, u32[]{:S(2)}, u32[]{:S(2)}) collective-permute-start(bf16[64,2048]{1,0:T(8,128)(2,1)} %get-tuple-element.430), channel_id=1, source_target_pairs={{0,8},{1,9},{2,10},{3,11},{4,12},{5,13},{6,14},{7,15},{8,0},{9,1},... | collective-permute-start | bytes 786440 | tf_op jit(solution)/shard_map/ppermute | solution.py:206
  150.9 36.4 %collective-permute-start.26 = (bf16[64,2048]{1,0:T(8,128)(2,1)}, bf16[64,2048]{1,0:T(8,128)(2,1)}, u32[]{:S(2)}, u32[]{:S(2)}) collective-permute-start(bf16[64,2048]{1,0:T(8,128)(2,1)} %get-tuple-element.431), channel_id=1, source_target_pairs={{0,12},{1,13},{2,14},{3,15},{4,8},{5,9},{6,10},{7,11},{8,4},{9,5},... | collective-permute-start | bytes 786440 | tf_op jit(solution)/shard_map/ppermute | solution.py:206
  151.3 40.0 %copy-start.1 = (bf16[512,2048]{1,0:T(8,128)(2,1)S(1)}, bf16[512,2048]{1,0:T(8,128)(2,1)}, u32[]{:S(2)}) copy-start(bf16[512,2048]{1,0:T(8,128)(2,1)} %a.3) | copy-start | bytes 6291460
  151.3 4.4 %copy-start.10 = (s32[8]{0:T(128)S(1)}, s32[8]{0:T(128)}, u32[]{:S(2)}) copy-start(s32[8]{0:T(128)} %get-tuple-element.246) | copy-start | bytes 100 | tf_op jit(solution)/shard_map/cond
  151.3 36.0 %all-to-all-start.2 = ((bf16[4,64,2048]{2,1,0:T(8,128)(2,1)}), bf16[4,64,2048]{2,1,0:T(8,128)(2,1)}, u32[]{:S(2)}, u32[]{:S(2)}) async-start(bf16[4,64,2048]{2,1,0:T(8,128)(2,1)} %bitcast.17), calls=%async_computation.2 | async-start | bytes 2097152 | tf_op jit(solution)/shard_map/cond/branch_1_fun/all_to_all | solution.py:226
  160.2 7.9 %collective-permute-start.6 = (bf16[4,32,512]{2,1,0:T(8,128)(2,1)S(1)}, bf16[4,32,512]{2,1,0:T(8,128)(2,1)S(1)}, u32[]{:S(2)}, u32[]{:S(2)}) collective-permute-start(bf16[4,32,512]{2,1,0:T(8,128)(2,1)S(1)} %get-tuple-element.552), channel_id=1, source_target_pairs={{0,2},{1,3},{2,0},{3,1},{4,6},{5,7},{6,4},{7,5},{8,10},{9,11},{10,... | collective-permute-start | bytes 393224 | tf_op jit(solution)/shard_map/cond/branch_1_fun/ppermute | solution.py:209
  162.2 6.0 %collective-permute-start.7 = (bf16[4,32,512]{2,1,0:T(8,128)(2,1)S(1)}, bf16[4,32,512]{2,1,0:T(8,128)(2,1)S(1)}, u32[]{:S(2)}, u32[]{:S(2)}) collective-permute-start(bf16[4,32,512]{2,1,0:T(8,128)(2,1)S(1)} %get-tuple-element.553), channel_id=1, source_target_pairs={{0,3},{1,2},{2,1},{3,0},{4,7},{5,6},{6,5},{7,4},{8,11},{9,10},{10,... | collective-permute-start | bytes 393224 | tf_op jit(solution)/shard_map/cond/branch_1_fun/ppermute | solution.py:209
  162.3 6.0 %collective-permute-start.5 = (bf16[4,32,512]{2,1,0:T(8,128)(2,1)S(1)}, bf16[4,32,512]{2,1,0:T(8,128)(2,1)S(1)}, u32[]{:S(2)}, u32[]{:S(2)}) collective-permute-start(bf16[4,32,512]{2,1,0:T(8,128)(2,1)S(1)} %fusion.18), channel_id=1, source_target_pairs={{0,1},{1,0},{2,3},{3,2},{4,5},{5,4},{6,7},{7,6},{8,9},{9,8},{10,11... | collective-permute-start | bytes 393224 | tf_op jit(solution)/shard_map/cond/branch_1_fun/ppermute | solution.py:209
  168.3 9.4 %collective-permute-start.10 = (bf16[4,32,512]{2,1,0:T(8,128)(2,1)S(1)}, bf16[4,32,512]{2,1,0:T(8,128)(2,1)S(1)}, u32[]{:S(2)}, u32[]{:S(2)}) collective-permute-start(bf16[4,32,512]{2,1,0:T(8,128)(2,1)S(1)} %fusion.17), channel_id=1, source_target_pairs={{0,12},{1,13},{2,14},{3,15},{4,8},{5,9},{6,10},{7,11},{8,4},{9,5},... | collective-permute-start | bytes 393224 | tf_op jit(solution)/shard_map/cond/branch_1_fun/ppermute | solution.py:206
  174.7 12.5 %collective-permute-start.9 = (bf16[4,32,512]{2,1,0:T(8,128)(2,1)S(1)}, bf16[4,32,512]{2,1,0:T(8,128)(2,1)S(1)}, u32[]{:S(2)}, u32[]{:S(2)}) collective-permute-start(bf16[4,32,512]{2,1,0:T(8,128)(2,1)S(1)} %fusion.17), channel_id=1, source_target_pairs={{0,8},{1,9},{2,10},{3,11},{4,12},{5,13},{6,14},{7,15},{8,0},{9,1},... | collective-permute-start | bytes 393224 | tf_op jit(solution)/shard_map/cond/branch_1_fun/ppermute | solution.py:206
  176.3 9.2 %collective-permute-start.8 = (bf16[4,32,512]{2,1,0:T(8,128)(2,1)S(1)}, bf16[4,32,512]{2,1,0:T(8,128)(2,1)S(1)}, u32[]{:S(2)}, u32[]{:S(2)}) collective-permute-start(bf16[4,32,512]{2,1,0:T(8,128)(2,1)S(1)} %fusion.17), channel_id=1, source_target_pairs={{0,4},{1,5},{2,6},{3,7},{4,0},{5,1},{6,2},{7,3},{8,12},{9,13},{10,... | collective-permute-start | bytes 393224 | tf_op jit(solution)/shard_map/cond/branch_1_fun/ppermute | solution.py:206
  187.3 24.1 %collective-permute-start.27 = (bf16[64,2048]{1,0:T(8,128)(2,1)}, bf16[64,2048]{1,0:T(8,128)(2,1)S(1)}, u32[]{:S(2)}, u32[]{:S(2)}) collective-permute-start(bf16[64,2048]{1,0:T(8,128)(2,1)} %get-tuple-element.438), channel_id=1, source_target_pairs={{0,10},{1,11},{2,8},{3,9},{4,14},{5,15},{6,12},{7,13},{8,2},{9,3},... | collective-permute-start | bytes 786440 | tf_op jit(solution)/shard_map/ppermute | solution.py:206
  188.8 22.6 %collective-permute-start.28 = (bf16[64,2048]{1,0:T(8,128)(2,1)}, bf16[64,2048]{1,0:T(8,128)(2,1)S(1)}, u32[]{:S(2)}, u32[]{:S(2)}) collective-permute-start(bf16[64,2048]{1,0:T(8,128)(2,1)} %get-tuple-element.439), channel_id=1, source_target_pairs={{0,14},{1,15},{2,12},{3,13},{4,10},{5,11},{6,8},{7,9},{8,6},{9,7},... | collective-permute-start | bytes 786440 | tf_op jit(solution)/shard_map/ppermute | solution.py:206
  191.3 10.4 %collective-permute-start.2 = (bf16[4,32,512]{2,1,0:T(8,128)(2,1)S(1)}, bf16[4,32,512]{2,1,0:T(8,128)(2,1)S(1)}, u32[]{:S(2)}, u32[]{:S(2)}) collective-permute-start(bf16[4,32,512]{2,1,0:T(8,128)(2,1)S(1)} %get-tuple-element.266.refs_0_), channel_id=1, source_target_pairs={{0,1},{1,0},{2,3},{3,2},{4,5},{5,4},{6,7},{7,6},{8,9},{9,8},{10,11... | collective-permute-start | bytes 393224 | tf_op jit(solution)/shard_map/cond/branch_1_fun/ppermute | solution.py:209
  191.3 10.4 %collective-permute-start.3 = (bf16[4,32,512]{2,1,0:T(8,128)(2,1)S(1)}, bf16[4,32,512]{2,1,0:T(8,128)(2,1)S(1)}, u32[]{:S(2)}, u32[]{:S(2)}) collective-permute-start(bf16[4,32,512]{2,1,0:T(8,128)(2,1)S(1)} %get-tuple-element.266.refs_0_), channel_id=1, source_target_pairs={{0,2},{1,3},{2,0},{3,1},{4,6},{5,7},{6,4},{7,5},{8,10},{9,11},{10,... | collective-permute-start | bytes 393224 | tf_op jit(solution)/shard_map/cond/branch_1_fun/ppermute | solution.py:209
  192.5 18.2 %collective-permute-start.4 = (bf16[4,32,512]{2,1,0:T(8,128)(2,1)S(1)}, bf16[4,32,512]{2,1,0:T(8,128)(2,1)S(1)}, u32[]{:S(2)}, u32[]{:S(2)}) collective-permute-start(bf16[4,32,512]{2,1,0:T(8,128)(2,1)S(1)} %get-tuple-element.266.refs_0_), channel_id=1, source_target_pairs={{0,3},{1,2},{2,1},{3,0},{4,7},{5,6},{6,5},{7,4},{8,11},{9,10},{10,... | collective-permute-start | bytes 393224 | tf_op jit(solution)/shard_map/cond/branch_1_fun/ppermute | solution.py:209
  193.3 3.8 %copy-start.3 = (bf16[512,512]{1,0:T(8,128)(2,1)S(1)}, bf16[512,512]{1,0:T(8,128)(2,1)}, u32[]{:S(2)}) copy-start(bf16[512,512]{1,0:T(8,128)(2,1)} %get-tuple-element.267.matrix) | copy-start | bytes 1572868 | tf_op jit(solution)/shard_map/cond
  211.4 1.1 copy-start.4

commit v7 on v6

--- a/solution.py
+++ b/solution.py
@@ -356,14 +356,11 @@
         )
         terms = add(mine(0), [near(mine(i).astype(BF16), i) for i in (1, 2, 3)])
         terms = terms.astype(BF16)
-        got = [terms] + [chip(terms, 2 * k) for k in range(1, far)]
-        got = [
-            jnp.stack([g[k ^ j] for j in range(far)]).astype(F32) if k else g.astype(F32)
-            for k, g in enumerate(got)
-        ]
-        while len(got) > 1:
-            got = [x + y for x, y in zip(got[::2], got[1::2])]
-        return got[0].astype(BF16), side
+        for bit in [1 << i for i in reversed(range(far.bit_length() - 1))]:
+            received = chip(terms, 2 * bit)
+            received = jnp.stack([received[j ^ bit] for j in range(far)])
+            terms = (terms.astype(F32) + received.astype(F32)).astype(BF16)
+        return terms, side
 
     own, gated_side = phase(home, gated[0], backs, permuted, reorder, relative[:far] * slab)
     rest, own, arrived = lax.optimization_barrier(

time: 215 us -> 214 us (level)
    ppermute x10, waiting for transfers between devices: 17 us -> 11.5 us  [near(): return lax.ppermute(x, 'seq', [(s, s ^ i) for s in range(count)])]
    ppermute x19 -> x18, waiting for transfers between devices: 10.8 us -> 15.4 us  [chip(): return lax.ppermute(x, 'seq', [(s, s ^ 2 * k) for s in range(count)])]
    ppermute x19 -> x18, starting transfers between devices: 41.2 us -> 40 us  [chip(): return lax.ppermute(x, 'seq', [(s, s ^ 2 * k) for s in range(count)])]
  transfers between devices with their start and end apart: 32 -> 31, of which waited for: 9 -> 9; matrix products, arithmetic and copies ran while one was open for 9% -> 10% of each run, Pallas kernels for 20% -> 20%
where the time goes in v7:
time: 214 us; the launch traced here: 212 us
  waiting for transfers between devices  60.1 us (28%)
  starting transfers between devices  58 us (27%)
  Pallas kernels  43.2 us (20%)
  blocking collectives  24.4 us (11%)
  matrix products  9.67 us (5%)
  other arithmetic  7.53 us (4%)
  local copies, waits for them, and re-layouts  7.38 us (3%)
    pallas_call x11, Pallas kernels, by_columns(): pl.pallas_call(kernel, grid=(width // columns,), in_specs=[pl.BlockSpec(m...  41 us
    ppermute x18, starting transfers between devices, chip(): return lax.ppermute(x, 'seq', [(s, s ^ 2 * k) for s in range(count)])  40 us
    all_to_all x3, waiting for transfers between devices, send_side(): lax.all_to_all(x, 'seq', split_axis=0, concat_axis=0, tiled=True, axis_in...  33.2 us
    all_to_all x1, blocking collectives, send_side(): lax.all_to_all(x, 'seq', split_axis=0, concat_axis=0, tiled=True, axis_in...  24.4 us
    ppermute x18, waiting for transfers between devices, chip(): return lax.ppermute(x, 'seq', [(s, s ^ 2 * k) for s in range(count)])  15.4 us
    all_to_all x3, starting transfers between devices, send_side(): lax.all_to_all(x, 'seq', split_axis=0, concat_axis=0, tiled=True, axis_in...  12.7 us
    ppermute x10, waiting for transfers between devices, near(): return lax.ppermute(x, 'seq', [(s, s ^ i) for s in range(count)])  11.5 us
    ppermute x10, starting transfers between devices, near(): return lax.ppermute(x, 'seq', [(s, s ^ i) for s in range(count)])  5.26 us
  transfers between devices with their start and end apart: 31, of which 9 were waited for; matrix products, arithmetic and copies ran while one was open for 10% of the time, Pallas kernels for 20%

profile of v7, /device:TPU:0, one launch (start us, length us, event | category | flops | bytes accessed | tf_op | source)
XLA Modules:
  0.0 212.3 jit_solution(2794963938287771841)
XLA Ops:
  0.7 2.7 %dynamic-slice_multiply_fusion.1 = (bf16[64,2048]{1,0:T(8,128)(2,1)}, bf16[64,2048]{1,0:T(8,128)(2,1)}, bf16[64,2048]{1,0:T(8,128)(2,1)}, bf16[64,2048]{1,0:T(8,128)(2,1)}) fusion(bf16[512,2048]{1,0:T(8,128)(2,1)} %param.19, s32[]{:T(128)S(6)} %select_n.112, bf16[512,2048]{1,0:T(8,128)(2,1)} %a.3, s32[]{:T(128)S(6)} %select_n.111, s32[]{:T(128)S(6)} %select_n.110, ...), kind=kLoop, calls=%fused_computation.57 | loop fusion | flops 2097152 | bytes 3145744 | tf_op jit(solution)/shard_map/mul | solution.py:251
  3.4 4.0 %collective-permute-start.12 = (bf16[64,2048]{1,0:T(8,128)(2,1)}, bf16[64,2048]{1,0:T(8,128)(2,1)}, u32[]{:S(2)}, u32[]{:S(2)}) collective-permute-start(bf16[64,2048]{1,0:T(8,128)(2,1)} %get-tuple-element.377), channel_id=1, source_target_pairs={{0,8},{1,9},{2,10},{3,11},{4,12},{5,13},{6,14},{7,15},{8,0},{9,1},... | collective-permute-start | bytes 786440 | tf_op jit(solution)/shard_map/ppermute | solution.py:206
  7.4 1.3 collective-permute-start.13
  8.7 3.6 %collective-permute-start.14 = (bf16[64,2048]{1,0:T(8,128)(2,1)}, bf16[64,2048]{1,0:T(8,128)(2,1)}, u32[]{:S(2)}, u32[]{:S(2)}) collective-permute-start(bf16[64,2048]{1,0:T(8,128)(2,1)} %get-tuple-element.379), channel_id=1, source_target_pairs={{0,12},{1,13},{2,14},{3,15},{4,8},{5,9},{6,10},{7,11},{8,4},{9,5},... | collective-permute-start | bytes 786440 | tf_op jit(solution)/shard_map/ppermute | solution.py:206
  13.9 18.6 %conditional.6 = (bf16[256,2048]{1,0:T(8,128)(2,1)}, bf16[64,2048]{1,0:T(8,128)(2,1)}, bf16[64,2048]{1,0:T(8,128)(2,1)}, bf16[64,2048]{1,0:T(8,128)(2,1)}, bf16[...) conditional(s32[]{:T(128)} %bitcast.23, () %tuple.70, ...), branch_computations={%region_0.1_spmd, %region_1.2_spmd} | conditional | flops 1622943616 | bytes 8788276 | solution.py:203
  14.1 1.6 convolution_convert_fusion.2.matrix
  15.8 4.2 %convolution_convert_fusion.rows = bf16[512,2048]{1,0:T(8,128)(2,1)} fusion(bf16[512,2048]{1,0:T(8,128)(2,1)} %get-tuple-element.197, s32[512]{0:T(512)S(1)} %get-tuple-element.196), kind=kOutput, calls=%fused_computation | convolution fusion | flops 1075052544 | bytes 4196352 | tf_op jit(solution)/shard_map/cond/branch_1_fun/dot_general | solution.py:269
  20.0 4.4 %branch_1_fun.12 = (bf16[256,2048]{1,0:T(8,128)(2,1)}, bf16[64,2048]{1,0:T(8,128)(2,1)}, bf16[64,2048]{1,0:T(8,128)(2,1)}, bf16[64,2048]{1,0:T(8,128)(2,1)}, bf16[64,2048]{1,0:T(8,128)(2,1)}) custom-call(bf16[512,512]{1,0:T(8,128)(2,1)S(1)} %convolution_convert_fusion.2.matrix, bf16[512,2048]{1,0:T(8,128)(2,1)} %convolution_convert_fusion.rows), custom_call_target="tpu_custom_call" | custom-call | tf_op jit(solution)/shard_map/cond/branch_1_fun/pallas_call | solution.py:159
  25.2 1.3 broadcast_in_dim.2
  26.8 2.0 fusion
  28.9 1.9 copy.54
  33.5 1.6 dynamic-slice_multiply_fusion
  35.1 24.5 %conditional.7 = (bf16[256,2048]{1,0:T(8,128)(2,1)S(1)}) conditional(s32[]{:T(128)} %bitcast.23, () %tuple.73, bf16[256,2048]{1,0:T(8,128)(2,1)S(1)} %dynamic-slice_multiply_fusion), branch_computations={%region_2.3_spmd, %region_3.4_spmd} | conditional | bytes 2097160 | solution.py:203
  35.1 24.4 %all_to_all.36 = bf16[4,64,2048]{2,1,0:T(8,128)(2,1)S(1)} all-to-all(bf16[4,64,2048]{2,1,0:T(8,128)(2,1)S(1)} %bitcast.68), channel_id=1, replica_groups={{0,2,4,6},{1,3,5,7},{8,10,12,14},{9,11,13,15},{16,18,20,22},{17,19,21,2..., dimensions={0} | all-to-all | bytes 2097152 | tf_op jit(solution)/shard_map/cond/branch_1_fun/all_to_all | solution.py:226
  59.6 3.1 %collective-permute-start.17 = (bf16[64,2048]{1,0:T(8,128)(2,1)}, bf16[64,2048]{1,0:T(8,128)(2,1)S(1)}, u32[]{:S(2)}, u32[]{:S(2)}) collective-permute-start(bf16[64,2048]{1,0:T(8,128)(2,1)} %get-tuple-element.394), channel_id=1, source_target_pairs={{0,10},{1,11},{2,8},{3,9},{4,14},{5,15},{6,12},{7,13},{8,2},{9,3},... | collective-permute-start | bytes 786440 | tf_op jit(solution)/shard_map/ppermute | solution.py:206
  63.7 3.8 %collective-permute-start.19 = (bf16[64,2048]{1,0:T(8,128)(2,1)}, bf16[64,2048]{1,0:T(8,128)(2,1)}, u32[]{:S(2)}, u32[]{:S(2)}) collective-permute-start(bf16[64,2048]{1,0:T(8,128)(2,1)} %get-tuple-element.396), channel_id=1, source_target_pairs={{0,14},{1,15},{2,12},{3,13},{4,10},{5,11},{6,8},{7,9},{8,6},{9,7},... | collective-permute-start | bytes 786440 | tf_op jit(solution)/shard_map/ppermute | solution.py:206
  67.5 30.9 %conditional.8 = (bf16[256,2048]{1,0:T(8,128)(2,1)}, bf16[256,2048]{1,0:T(8,128)(2,1)}, bf16[64,2048]{1,0:T(8,128)(2,1)}, bf16[64,2048]{1,0:T(8,128)(2,1)}, bf16...) conditional(s32[]{:T(128)} %bitcast.23, () %tuple.68, ...), branch_computations={%region_4.5_spmd, %region_5.6_spmd} | conditional | bytes 12583088 | solution.py:203
  67.5 3.5 %branch_1_fun.13 = (bf16[256,2048]{1,0:T(8,128)(2,1)}, bf16[256,2048]{1,0:T(8,128)(2,1)S(1)}) custom-call(s32[1]{0:T(128)} %get-tuple-element.208.core, bf16[256,2048]{1,0:T(8,128)(2,1)S(1)} %get-tuple-element.210.refs_0_, bf16[64,2048]{1,0:T(8,128)(2,1)} %get-tuple-element.211.refs_1_, bf16[64,2048]{1,0:T(8,128)(2,1)} %get-tuple-element.212.refs_2_, ...), custom_call_target="tpu_custom_call" | custom-call | tf_op jit(solution)/shard_map/cond/branch_1_fun/pallas_call | solution.py:159
  71.0 4.2 %all-to-all-start.1 = ((bf16[4,64,2048]{2,1,0:T(8,128)(2,1)}), bf16[4,64,2048]{2,1,0:T(8,128)(2,1)}, u32[]{:S(2)}, u32[]{:S(2)}) async-start(bf16[4,64,2048]{2,1,0:T(8,128)(2,1)} %bitcast.5), calls=%async_computation.1 | async-start | bytes 2097152 | tf_op jit(solution)/shard_map/cond/branch_1_fun/all_to_all | solution.py:226
  76.5 3.5 %branch_1_fun.14 = (bf16[256,2048]{1,0:T(8,128)(2,1)S(1)}, bf16[256,2048]{1,0:T(8,128)(2,1)S(1)}) custom-call(bf16[512,512]{1,0:T(8,128)(2,1)S(1)} %copy.19.matrix, bf16[256,2048]{1,0:T(8,128)(2,1)} %get-tuple-element.605.own, bf16[256,2048]{1,0:T(8,128)(2,1)} %collective-permute-done.other), custom_call_target="tpu_custom_call" | custom-call | tf_op jit(solution)/shard_map/cond/branch_1_fun/pallas_call | solution.py:159
  80.6 2.3 %collective-permute-done.1.other = bf16[256,2048]{1,0:T(8,128)(2,1)S(1)} collective-permute-done((bf16[256,2048]{1,0:T(8,128)(2,1)S(1)}, bf16[256,2048]{1,0:T(8,128)(2,1)S(1)}, u32[]{:S(2)}, u32[]{:S(2)}) %collective-permute-start.1) | collective-permute-done | bytes 1048608 | tf_op jit(solution)/shard_map/cond/branch_1_fun/ppermute | solution.py:209
  82.9 2.0 branch_1_fun.15
  84.9 13.5 %all-to-all-done.1 = bf16[4,64,2048]{2,1,0:T(8,128)(2,1)} async-done(((bf16[4,64,2048]{2,1,0:T(8,128)(2,1)}), bf16[4,64,2048]{2,1,0:T(8,128)(2,1)}, u32[]{:S(2)}, u32[]{:S(2)}) %all-to-all-start.1) | async-done | bytes 1048608 | tf_op jit(solution)/shard_map/cond/branch_1_fun/all_to_all | solution.py:226
  98.4 3.6 %collective-permute-start.20 = (bf16[64,2048]{1,0:T(8,128)(2,1)}, bf16[64,2048]{1,0:T(8,128)(2,1)}, u32[]{:S(2)}, u32[]{:S(2)}) collective-permute-start(bf16[64,2048]{1,0:T(8,128)(2,1)} %get-tuple-element.398), channel_id=1, source_target_pairs={{0,8},{1,9},{2,10},{3,11},{4,12},{5,13},{6,14},{7,15},{8,0},{9,1},... | collective-permute-start | bytes 786440 | tf_op jit(solution)/shard_map/ppermute | solution.py:206
  102.4 3.5 %collective-permute-start.22 = (bf16[64,2048]{1,0:T(8,128)(2,1)}, bf16[64,2048]{1,0:T(8,128)(2,1)}, u32[]{:S(2)}, u32[]{:S(2)}) collective-permute-start(bf16[64,2048]{1,0:T(8,128)(2,1)} %get-tuple-element.400), channel_id=1, source_target_pairs={{0,12},{1,13},{2,14},{3,15},{4,8},{5,9},{6,10},{7,11},{8,4},{9,5},... | collective-permute-start | bytes 786440 | tf_op jit(solution)/shard_map/ppermute | solution.py:206
  106.8 41.4 %conditional.9 = (bf16[256,2048]{1,0:T(8,128)(2,1)}, bf16[256,2048]{1,0:T(8,128)(2,1)}, bf16[64,2048]{1,0:T(8,128)(2,1)}, bf16[64,2048]{1,0:T(8,128)(2,1)}, bf16...) conditional(s32[]{:T(128)} %bitcast.23, () %tuple.77, ...), branch_computations={%region_6.7_spmd, %region_7.8_spmd} | conditional | flops 1843200 | bytes 14615264 | solution.py:203
  107.6 2.5 %branch_1_fun.16 = (bf16[256,2048]{1,0:T(8,128)(2,1)S(1)}, bf16[256,2048]{1,0:T(8,128)(2,1)S(1)}) custom-call(s32[1]{0:T(128)} %get-tuple-element.225.core, bf16[256,2048]{1,0:T(8,128)(2,1)} %get-tuple-element.227.refs_0_, bf16[64,2048]{1,0:T(8,128)(2,1)} %copy-done.5, bf16[64,2048]{1,0:T(8,128)(2,1)} %copy-done.6, ...), custom_call_target="tpu_custom_call" | custom-call | tf_op jit(solution)/shard_map/cond/branch_1_fun/pallas_call | solution.py:159
  110.1 4.3 %all-to-all-start.3 = ((bf16[4,64,2048]{2,1,0:T(8,128)(2,1)}), bf16[4,64,2048]{2,1,0:T(8,128)(2,1)}, u32[]{:S(2)}, u32[]{:S(2)}) async-start(bf16[4,64,2048]{2,1,0:T(8,128)(2,1)} %bitcast.69), calls=%async_computation.3 | async-start | bytes 2097152 | tf_op jit(solution)/shard_map/cond/branch_1_fun/all_to_all | solution.py:226
  114.4 3.9 %branch_1_fun.17 = (bf16[256,2048]{1,0:T(8,128)(2,1)S(1)}, bf16[256,2048]{1,0:T(8,128)(2,1)}) custom-call(bf16[512,512]{1,0:T(8,128)(2,1)} %get-tuple-element.226.matrix, bf16[256,2048]{1,0:T(8,128)(2,1)S(1)} %get-tuple-element.232.own.refs_2_, bf16[256,2048]{1,0:T(8,128)(2,1)S(1)} %collective-permute-done.10.other.refs_3_), custom_call_target="tpu_custom_call" | custom-call | tf_op jit(solution)/shard_map/cond/branch_1_fun/pallas_call | solution.py:159
  118.9 4.8 %branch_1_fun.19 = f32[512,16]{1,0:T(8,128)S(1)} custom-call(bf16[512,512]{1,0:T(8,128)(2,1)S(1)} %convert_element_type.67.same, bf16[512,16]{1,0:T(8,128)(2,1)} %get-tuple-element.242.spread_out, bf16[256,2048]{1,0:T(8,128)(2,1)} %get-tuple-element.243.refs_0_, bf16[256,2048]{1,0:T(8,128)(2,1)} %get-tuple-element.244.refs_1_, ...), custom_call_target="tpu_custom_call" | custom-call | tf_op jit(solution)/shard_map/cond/branch_1_fun/pallas_call | solution.py:159
  124.9 3.6 %branch_1_fun.18 = (bf16[256,2048]{1,0:T(8,128)(2,1)}, bf16[64,2048]{1,0:T(8,128)(2,1)}, bf16[64,2048]{1,0:T(8,128)(2,1)}, bf16[64,2048]{1,0:T(8,128)(2,1)}, bf16[64,2048]{1,0:T(8,128)(2,1)}) custom-call(s32[1]{0:T(128)} %get-tuple-element.225.core, bf16[256,2048]{1,0:T(8,128)(2,1)S(1)} %get-tuple-element.234.own, ...), custom_call_target="tpu_custom_call" | custom-call | tf_op jit(solution)/shard_map/cond/branch_1_fun/pallas_call | solution.py:159
  128.5 19.7 %all-to-all-done.3 = bf16[4,64,2048]{2,1,0:T(8,128)(2,1)} async-done(((bf16[4,64,2048]{2,1,0:T(8,128)(2,1)}), bf16[4,64,2048]{2,1,0:T(8,128)(2,1)}, u32[]{:S(2)}, u32[]{:S(2)}) %all-to-all-start.3) | async-done | bytes 1048608 | tf_op jit(solution)/shard_map/cond/branch_1_fun/all_to_all | solution.py:226
  148.2 2.6 %collective-permute-start.24 = (bf16[64,2048]{1,0:T(8,128)(2,1)}, bf16[64,2048]{1,0:T(8,128)(2,1)}, u32[]{:S(2)}, u32[]{:S(2)}) collective-permute-start(bf16[64,2048]{1,0:T(8,128)(2,1)} %get-tuple-element.430), channel_id=1, source_target_pairs={{0,8},{1,9},{2,10},{3,11},{4,12},{5,13},{6,14},{7,15},{8,0},{9,1},... | collective-permute-start | bytes 786440 | tf_op jit(solution)/shard_map/ppermute | solution.py:206
  151.3 34.8 %conditional.10 = (bf16[4,32,512]{2,1,0:T(8,128)(2,1)S(1)}, bf16[256,2048]{1,0:T(8,128)(2,1)}) conditional(s32[]{:T(128)} %bitcast.23, () %tuple.80, (s32[8]{0:T(128)}, bf16[512,512]{1,0:T(8,128)(2,1)}, bf16[512,2048]{1,0:T(8,128)(2,1)}, bf16[256,2048]{1,0:T(8,128)(2,1)}, bf16[64,2048]{1,0:T(8,128)(2,1)}, /*index=5*/bf16[64,2048]{1,0:T(8,128)(2,1)}, ...), branch_computations={%region_8.9_spmd, %region_9.10_spmd} | conditional | flops 1245195 | bytes 10223992 | solution.py:203
  152.1 4.4 %branch_1_fun.20 = f32[512,512]{1,0:T(8,128)S(1)} custom-call(s32[4]{0:T(128)S(1)} %slice_multiply_fusion.starts, bf16[512,512]{1,0:T(8,128)(2,1)} %get-tuple-element.247.order, bf16[512,2048]{1,0:T(8,128)(2,1)} %get-tuple-element.248.right, bf16[256,2048]{1,0:T(8,128)(2,1)} %get-tuple-element.249.side, bf16[64,2048]{1,0:T(8,128)(2,1)} %get-tuple-element.250.refs_0_, ...), custom_call_target="tpu_custom_call" | custom-call | tf_op jit(solution)/shard_map/cond/branch_1_fun/pallas_call | solution.py:159
  157.2 1.4 collective-permute-start.6
  158.6 4.2 %all-to-all-start.2 = ((bf16[4,64,2048]{2,1,0:T(8,128)(2,1)}), bf16[4,64,2048]{2,1,0:T(8,128)(2,1)}, u32[]{:S(2)}, u32[]{:S(2)}) async-start(bf16[4,64,2048]{2,1,0:T(8,128)(2,1)} %bitcast.17), calls=%async_computation.2 | async-start | bytes 2097152 | tf_op jit(solution)/shard_map/cond/branch_1_fun/all_to_all | solution.py:226
  164.9 1.7 collective-permute-start.8
  166.5 11.6 %collective-permute-done.8 = bf16[4,32,512]{2,1,0:T(8,128)(2,1)S(1)} collective-permute-done((bf16[4,32,512]{2,1,0:T(8,128)(2,1)S(1)}, bf16[4,32,512]{2,1,0:T(8,128)(2,1)S(1)}, u32[]{:S(2)}, u32[]{:S(2)}) %collective-permute-start.8) | collective-permute-done | bytes 131104 | tf_op jit(solution)/shard_map/cond/branch_1_fun/ppermute | solution.py:206
  178.2 4.1 %collective-permute-start.9 = (bf16[4,32,512]{2,1,0:T(8,128)(2,1)S(1)}, bf16[4,32,512]{2,1,0:T(8,128)(2,1)S(1)}, u32[]{:S(2)}, u32[]{:S(2)}) collective-permute-start(bf16[4,32,512]{2,1,0:T(8,128)(2,1)S(1)} %add_convert_fusion.1), channel_id=1, source_target_pairs={{0,4},{1,5},{2,6},{3,7},{4,0},{5,1},{6,2},{7,3},{8,12},{9,13},{10,... | collective-permute-start | bytes 393224 | tf_op jit(solution)/shard_map/cond/branch_1_fun/ppermute | solution.py:206
  182.3 3.8 %collective-permute-done.9 = bf16[4,32,512]{2,1,0:T(8,128)(2,1)S(1)} collective-permute-done((bf16[4,32,512]{2,1,0:T(8,128)(2,1)S(1)}, bf16[4,32,512]{2,1,0:T(8,128)(2,1)S(1)}, u32[]{:S(2)}, u32[]{:S(2)}) %collective-permute-start.9) | collective-permute-done | bytes 131104 | tf_op jit(solution)/shard_map/cond/branch_1_fun/ppermute | solution.py:206
  186.2 2.3 %collective-permute-start.26 = (bf16[64,2048]{1,0:T(8,128)(2,1)}, bf16[64,2048]{1,0:T(8,128)(2,1)S(1)}, u32[]{:S(2)}, u32[]{:S(2)}) collective-permute-start(bf16[64,2048]{1,0:T(8,128)(2,1)} %get-tuple-element.438), channel_id=1, source_target_pairs={{0,10},{1,11},{2,8},{3,9},{4,14},{5,15},{6,12},{7,13},{8,2},{9,3},... | collective-permute-start | bytes 786440 | tf_op jit(solution)/shard_map/ppermute | solution.py:206
  188.4 2.8 %collective-permute-start.27 = (bf16[64,2048]{1,0:T(8,128)(2,1)}, bf16[64,2048]{1,0:T(8,128)(2,1)S(1)}, u32[]{:S(2)}, u32[]{:S(2)}) collective-permute-start(bf16[64,2048]{1,0:T(8,128)(2,1)} %get-tuple-element.439), channel_id=1, source_target_pairs={{0,14},{1,15},{2,12},{3,13},{4,10},{5,11},{6,8},{7,9},{8,6},{9,7},... | collective-permute-start | bytes 786440 | tf_op jit(solution)/shard_map/ppermute | solution.py:206
  191.2 19.3 %conditional.11 = (f32[512,512]{1,0:T(8,128)S(1)}, bf16[512,2048]{1,0:T(8,128)(2,1)}, bf16[512,2048]{1,0:T(8,128)(2,1)}) conditional(s32[]{:T(128)} %bitcast.23, () %tuple.67, (s32[]{:T(128)}, s32[16]{0:T(128)S(1)}, s32[16]{0:T(128)S(1)}, s32[16]{0:T(128)S(1)}, pred[16]{0:T(512)(128)(4,1)S(1)}, /*index=5*/s32[16]{0:T(128)S(1)}, s32[16]{0:T(128)S(1)}, ...), branch_computations={%region_10.11_spmd, %region_11.12_spmd} | conditional | flops 550 | bytes 5242912 | solution.py:203
  193.2 3.8 %branch_1_fun.23 = bf16[512,2048]{1,0:T(8,128)(2,1)} custom-call(s32[3]{0:T(128)S(1)} %pad_add_fusion.starts, bf16[512,2048]{1,0:T(8,128)(2,1)S(1)} %get-tuple-element.276.a, bf16[256,2048]{1,0:T(8,128)(2,1)} %get-tuple-element.277.refs_0_, bf16[64,2048]{1,0:T(8,128)(2,1)} %get-tuple-element.278.refs_1_, bf16[64,2048]{1,0:T(8,128)(2,1)} %get-tuple-element.279.refs_2_), custom_call_target="tpu_custom_call" | custom-call | tf_op jit(solution)/shard_map/cond/branch_1_fun/pallas_call | solution.py:159
  197.1 4.5 %branch_1_fun.22 = bf16[512,2048]{1,0:T(8,128)(2,1)} custom-call(bf16[512,512]{1,0:T(8,128)(2,1)S(1)} %copy-done.3, bf16[256,2048]{1,0:T(8,128)(2,1)} %get-tuple-element.268.refs_0_, bf16[64,2048]{1,0:T(8,128)(2,1)} %get-tuple-element.269.refs_1_, bf16[64,2048]{1,0:T(8,128)(2,1)} %get-tuple-element.270.refs_2_, bf16[64,2048]{1,0:T(8,128)(2,1)} %get-tuple-element.271.refs_3_, ...), custom_call_target="tpu_custom_call" | custom-call | tf_op jit(solution)/shard_map/cond/branch_1_fun/pallas_call | solution.py:159
  201.7 5.9 %collective-permute-done.3.refs_2_ = bf16[4,32,512]{2,1,0:T(8,128)(2,1)S(1)} collective-permute-done((bf16[4,32,512]{2,1,0:T(8,128)(2,1)S(1)}, bf16[4,32,512]{2,1,0:T(8,128)(2,1)S(1)}, u32[]{:S(2)}, u32[]{:S(2)}) %collective-permute-start.3) | collective-permute-done | bytes 131104 | tf_op jit(solution)/shard_map/cond/branch_1_fun/ppermute | solution.py:209
  207.6 2.3 %collective-permute-done.4.refs_3_ = bf16[4,32,512]{2,1,0:T(8,128)(2,1)S(1)} collective-permute-done((bf16[4,32,512]{2,1,0:T(8,128)(2,1)S(1)}, bf16[4,32,512]{2,1,0:T(8,128)(2,1)S(1)}, u32[]{:S(2)}, u32[]{:S(2)}) %collective-permute-start.4) | collective-permute-done | bytes 131104 | tf_op jit(solution)/shard_map/cond/branch_1_fun/ppermute | solution.py:209
  (109 shorter events, 19.8 us)
Async XLA Ops:
  0.6 12.0 %copy-start.10 = (s32[512]{0:T(512)S(1)}, s32[512]{0:T(512)}, u32[]{:S(2)}) copy-start(s32[512]{0:T(512)} %param.23) | copy-start | bytes 6148
  0.6 13.2 %copy-start.8 = (bf16[32,16,16]{0,2,1:T(8,128)(2,1)S(1)}, bf16[32,16,16]{0,2,1:T(8,128)(2,1)}, u32[]{:S(2)}) copy-start(bf16[32,16,16]{0,2,1:T(8,128)(2,1)} %param.22) | copy-start | bytes 49156
  3.4 56.2 %collective-permute-start.12 = (bf16[64,2048]{1,0:T(8,128)(2,1)}, bf16[64,2048]{1,0:T(8,128)(2,1)}, u32[]{:S(2)}, u32[]{:S(2)}) collective-permute-start(bf16[64,2048]{1,0:T(8,128)(2,1)} %get-tuple-element.377), channel_id=1, source_target_pairs={{0,8},{1,9},{2,10},{3,11},{4,12},{5,13},{6,14},{7,15},{8,0},{9,1},... | collective-permute-start | bytes 786440 | tf_op jit(solution)/shard_map/ppermute | solution.py:206
  7.4 52.1 %collective-permute-start.13 = (bf16[64,2048]{1,0:T(8,128)(2,1)}, bf16[64,2048]{1,0:T(8,128)(2,1)}, u32[]{:S(2)}, u32[]{:S(2)}) collective-permute-start(bf16[64,2048]{1,0:T(8,128)(2,1)} %get-tuple-element.378), channel_id=1, source_target_pairs={{0,10},{1,11},{2,8},{3,9},{4,14},{5,15},{6,12},{7,13},{8,2},{9,3},... | collective-permute-start | bytes 786440 | tf_op jit(solution)/shard_map/ppermute | solution.py:206
  8.7 50.8 %collective-permute-start.14 = (bf16[64,2048]{1,0:T(8,128)(2,1)}, bf16[64,2048]{1,0:T(8,128)(2,1)}, u32[]{:S(2)}, u32[]{:S(2)}) collective-permute-start(bf16[64,2048]{1,0:T(8,128)(2,1)} %get-tuple-element.379), channel_id=1, source_target_pairs={{0,12},{1,13},{2,14},{3,15},{4,8},{5,9},{6,10},{7,11},{8,4},{9,5},... | collective-permute-start | bytes 786440 | tf_op jit(solution)/shard_map/ppermute | solution.py:206
  12.3 47.3 %collective-permute-start.15 = (bf16[64,2048]{1,0:T(8,128)(2,1)}, bf16[64,2048]{1,0:T(8,128)(2,1)}, u32[]{:S(2)}, u32[]{:S(2)}) collective-permute-start(bf16[64,2048]{1,0:T(8,128)(2,1)} %get-tuple-element.380), channel_id=1, source_target_pairs={{0,14},{1,15},{2,12},{3,13},{4,10},{5,11},{6,8},{7,9},{8,6},{9,7},... | collective-permute-start | bytes 786440 | tf_op jit(solution)/shard_map/ppermute | solution.py:206
  12.6 1.3 copy-start.9
  13.9 19.6 %copy-start = (bf16[512,2048]{1,0:T(8,128)(2,1)S(1)}, bf16[512,2048]{1,0:T(8,128)(2,1)}, u32[]{:S(2)}) copy-start(bf16[512,2048]{1,0:T(8,128)(2,1)} %a.3) | copy-start | bytes 6291460
  32.5 2.6 %copy-start.2 = (bf16[512,512]{1,0:T(8,128)(2,1)}, bf16[512,512]{1,0:T(8,128)(2,1)S(1)}, u32[]{:S(2)}) copy-start(bf16[512,512]{1,0:T(8,128)(2,1)S(1)} %get-tuple-element.433) | copy-start | bytes 1572868
  32.5 65.9 %collective-permute-start.16 = (bf16[64,2048]{1,0:T(8,128)(2,1)}, bf16[64,2048]{1,0:T(8,128)(2,1)S(1)}, u32[]{:S(2)}, u32[]{:S(2)}) collective-permute-start(bf16[64,2048]{1,0:T(8,128)(2,1)} %get-tuple-element.369), channel_id=1, source_target_pairs={{0,8},{1,9},{2,10},{3,11},{4,12},{5,13},{6,14},{7,15},{8,0},{9,1},... | collective-permute-start | bytes 786440 | tf_op jit(solution)/shard_map/ppermute | solution.py:206
  59.6 38.8 %collective-permute-start.17 = (bf16[64,2048]{1,0:T(8,128)(2,1)}, bf16[64,2048]{1,0:T(8,128)(2,1)S(1)}, u32[]{:S(2)}, u32[]{:S(2)}) collective-permute-start(bf16[64,2048]{1,0:T(8,128)(2,1)} %get-tuple-element.394), channel_id=1, source_target_pairs={{0,10},{1,11},{2,8},{3,9},{4,14},{5,15},{6,12},{7,13},{8,2},{9,3},... | collective-permute-start | bytes 786440 | tf_op jit(solution)/shard_map/ppermute | solution.py:206
  62.7 35.7 %collective-permute-start.18 = (bf16[64,2048]{1,0:T(8,128)(2,1)}, bf16[64,2048]{1,0:T(8,128)(2,1)}, u32[]{:S(2)}, u32[]{:S(2)}) collective-permute-start(bf16[64,2048]{1,0:T(8,128)(2,1)} %get-tuple-element.395), channel_id=1, source_target_pairs={{0,12},{1,13},{2,14},{3,15},{4,8},{5,9},{6,10},{7,11},{8,4},{9,5},... | collective-permute-start | bytes 786440 | tf_op jit(solution)/shard_map/ppermute | solution.py:206
  63.7 34.7 %collective-permute-start.19 = (bf16[64,2048]{1,0:T(8,128)(2,1)}, bf16[64,2048]{1,0:T(8,128)(2,1)}, u32[]{:S(2)}, u32[]{:S(2)}) collective-permute-start(bf16[64,2048]{1,0:T(8,128)(2,1)} %get-tuple-element.396), channel_id=1, source_target_pairs={{0,14},{1,15},{2,12},{3,13},{4,10},{5,11},{6,8},{7,9},{8,6},{9,7},... | collective-permute-start | bytes 786440 | tf_op jit(solution)/shard_map/ppermute | solution.py:206
  71.0 5.5 %collective-permute-start = (bf16[256,2048]{1,0:T(8,128)(2,1)S(1)}, bf16[256,2048]{1,0:T(8,128)(2,1)}, u32[]{:S(2)}, u32[]{:S(2)}) collective-permute-start(bf16[256,2048]{1,0:T(8,128)(2,1)S(1)} %get-tuple-element.216), channel_id=1, source_target_pairs={{0,1},{1,0},{2,3},{3,2},{4,5},{5,4},{6,7},{7,6},{8,9},{9,8},{10,11... | collective-permute-start | bytes 3145736 | tf_op jit(solution)/shard_map/cond/branch_1_fun/ppermute | solution.py:209
  71.0 27.4 %all-to-all-start.1 = ((bf16[4,64,2048]{2,1,0:T(8,128)(2,1)}), bf16[4,64,2048]{2,1,0:T(8,128)(2,1)}, u32[]{:S(2)}, u32[]{:S(2)}) async-start(bf16[4,64,2048]{2,1,0:T(8,128)(2,1)} %bitcast.5), calls=%async_computation.1 | async-start | bytes 2097152 | tf_op jit(solution)/shard_map/cond/branch_1_fun/all_to_all | solution.py:226
  80.0 2.9 %collective-permute-start.1 = (bf16[256,2048]{1,0:T(8,128)(2,1)S(1)}, bf16[256,2048]{1,0:T(8,128)(2,1)S(1)}, u32[]{:S(2)}, u32[]{:S(2)}) collective-permute-start(bf16[256,2048]{1,0:T(8,128)(2,1)S(1)} %get-tuple-element.218), channel_id=1, source_target_pairs={{0,1},{1,0},{2,3},{3,2},{4,5},{5,4},{6,7},{7,6},{8,9},{9,8},{10,11... | collective-permute-start | bytes 3145736 | tf_op jit(solution)/shard_map/cond/branch_1_fun/ppermute | solution.py:209
  98.4 49.8 %collective-permute-start.20 = (bf16[64,2048]{1,0:T(8,128)(2,1)}, bf16[64,2048]{1,0:T(8,128)(2,1)}, u32[]{:S(2)}, u32[]{:S(2)}) collective-permute-start(bf16[64,2048]{1,0:T(8,128)(2,1)} %get-tuple-element.398), channel_id=1, source_target_pairs={{0,8},{1,9},{2,10},{3,11},{4,12},{5,13},{6,14},{7,15},{8,0},{9,1},... | collective-permute-start | bytes 786440 | tf_op jit(solution)/shard_map/ppermute | solution.py:206
  102.0 46.2 %collective-permute-start.21 = (bf16[64,2048]{1,0:T(8,128)(2,1)}, bf16[64,2048]{1,0:T(8,128)(2,1)}, u32[]{:S(2)}, u32[]{:S(2)}) collective-permute-start(bf16[64,2048]{1,0:T(8,128)(2,1)} %get-tuple-element.399), channel_id=1, source_target_pairs={{0,10},{1,11},{2,8},{3,9},{4,14},{5,15},{6,12},{7,13},{8,2},{9,3},... | collective-permute-start | bytes 786440 | tf_op jit(solution)/shard_map/ppermute | solution.py:206
  102.4 45.8 %collective-permute-start.22 = (bf16[64,2048]{1,0:T(8,128)(2,1)}, bf16[64,2048]{1,0:T(8,128)(2,1)}, u32[]{:S(2)}, u32[]{:S(2)}) collective-permute-start(bf16[64,2048]{1,0:T(8,128)(2,1)} %get-tuple-element.400), channel_id=1, source_target_pairs={{0,12},{1,13},{2,14},{3,15},{4,8},{5,9},{6,10},{7,11},{8,4},{9,5},... | collective-permute-start | bytes 786440 | tf_op jit(solution)/shard_map/ppermute | solution.py:206
  105.9 42.3 %collective-permute-start.23 = (bf16[64,2048]{1,0:T(8,128)(2,1)}, bf16[64,2048]{1,0:T(8,128)(2,1)}, u32[]{:S(2)}, u32[]{:S(2)}) collective-permute-start(bf16[64,2048]{1,0:T(8,128)(2,1)} %get-tuple-element.401), channel_id=1, source_target_pairs={{0,14},{1,15},{2,12},{3,13},{4,10},{5,11},{6,8},{7,9},{8,6},{9,7},... | collective-permute-start | bytes 786440 | tf_op jit(solution)/shard_map/ppermute | solution.py:206
  106.8 0.7 copy-start.5
  106.8 0.8 copy-start.6
  110.0 4.3 %collective-permute-start.10 = (bf16[256,2048]{1,0:T(8,128)(2,1)S(1)}, bf16[256,2048]{1,0:T(8,128)(2,1)S(1)}, u32[]{:S(2)}, u32[]{:S(2)}) collective-permute-start(bf16[256,2048]{1,0:T(8,128)(2,1)S(1)} %get-tuple-element.233), channel_id=1, source_target_pairs={{0,1},{1,0},{2,3},{3,2},{4,5},{5,4},{6,7},{7,6},{8,9},{9,8},{10,11... | collective-permute-start | bytes 3145736 | tf_op jit(solution)/shard_map/cond/branch_1_fun/ppermute | solution.py:209
  110.1 38.1 %all-to-all-start.3 = ((bf16[4,64,2048]{2,1,0:T(8,128)(2,1)}), bf16[4,64,2048]{2,1,0:T(8,128)(2,1)}, u32[]{:S(2)}, u32[]{:S(2)}) async-start(bf16[4,64,2048]{2,1,0:T(8,128)(2,1)} %bitcast.69), calls=%async_computation.3 | async-start | bytes 2097152 | tf_op jit(solution)/shard_map/cond/branch_1_fun/all_to_all | solution.py:226
  118.3 6.6 %collective-permute-start.11 = (bf16[256,2048]{1,0:T(8,128)(2,1)}, bf16[256,2048]{1,0:T(8,128)(2,1)}, u32[]{:S(2)}, u32[]{:S(2)}) collective-permute-start(bf16[256,2048]{1,0:T(8,128)(2,1)} %get-tuple-element.235), channel_id=1, source_target_pairs={{0,1},{1,0},{2,3},{3,2},{4,5},{5,4},{6,7},{7,6},{8,9},{9,8},{10,11... | collective-permute-start | bytes 3145736 | tf_op jit(solution)/shard_map/cond/branch_1_fun/ppermute | solution.py:209
  148.2 3.1 %copy-start.7 = (f32[32,16,16]{0,2,1:T(8,128)}, f32[32,16,16]{0,2,1:T(8,128)S(1)}, u32[]{:S(2)}) copy-start(f32[32,16,16]{0,2,1:T(8,128)S(1)} %get-tuple-element.540) | copy-start | bytes 98308
  148.2 37.9 %collective-permute-start.24 = (bf16[64,2048]{1,0:T(8,128)(2,1)}, bf16[64,2048]{1,0:T(8,128)(2,1)}, u32[]{:S(2)}, u32[]{:S(2)}) collective-permute-start(bf16[64,2048]{1,0:T(8,128)(2,1)} %get-tuple-element.430), channel_id=1, source_target_pairs={{0,8},{1,9},{2,10},{3,11},{4,12},{5,13},{6,14},{7,15},{8,0},{9,1},... | collective-permute-start | bytes 786440 | tf_op jit(solution)/shard_map/ppermute | solution.py:206
  150.9 35.3 %collective-permute-start.25 = (bf16[64,2048]{1,0:T(8,128)(2,1)}, bf16[64,2048]{1,0:T(8,128)(2,1)}, u32[]{:S(2)}, u32[]{:S(2)}) collective-permute-start(bf16[64,2048]{1,0:T(8,128)(2,1)} %get-tuple-element.431), channel_id=1, source_target_pairs={{0,12},{1,13},{2,14},{3,15},{4,8},{5,9},{6,10},{7,11},{8,4},{9,5},... | collective-permute-start | bytes 786440 | tf_op jit(solution)/shard_map/ppermute | solution.py:206
  151.3 39.9 %copy-start.1 = (bf16[512,2048]{1,0:T(8,128)(2,1)S(1)}, bf16[512,2048]{1,0:T(8,128)(2,1)}, u32[]{:S(2)}) copy-start(bf16[512,2048]{1,0:T(8,128)(2,1)} %a.3) | copy-start | bytes 6291460
  157.2 6.5 %collective-permute-start.6 = (bf16[4,32,512]{2,1,0:T(8,128)(2,1)}, bf16[4,32,512]{2,1,0:T(8,128)(2,1)S(1)}, u32[]{:S(2)}, u32[]{:S(2)}) collective-permute-start(bf16[4,32,512]{2,1,0:T(8,128)(2,1)} %get-tuple-element.552), channel_id=1, source_target_pairs={{0,2},{1,3},{2,0},{3,1},{4,6},{5,7},{6,4},{7,5},{8,10},{9,11},{10,... | collective-permute-start | bytes 393224 | tf_op jit(solution)/shard_map/cond/branch_1_fun/ppermute | solution.py:209
  158.6 5.7 %collective-permute-start.7 = (bf16[4,32,512]{2,1,0:T(8,128)(2,1)S(1)}, bf16[4,32,512]{2,1,0:T(8,128)(2,1)S(1)}, u32[]{:S(2)}, u32[]{:S(2)}) collective-permute-start(bf16[4,32,512]{2,1,0:T(8,128)(2,1)S(1)} %get-tuple-element.553), channel_id=1, source_target_pairs={{0,3},{1,2},{2,1},{3,0},{4,7},{5,6},{6,5},{7,4},{8,11},{9,10},{10,... | collective-permute-start | bytes 393224 | tf_op jit(solution)/shard_map/cond/branch_1_fun/ppermute | solution.py:209
  158.6 27.5 %all-to-all-start.2 = ((bf16[4,64,2048]{2,1,0:T(8,128)(2,1)}), bf16[4,64,2048]{2,1,0:T(8,128)(2,1)}, u32[]{:S(2)}, u32[]{:S(2)}) async-start(bf16[4,64,2048]{2,1,0:T(8,128)(2,1)} %bitcast.17), calls=%async_computation.2 | async-start | bytes 2097152 | tf_op jit(solution)/shard_map/cond/branch_1_fun/all_to_all | solution.py:226
  162.9 1.8 collective-permute-start.5
  164.9 13.3 %collective-permute-start.8 = (bf16[4,32,512]{2,1,0:T(8,128)(2,1)S(1)}, bf16[4,32,512]{2,1,0:T(8,128)(2,1)S(1)}, u32[]{:S(2)}, u32[]{:S(2)}) collective-permute-start(bf16[4,32,512]{2,1,0:T(8,128)(2,1)S(1)} %fusion.17), channel_id=1, source_target_pairs={{0,8},{1,9},{2,10},{3,11},{4,12},{5,13},{6,14},{7,15},{8,0},{9,1},... | collective-permute-start | bytes 393224 | tf_op jit(solution)/shard_map/cond/branch_1_fun/ppermute | solution.py:206
  178.2 7.9 %collective-permute-start.9 = (bf16[4,32,512]{2,1,0:T(8,128)(2,1)S(1)}, bf16[4,32,512]{2,1,0:T(8,128)(2,1)S(1)}, u32[]{:S(2)}, u32[]{:S(2)}) collective-permute-start(bf16[4,32,512]{2,1,0:T(8,128)(2,1)S(1)} %add_convert_fusion.1), channel_id=1, source_target_pairs={{0,4},{1,5},{2,6},{3,7},{4,0},{5,1},{6,2},{7,3},{8,12},{9,13},{10,... | collective-permute-start | bytes 393224 | tf_op jit(solution)/shard_map/cond/branch_1_fun/ppermute | solution.py:206
  186.2 24.4 %collective-permute-start.26 = (bf16[64,2048]{1,0:T(8,128)(2,1)}, bf16[64,2048]{1,0:T(8,128)(2,1)S(1)}, u32[]{:S(2)}, u32[]{:S(2)}) collective-permute-start(bf16[64,2048]{1,0:T(8,128)(2,1)} %get-tuple-element.438), channel_id=1, source_target_pairs={{0,10},{1,11},{2,8},{3,9},{4,14},{5,15},{6,12},{7,13},{8,2},{9,3},... | collective-permute-start | bytes 786440 | tf_op jit(solution)/shard_map/ppermute | solution.py:206
  188.4 22.1 %collective-permute-start.27 = (bf16[64,2048]{1,0:T(8,128)(2,1)}, bf16[64,2048]{1,0:T(8,128)(2,1)S(1)}, u32[]{:S(2)}, u32[]{:S(2)}) collective-permute-start(bf16[64,2048]{1,0:T(8,128)(2,1)} %get-tuple-element.439), channel_id=1, source_target_pairs={{0,14},{1,15},{2,12},{3,13},{4,10},{5,11},{6,8},{7,9},{8,6},{9,7},... | collective-permute-start | bytes 786440 | tf_op jit(solution)/shard_map/ppermute | solution.py:206
  191.2 10.4 %collective-permute-start.2 = (bf16[4,32,512]{2,1,0:T(8,128)(2,1)S(1)}, bf16[4,32,512]{2,1,0:T(8,128)(2,1)S(1)}, u32[]{:S(2)}, u32[]{:S(2)}) collective-permute-start(bf16[4,32,512]{2,1,0:T(8,128)(2,1)S(1)} %get-tuple-element.266.refs_0_), channel_id=1, source_target_pairs={{0,1},{1,0},{2,3},{3,2},{4,5},{5,4},{6,7},{7,6},{8,9},{9,8},{10,11... | collective-permute-start | bytes 393224 | tf_op jit(solution)/shard_map/cond/branch_1_fun/ppermute | solution.py:209
  191.3 16.2 %collective-permute-start.3 = (bf16[4,32,512]{2,1,0:T(8,128)(2,1)S(1)}, bf16[4,32,512]{2,1,0:T(8,128)(2,1)S(1)}, u32[]{:S(2)}, u32[]{:S(2)}) collective-permute-start(bf16[4,32,512]{2,1,0:T(8,128)(2,1)S(1)} %get-tuple-element.266.refs_0_), channel_id=1, source_target_pairs={{0,2},{1,3},{2,0},{3,1},{4,6},{5,7},{6,4},{7,5},{8,10},{9,11},{10,... | collective-permute-start | bytes 393224 | tf_op jit(solution)/shard_map/cond/branch_1_fun/ppermute | solution.py:209
  192.4 17.4 %collective-permute-start.4 = (bf16[4,32,512]{2,1,0:T(8,128)(2,1)S(1)}, bf16[4,32,512]{2,1,0:T(8,128)(2,1)S(1)}, u32[]{:S(2)}, u32[]{:S(2)}) collective-permute-start(bf16[4,32,512]{2,1,0:T(8,128)(2,1)S(1)} %get-tuple-element.266.refs_0_), channel_id=1, source_target_pairs={{0,3},{1,2},{2,1},{3,0},{4,7},{5,6},{6,5},{7,4},{8,11},{9,10},{10,... | collective-permute-start | bytes 393224 | tf_op jit(solution)/shard_map/cond/branch_1_fun/ppermute | solution.py:209
  193.2 3.8 %copy-start.3 = (bf16[512,512]{1,0:T(8,128)(2,1)S(1)}, bf16[512,512]{1,0:T(8,128)(2,1)}, u32[]{:S(2)}) copy-start(bf16[512,512]{1,0:T(8,128)(2,1)} %get-tuple-element.267.matrix) | copy-start | bytes 1572868 | tf_op jit(solution)/shard_map/cond
  210.5 1.1 copy-start.4

commit v8 on v7

--- a/solution.py
+++ b/solution.py
@@ -10,7 +10,7 @@
 
 F32 = jnp.float32
 BF16 = jnp.bfloat16
-COLUMNS = 512
+COLUMNS = 1024
 LIMIT = pltpu.CompilerParams(vmem_limit_bytes=40 * 1024 * 1024)
 
 
@@ -378,11 +378,9 @@
         return total
 
     def finish(got, position, backs, home_factor, cotangent, starts, slabs):
-        rows = in_order(
-            position,
-            [got] + [near(got, i) for i in (1, 2, 3)],
-            1.0 / math.sqrt(count * width),
-        )
+        parts = [got, near(got, 2)]
+        parts += [sibling(x) for x in parts]
+        rows = in_order(position, parts, 1.0 / math.sqrt(count * width))
         grad_signal = by_columns(
             whole_kernel, backs, [block], width, (), [home_factor], result=True
         )[0]
@@ -399,8 +397,8 @@
             grad_gate = place(jnp.zeros_like(cotangent), starts, slabs)
         return rows.reshape(block, block), grad_signal, grad_gate
 
-    k = every % far * 2 + every // far // 2
-    position = jnp.bitwise_xor(h, k) * 2 + jnp.bitwise_xor(e, every // far % 2)
+    k = every % far * 2 + every // far % 2
+    position = jnp.bitwise_xor(h, k) * 2 + jnp.bitwise_xor(e, every // chips)
     grad_block, grad_signal, grad_gate = phase(
         finish,
         own,

time: 214 us -> 212 us (level)
  Pallas kernels: 43.2 us -> 33.9 us
  waiting for transfers between devices: 60.1 us -> 67 us
    pallas_call x11, Pallas kernels: 41 us -> 31.8 us  [by_columns(): pl.pallas_call(kernel, grid=(width // columns,), in_specs=[pl.BlockSpec(m...]
    ppermute x18, waiting for transfers between devices: 15.4 us -> 23.9 us  [chip(): return lax.ppermute(x, 'seq', [(s, s ^ 2 * k) for s in range(count)])]
    ppermute x10, waiting for transfers between devices: 11.5 us -> 4.24 us  [near(): return lax.ppermute(x, 'seq', [(s, s ^ i) for s in range(count)])]
    all_to_all x3, waiting for transfers between devices: 33.2 us -> 38.9 us  [send_side(): lax.all_to_all(x, 'seq', split_axis=0, concat_axis=0, tiled=True, axis_in...]
  transfers between devices with their start and end apart: 31 -> 31, of which waited for: 9 -> 9; matrix products, arithmetic and copies ran while one was open for 10% -> 10% of each run, Pallas kernels for 20% -> 16%
where the time goes in v8:
time: 212 us; the launch traced here: 208 us
  waiting for transfers between devices  67 us (32%)
  starting transfers between devices  56.5 us (27%)
  Pallas kernels  33.9 us (16%)
  blocking collectives  25.4 us (12%)
  matrix products  9.66 us (5%)
  local copies, waits for them, and re-layouts  7.15 us (3%)
  other arithmetic  6.71 us (3%)
    ppermute x18, starting transfers between devices, chip(): return lax.ppermute(x, 'seq', [(s, s ^ 2 * k) for s in range(count)])  39.1 us
    all_to_all x3, waiting for transfers between devices, send_side(): lax.all_to_all(x, 'seq', split_axis=0, concat_axis=0, tiled=True, axis_in...  38.9 us
    pallas_call x11, Pallas kernels, by_columns(): pl.pallas_call(kernel, grid=(width // columns,), in_specs=[pl.BlockSpec(m...  31.8 us
    all_to_all x1, blocking collectives, send_side(): lax.all_to_all(x, 'seq', split_axis=0, concat_axis=0, tiled=True, axis_in...  25.4 us
    ppermute x18, waiting for transfers between devices, chip(): return lax.ppermute(x, 'seq', [(s, s ^ 2 * k) for s in range(count)])  23.9 us
    all_to_all x3, starting transfers between devices, send_side(): lax.all_to_all(x, 'seq', split_axis=0, concat_axis=0, tiled=True, axis_in...  12.7 us
    ppermute x10, starting transfers between devices, near(): return lax.ppermute(x, 'seq', [(s, s ^ i) for s in range(count)])  4.64 us
    ppermute x10, waiting for transfers between devices, near(): return lax.ppermute(x, 'seq', [(s, s ^ i) for s in range(count)])  4.24 us
  transfers between devices with their start and end apart: 31, of which 9 were waited for; matrix products, arithmetic and copies ran while one was open for 10% of the time, Pallas kernels for 16%

profile of v8, /device:TPU:0, one launch (start us, length us, event | category | flops | bytes accessed | tf_op | source)
XLA Modules:
  0.0 208.3 jit_solution(8320959328129004785)
XLA Ops:
  0.7 2.7 %dynamic-slice_multiply_fusion.1 = (bf16[64,2048]{1,0:T(8,128)(2,1)}, bf16[64,2048]{1,0:T(8,128)(2,1)}, bf16[64,2048]{1,0:T(8,128)(2,1)}, bf16[64,2048]{1,0:T(8,128)(2,1)}) fusion(bf16[512,2048]{1,0:T(8,128)(2,1)} %param.19, s32[]{:T(128)S(6)} %select_n.107, bf16[512,2048]{1,0:T(8,128)(2,1)} %a.3, s32[]{:T(128)S(6)} %select_n.106, s32[]{:T(128)S(6)} %select_n.105, ...), kind=kLoop, calls=%fused_computation.54 | loop fusion | flops 2097152 | bytes 3145744 | tf_op jit(solution)/shard_map/mul | solution.py:251
  3.4 4.0 %collective-permute-start.12 = (bf16[64,2048]{1,0:T(8,128)(2,1)}, bf16[64,2048]{1,0:T(8,128)(2,1)}, u32[]{:S(2)}, u32[]{:S(2)}) collective-permute-start(bf16[64,2048]{1,0:T(8,128)(2,1)} %get-tuple-element.349), channel_id=1, source_target_pairs={{0,8},{1,9},{2,10},{3,11},{4,12},{5,13},{6,14},{7,15},{8,0},{9,1},... | collective-permute-start | bytes 786440 | tf_op jit(solution)/shard_map/ppermute | solution.py:206
  7.4 1.3 collective-permute-start.13
  8.7 3.6 %collective-permute-start.14 = (bf16[64,2048]{1,0:T(8,128)(2,1)}, bf16[64,2048]{1,0:T(8,128)(2,1)}, u32[]{:S(2)}, u32[]{:S(2)}) collective-permute-start(bf16[64,2048]{1,0:T(8,128)(2,1)} %get-tuple-element.351), channel_id=1, source_target_pairs={{0,12},{1,13},{2,14},{3,15},{4,8},{5,9},{6,10},{7,11},{8,4},{9,5},... | collective-permute-start | bytes 786440 | tf_op jit(solution)/shard_map/ppermute | solution.py:206
  13.8 17.7 %conditional.6 = (bf16[256,2048]{1,0:T(8,128)(2,1)}, bf16[64,2048]{1,0:T(8,128)(2,1)}, bf16[64,2048]{1,0:T(8,128)(2,1)}, bf16[64,2048]{1,0:T(8,128)(2,1)}, bf16[...) conditional(s32[]{:T(128)} %bitcast.23, () %tuple.69, ...), branch_computations={%region_0.1_spmd, %region_1.2_spmd} | conditional | flops 1622943488 | bytes 8787936 | solution.py:203
  14.0 1.6 convolution_convert_fusion.2.matrix
  15.7 4.2 %convolution_convert_fusion.rows = bf16[512,2048]{1,0:T(8,128)(2,1)} fusion(bf16[512,2048]{1,0:T(8,128)(2,1)} %get-tuple-element.172, s32[512]{0:T(512)S(1)} %get-tuple-element.171), kind=kOutput, calls=%fused_computation | convolution fusion | flops 1075052544 | bytes 4196352 | tf_op jit(solution)/shard_map/cond/branch_1_fun/dot_general | solution.py:269
  19.9 3.6 %branch_1_fun.12 = (bf16[256,2048]{1,0:T(8,128)(2,1)}, bf16[64,2048]{1,0:T(8,128)(2,1)}, bf16[64,2048]{1,0:T(8,128)(2,1)}, bf16[64,2048]{1,0:T(8,128)(2,1)}, bf16[64,2048]{1,0:T(8,128)(2,1)}) custom-call(bf16[512,512]{1,0:T(8,128)(2,1)S(1)} %convolution_convert_fusion.2.matrix, bf16[512,2048]{1,0:T(8,128)(2,1)} %convolution_convert_fusion.rows), custom_call_target="tpu_custom_call" | custom-call | tf_op jit(solution)/shard_map/cond/branch_1_fun/pallas_call | solution.py:159
  24.2 1.4 broadcast_in_dim.2
  25.9 2.0 fusion
  28.0 1.9 copy.54
  32.5 1.6 dynamic-slice_multiply_fusion
  34.2 25.4 %conditional.7 = (bf16[256,2048]{1,0:T(8,128)(2,1)S(1)}) conditional(s32[]{:T(128)} %bitcast.23, () %tuple.72, bf16[256,2048]{1,0:T(8,128)(2,1)S(1)} %dynamic-slice_multiply_fusion), branch_computations={%region_2.3_spmd, %region_3.4_spmd} | conditional | bytes 2097160 | solution.py:203
  34.2 25.4 %all_to_all.36 = bf16[4,64,2048]{2,1,0:T(8,128)(2,1)S(1)} all-to-all(bf16[4,64,2048]{2,1,0:T(8,128)(2,1)S(1)} %bitcast.68), channel_id=1, replica_groups={{0,2,4,6},{1,3,5,7},{8,10,12,14},{9,11,13,15},{16,18,20,22},{17,19,21,2..., dimensions={0} | all-to-all | bytes 2097152 | tf_op jit(solution)/shard_map/cond/branch_1_fun/all_to_all | solution.py:226
  59.6 3.1 %collective-permute-start.17 = (bf16[64,2048]{1,0:T(8,128)(2,1)}, bf16[64,2048]{1,0:T(8,128)(2,1)S(1)}, u32[]{:S(2)}, u32[]{:S(2)}) collective-permute-start(bf16[64,2048]{1,0:T(8,128)(2,1)} %get-tuple-element.366), channel_id=1, source_target_pairs={{0,10},{1,11},{2,8},{3,9},{4,14},{5,15},{6,12},{7,13},{8,2},{9,3},... | collective-permute-start | bytes 786440 | tf_op jit(solution)/shard_map/ppermute | solution.py:206
  63.7 3.8 %collective-permute-start.19 = (bf16[64,2048]{1,0:T(8,128)(2,1)}, bf16[64,2048]{1,0:T(8,128)(2,1)}, u32[]{:S(2)}, u32[]{:S(2)}) collective-permute-start(bf16[64,2048]{1,0:T(8,128)(2,1)} %get-tuple-element.368), channel_id=1, source_target_pairs={{0,14},{1,15},{2,12},{3,13},{4,10},{5,11},{6,8},{7,9},{8,6},{9,7},... | collective-permute-start | bytes 786440 | tf_op jit(solution)/shard_map/ppermute | solution.py:206
  67.5 30.9 %conditional.8 = (bf16[256,2048]{1,0:T(8,128)(2,1)}, bf16[256,2048]{1,0:T(8,128)(2,1)}, bf16[64,2048]{1,0:T(8,128)(2,1)}, bf16[64,2048]{1,0:T(8,128)(2,1)}, bf16...) conditional(s32[]{:T(128)} %bitcast.23, () %tuple.67, ...), branch_computations={%region_4.5_spmd, %region_5.6_spmd} | conditional | bytes 12583088 | solution.py:203
  67.5 2.2 %branch_1_fun.13 = (bf16[256,2048]{1,0:T(8,128)(2,1)}, bf16[256,2048]{1,0:T(8,128)(2,1)S(1)}) custom-call(s32[1]{0:T(128)} %get-tuple-element.183.core, bf16[256,2048]{1,0:T(8,128)(2,1)S(1)} %get-tuple-element.185.refs_0_, bf16[64,2048]{1,0:T(8,128)(2,1)} %get-tuple-element.186.refs_1_, bf16[64,2048]{1,0:T(8,128)(2,1)} %get-tuple-element.187.refs_2_, ...), custom_call_target="tpu_custom_call" | custom-call | tf_op jit(solution)/shard_map/cond/branch_1_fun/pallas_call | solution.py:159
  69.7 4.2 %all-to-all-start.1 = ((bf16[4,64,2048]{2,1,0:T(8,128)(2,1)}), bf16[4,64,2048]{2,1,0:T(8,128)(2,1)}, u32[]{:S(2)}, u32[]{:S(2)}) async-start(bf16[4,64,2048]{2,1,0:T(8,128)(2,1)} %bitcast.5), calls=%async_computation.1 | async-start | bytes 2097152 | tf_op jit(solution)/shard_map/cond/branch_1_fun/all_to_all | solution.py:226
  74.0 1.3 copy.19.matrix
  75.3 2.8 %branch_1_fun.14 = (bf16[256,2048]{1,0:T(8,128)(2,1)S(1)}, bf16[256,2048]{1,0:T(8,128)(2,1)S(1)}) custom-call(bf16[512,512]{1,0:T(8,128)(2,1)S(1)} %copy.19.matrix, bf16[256,2048]{1,0:T(8,128)(2,1)} %get-tuple-element.554.own, bf16[256,2048]{1,0:T(8,128)(2,1)} %collective-permute-done.other), custom_call_target="tpu_custom_call" | custom-call | tf_op jit(solution)/shard_map/cond/branch_1_fun/pallas_call | solution.py:159
  78.6 2.3 %collective-permute-done.1.other = bf16[256,2048]{1,0:T(8,128)(2,1)S(1)} collective-permute-done((bf16[256,2048]{1,0:T(8,128)(2,1)S(1)}, bf16[256,2048]{1,0:T(8,128)(2,1)S(1)}, u32[]{:S(2)}, u32[]{:S(2)}) %collective-permute-start.1) | collective-permute-done | bytes 1048608 | tf_op jit(solution)/shard_map/cond/branch_1_fun/ppermute | solution.py:209
  80.9 1.6 branch_1_fun.15
  82.5 15.9 %all-to-all-done.1 = bf16[4,64,2048]{2,1,0:T(8,128)(2,1)} async-done(((bf16[4,64,2048]{2,1,0:T(8,128)(2,1)}), bf16[4,64,2048]{2,1,0:T(8,128)(2,1)}, u32[]{:S(2)}, u32[]{:S(2)}) %all-to-all-start.1) | async-done | bytes 1048608 | tf_op jit(solution)/shard_map/cond/branch_1_fun/all_to_all | solution.py:226
  98.4 3.7 %collective-permute-start.20 = (bf16[64,2048]{1,0:T(8,128)(2,1)}, bf16[64,2048]{1,0:T(8,128)(2,1)}, u32[]{:S(2)}, u32[]{:S(2)}) collective-permute-start(bf16[64,2048]{1,0:T(8,128)(2,1)} %get-tuple-element.370), channel_id=1, source_target_pairs={{0,8},{1,9},{2,10},{3,11},{4,12},{5,13},{6,14},{7,15},{8,0},{9,1},... | collective-permute-start | bytes 786440 | tf_op jit(solution)/shard_map/ppermute | solution.py:206
  102.4 3.5 %collective-permute-start.22 = (bf16[64,2048]{1,0:T(8,128)(2,1)}, bf16[64,2048]{1,0:T(8,128)(2,1)}, u32[]{:S(2)}, u32[]{:S(2)}) collective-permute-start(bf16[64,2048]{1,0:T(8,128)(2,1)} %get-tuple-element.372), channel_id=1, source_target_pairs={{0,12},{1,13},{2,14},{3,15},{4,8},{5,9},{6,10},{7,11},{8,4},{9,5},... | collective-permute-start | bytes 786440 | tf_op jit(solution)/shard_map/ppermute | solution.py:206
  106.8 41.4 %conditional.9 = (bf16[256,2048]{1,0:T(8,128)(2,1)}, bf16[256,2048]{1,0:T(8,128)(2,1)}, bf16[64,2048]{1,0:T(8,128)(2,1)}, bf16[64,2048]{1,0:T(8,128)(2,1)}, bf16...) conditional(s32[]{:T(128)} %bitcast.23, () %tuple.76, ...), branch_computations={%region_6.7_spmd, %region_7.8_spmd} | conditional | flops 1843200 | bytes 14615264 | solution.py:203
  107.6 1.7 branch_1_fun.16
  109.4 4.2 %all-to-all-start.3 = ((bf16[4,64,2048]{2,1,0:T(8,128)(2,1)}), bf16[4,64,2048]{2,1,0:T(8,128)(2,1)}, u32[]{:S(2)}, u32[]{:S(2)}) async-start(bf16[4,64,2048]{2,1,0:T(8,128)(2,1)} %bitcast.69), calls=%async_computation.3 | async-start | bytes 2097152 | tf_op jit(solution)/shard_map/cond/branch_1_fun/all_to_all | solution.py:226
  113.7 3.4 %branch_1_fun.17 = (bf16[256,2048]{1,0:T(8,128)(2,1)S(1)}, bf16[256,2048]{1,0:T(8,128)(2,1)}) custom-call(bf16[512,512]{1,0:T(8,128)(2,1)} %get-tuple-element.201.matrix, bf16[256,2048]{1,0:T(8,128)(2,1)S(1)} %get-tuple-element.207.own.refs_2_, bf16[256,2048]{1,0:T(8,128)(2,1)S(1)} %collective-permute-done.10.other.refs_3_), custom_call_target="tpu_custom_call" | custom-call | tf_op jit(solution)/shard_map/cond/branch_1_fun/pallas_call | solution.py:159
  117.8 4.0 %branch_1_fun.19 = f32[512,16]{1,0:T(8,128)S(1)} custom-call(bf16[512,512]{1,0:T(8,128)(2,1)S(1)} %convert_element_type.67.same, bf16[512,16]{1,0:T(8,128)(2,1)} %get-tuple-element.217.spread_out, bf16[256,2048]{1,0:T(8,128)(2,1)} %get-tuple-element.218.refs_0_, bf16[256,2048]{1,0:T(8,128)(2,1)} %get-tuple-element.219.refs_1_, ...), custom_call_target="tpu_custom_call" | custom-call | tf_op jit(solution)/shard_map/cond/branch_1_fun/pallas_call | solution.py:159
  122.8 2.5 %branch_1_fun.18 = (bf16[256,2048]{1,0:T(8,128)(2,1)}, bf16[64,2048]{1,0:T(8,128)(2,1)}, bf16[64,2048]{1,0:T(8,128)(2,1)}, bf16[64,2048]{1,0:T(8,128)(2,1)}, bf16[64,2048]{1,0:T(8,128)(2,1)}) custom-call(s32[1]{0:T(128)} %get-tuple-element.200.core, bf16[256,2048]{1,0:T(8,128)(2,1)S(1)} %get-tuple-element.209.own, ...), custom_call_target="tpu_custom_call" | custom-call | tf_op jit(solution)/shard_map/cond/branch_1_fun/pallas_call | solution.py:159
  125.3 22.9 %all-to-all-done.3 = bf16[4,64,2048]{2,1,0:T(8,128)(2,1)} async-done(((bf16[4,64,2048]{2,1,0:T(8,128)(2,1)}), bf16[4,64,2048]{2,1,0:T(8,128)(2,1)}, u32[]{:S(2)}, u32[]{:S(2)}) %all-to-all-start.3) | async-done | bytes 1048608 | tf_op jit(solution)/shard_map/cond/branch_1_fun/all_to_all | solution.py:226
  148.3 2.6 %collective-permute-start.24 = (bf16[64,2048]{1,0:T(8,128)(2,1)}, bf16[64,2048]{1,0:T(8,128)(2,1)}, u32[]{:S(2)}, u32[]{:S(2)}) collective-permute-start(bf16[64,2048]{1,0:T(8,128)(2,1)} %get-tuple-element.402), channel_id=1, source_target_pairs={{0,8},{1,9},{2,10},{3,11},{4,12},{5,13},{6,14},{7,15},{8,0},{9,1},... | collective-permute-start | bytes 786440 | tf_op jit(solution)/shard_map/ppermute | solution.py:206
  151.3 33.9 %conditional.10 = (bf16[4,32,512]{2,1,0:T(8,128)(2,1)S(1)}, bf16[256,2048]{1,0:T(8,128)(2,1)}) conditional(s32[]{:T(128)} %bitcast.23, () %tuple.79, (s32[8]{0:T(128)S(1)}, bf16[512,512]{1,0:T(8,128)(2,1)}, bf16[512,2048]{1,0:T(8,128)(2,1)}, bf16[256,2048]{1,0:T(8,128)(2,1)}, bf16[64,2048]{1,0:T(8,128)(2,1)}, /*index=5*/bf16[64,2048]{1,0:T(8,128)(2,1)}, ...), branch_computations={%region_8.9_spmd, %region_9.10_spmd} | conditional | flops 1245195 | bytes 10223992 | solution.py:203
  151.3 3.7 %branch_1_fun.20 = f32[512,512]{1,0:T(8,128)S(1)} custom-call(s32[4]{0:T(128)S(1)} %slice_multiply_fusion.starts, bf16[512,512]{1,0:T(8,128)(2,1)} %get-tuple-element.222.order, bf16[512,2048]{1,0:T(8,128)(2,1)} %get-tuple-element.223.right, bf16[256,2048]{1,0:T(8,128)(2,1)} %get-tuple-element.224.side, bf16[64,2048]{1,0:T(8,128)(2,1)} %get-tuple-element.225.refs_0_, ...), custom_call_target="tpu_custom_call" | custom-call | tf_op jit(solution)/shard_map/cond/branch_1_fun/pallas_call | solution.py:159
  155.8 1.4 collective-permute-start.6
  157.2 4.2 %all-to-all-start.2 = ((bf16[4,64,2048]{2,1,0:T(8,128)(2,1)}), bf16[4,64,2048]{2,1,0:T(8,128)(2,1)}, u32[]{:S(2)}, u32[]{:S(2)}) async-start(bf16[4,64,2048]{2,1,0:T(8,128)(2,1)} %bitcast.17), calls=%async_computation.2 | async-start | bytes 2097152 | tf_op jit(solution)/shard_map/cond/branch_1_fun/all_to_all | solution.py:226
  163.4 1.5 collective-permute-start.8
  164.9 12.0 %collective-permute-done.8 = bf16[4,32,512]{2,1,0:T(8,128)(2,1)S(1)} collective-permute-done((bf16[4,32,512]{2,1,0:T(8,128)(2,1)S(1)}, bf16[4,32,512]{2,1,0:T(8,128)(2,1)S(1)}, u32[]{:S(2)}, u32[]{:S(2)}) %collective-permute-start.8) | collective-permute-done | bytes 131104 | tf_op jit(solution)/shard_map/cond/branch_1_fun/ppermute | solution.py:206
  176.9 3.9 %collective-permute-start.9 = (bf16[4,32,512]{2,1,0:T(8,128)(2,1)S(1)}, bf16[4,32,512]{2,1,0:T(8,128)(2,1)S(1)}, u32[]{:S(2)}, u32[]{:S(2)}) collective-permute-start(bf16[4,32,512]{2,1,0:T(8,128)(2,1)S(1)} %add_convert_fusion.1), channel_id=1, source_target_pairs={{0,4},{1,5},{2,6},{3,7},{4,0},{5,1},{6,2},{7,3},{8,12},{9,13},{10,... | collective-permute-start | bytes 393224 | tf_op jit(solution)/shard_map/cond/branch_1_fun/ppermute | solution.py:206
  180.9 4.3 %collective-permute-done.9 = bf16[4,32,512]{2,1,0:T(8,128)(2,1)S(1)} collective-permute-done((bf16[4,32,512]{2,1,0:T(8,128)(2,1)S(1)}, bf16[4,32,512]{2,1,0:T(8,128)(2,1)S(1)}, u32[]{:S(2)}, u32[]{:S(2)}) %collective-permute-start.9) | collective-permute-done | bytes 131104 | tf_op jit(solution)/shard_map/cond/branch_1_fun/ppermute | solution.py:206
  185.3 2.3 %collective-permute-start.26 = (bf16[64,2048]{1,0:T(8,128)(2,1)}, bf16[64,2048]{1,0:T(8,128)(2,1)S(1)}, u32[]{:S(2)}, u32[]{:S(2)}) collective-permute-start(bf16[64,2048]{1,0:T(8,128)(2,1)} %get-tuple-element.410), channel_id=1, source_target_pairs={{0,10},{1,11},{2,8},{3,9},{4,14},{5,15},{6,12},{7,13},{8,2},{9,3},... | collective-permute-start | bytes 786440 | tf_op jit(solution)/shard_map/ppermute | solution.py:206
  187.6 2.2 %collective-permute-start.27 = (bf16[64,2048]{1,0:T(8,128)(2,1)}, bf16[64,2048]{1,0:T(8,128)(2,1)S(1)}, u32[]{:S(2)}, u32[]{:S(2)}) collective-permute-start(bf16[64,2048]{1,0:T(8,128)(2,1)} %get-tuple-element.411), channel_id=1, source_target_pairs={{0,14},{1,15},{2,12},{3,13},{4,10},{5,11},{6,8},{7,9},{8,6},{9,7},... | collective-permute-start | bytes 786440 | tf_op jit(solution)/shard_map/ppermute | solution.py:206
  189.9 9.3 %conditional.11 = (f32[512,512]{1,0:T(8,128)S(1)}, bf16[512,2048]{1,0:T(8,128)(2,1)}, bf16[512,2048]{1,0:T(8,128)(2,1)}) conditional(s32[]{:T(128)} %bitcast.23, () %tuple.66, (s32[]{:T(128)}, s32[16]{0:T(128)S(1)}, s32[16]{0:T(128)S(1)}, pred[16]{0:T(512)(128)(4,1)S(1)}, s32[16]{0:T(128)S(1)}, /*index=5*/s32[16]{0:T(128)S(1)}, s32[16]{0:T(128)S(1)}, ...), branch_computations={%region_10.11_spmd, %region_11.12_spmd} | conditional | flops 438 | bytes 5242912 | solution.py:203
  190.8 2.6 %branch_1_fun.23 = bf16[512,2048]{1,0:T(8,128)(2,1)} custom-call(s32[3]{0:T(128)S(1)} %pad_add_fusion.starts, bf16[512,2048]{1,0:T(8,128)(2,1)S(1)} %get-tuple-element.248.a, bf16[256,2048]{1,0:T(8,128)(2,1)} %get-tuple-element.249.refs_0_, bf16[64,2048]{1,0:T(8,128)(2,1)} %get-tuple-element.250.refs_1_, bf16[64,2048]{1,0:T(8,128)(2,1)} %get-tuple-element.251.refs_2_), custom_call_target="tpu_custom_call" | custom-call | tf_op jit(solution)/shard_map/cond/branch_1_fun/pallas_call | solution.py:159
  193.4 3.7 %branch_1_fun.22 = bf16[512,2048]{1,0:T(8,128)(2,1)} custom-call(bf16[512,512]{1,0:T(8,128)(2,1)S(1)} %copy-done.3, bf16[256,2048]{1,0:T(8,128)(2,1)} %get-tuple-element.240.refs_0_, bf16[64,2048]{1,0:T(8,128)(2,1)} %get-tuple-element.241.refs_1_, bf16[64,2048]{1,0:T(8,128)(2,1)} %get-tuple-element.242.refs_2_, bf16[64,2048]{1,0:T(8,128)(2,1)} %get-tuple-element.243.refs_3_, ...), custom_call_target="tpu_custom_call" | custom-call | tf_op jit(solution)/shard_map/cond/branch_1_fun/pallas_call | solution.py:159
  199.2 7.6 %collective-permute-done.26.slab = bf16[64,2048]{1,0:T(8,128)(2,1)S(1)} collective-permute-done((bf16[64,2048]{1,0:T(8,128)(2,1)}, bf16[64,2048]{1,0:T(8,128)(2,1)S(1)}, u32[]{:S(2)}, u32[]{:S(2)}) %collective-permute-start.26) | collective-permute-done | bytes 262176 | tf_op jit(solution)/shard_map/ppermute | solution.py:206
  (107 shorter events, 17.8 us)
Async XLA Ops:
  0.6 12.0 %copy-start.9 = (s32[512]{0:T(512)S(1)}, s32[512]{0:T(512)}, u32[]{:S(2)}) copy-start(s32[512]{0:T(512)} %param.23) | copy-start | bytes 6148
  0.6 13.2 %copy-start.8 = (bf16[32,16,16]{0,2,1:T(8,128)(2,1)S(1)}, bf16[32,16,16]{0,2,1:T(8,128)(2,1)}, u32[]{:S(2)}) copy-start(bf16[32,16,16]{0,2,1:T(8,128)(2,1)} %param.22) | copy-start | bytes 49156
  3.4 56.2 %collective-permute-start.12 = (bf16[64,2048]{1,0:T(8,128)(2,1)}, bf16[64,2048]{1,0:T(8,128)(2,1)}, u32[]{:S(2)}, u32[]{:S(2)}) collective-permute-start(bf16[64,2048]{1,0:T(8,128)(2,1)} %get-tuple-element.349), channel_id=1, source_target_pairs={{0,8},{1,9},{2,10},{3,11},{4,12},{5,13},{6,14},{7,15},{8,0},{9,1},... | collective-permute-start | bytes 786440 | tf_op jit(solution)/shard_map/ppermute | solution.py:206
  7.4 52.1 %collective-permute-start.13 = (bf16[64,2048]{1,0:T(8,128)(2,1)}, bf16[64,2048]{1,0:T(8,128)(2,1)}, u32[]{:S(2)}, u32[]{:S(2)}) collective-permute-start(bf16[64,2048]{1,0:T(8,128)(2,1)} %get-tuple-element.350), channel_id=1, source_target_pairs={{0,10},{1,11},{2,8},{3,9},{4,14},{5,15},{6,12},{7,13},{8,2},{9,3},... | collective-permute-start | bytes 786440 | tf_op jit(solution)/shard_map/ppermute | solution.py:206
  8.7 50.8 %collective-permute-start.14 = (bf16[64,2048]{1,0:T(8,128)(2,1)}, bf16[64,2048]{1,0:T(8,128)(2,1)}, u32[]{:S(2)}, u32[]{:S(2)}) collective-permute-start(bf16[64,2048]{1,0:T(8,128)(2,1)} %get-tuple-element.351), channel_id=1, source_target_pairs={{0,12},{1,13},{2,14},{3,15},{4,8},{5,9},{6,10},{7,11},{8,4},{9,5},... | collective-permute-start | bytes 786440 | tf_op jit(solution)/shard_map/ppermute | solution.py:206
  12.3 47.3 %collective-permute-start.15 = (bf16[64,2048]{1,0:T(8,128)(2,1)}, bf16[64,2048]{1,0:T(8,128)(2,1)}, u32[]{:S(2)}, u32[]{:S(2)}) collective-permute-start(bf16[64,2048]{1,0:T(8,128)(2,1)} %get-tuple-element.352), channel_id=1, source_target_pairs={{0,14},{1,15},{2,12},{3,13},{4,10},{5,11},{6,8},{7,9},{8,6},{9,7},... | collective-permute-start | bytes 786440 | tf_op jit(solution)/shard_map/ppermute | solution.py:206
  13.8 18.7 %copy-start = (bf16[512,2048]{1,0:T(8,128)(2,1)S(1)}, bf16[512,2048]{1,0:T(8,128)(2,1)}, u32[]{:S(2)}) copy-start(bf16[512,2048]{1,0:T(8,128)(2,1)} %a.3) | copy-start | bytes 6291460
  31.6 2.6 %copy-start.2 = (bf16[512,512]{1,0:T(8,128)(2,1)}, bf16[512,512]{1,0:T(8,128)(2,1)S(1)}, u32[]{:S(2)}) copy-start(bf16[512,512]{1,0:T(8,128)(2,1)S(1)} %get-tuple-element.405) | copy-start | bytes 1572868
  31.6 66.8 %collective-permute-start.16 = (bf16[64,2048]{1,0:T(8,128)(2,1)}, bf16[64,2048]{1,0:T(8,128)(2,1)S(1)}, u32[]{:S(2)}, u32[]{:S(2)}) collective-permute-start(bf16[64,2048]{1,0:T(8,128)(2,1)} %get-tuple-element.341), channel_id=1, source_target_pairs={{0,8},{1,9},{2,10},{3,11},{4,12},{5,13},{6,14},{7,15},{8,0},{9,1},... | collective-permute-start | bytes 786440 | tf_op jit(solution)/shard_map/ppermute | solution.py:206
  59.6 38.8 %collective-permute-start.17 = (bf16[64,2048]{1,0:T(8,128)(2,1)}, bf16[64,2048]{1,0:T(8,128)(2,1)S(1)}, u32[]{:S(2)}, u32[]{:S(2)}) collective-permute-start(bf16[64,2048]{1,0:T(8,128)(2,1)} %get-tuple-element.366), channel_id=1, source_target_pairs={{0,10},{1,11},{2,8},{3,9},{4,14},{5,15},{6,12},{7,13},{8,2},{9,3},... | collective-permute-start | bytes 786440 | tf_op jit(solution)/shard_map/ppermute | solution.py:206
  62.7 35.7 %collective-permute-start.18 = (bf16[64,2048]{1,0:T(8,128)(2,1)}, bf16[64,2048]{1,0:T(8,128)(2,1)}, u32[]{:S(2)}, u32[]{:S(2)}) collective-permute-start(bf16[64,2048]{1,0:T(8,128)(2,1)} %get-tuple-element.367), channel_id=1, source_target_pairs={{0,12},{1,13},{2,14},{3,15},{4,8},{5,9},{6,10},{7,11},{8,4},{9,5},... | collective-permute-start | bytes 786440 | tf_op jit(solution)/shard_map/ppermute | solution.py:206
  63.7 34.7 %collective-permute-start.19 = (bf16[64,2048]{1,0:T(8,128)(2,1)}, bf16[64,2048]{1,0:T(8,128)(2,1)}, u32[]{:S(2)}, u32[]{:S(2)}) collective-permute-start(bf16[64,2048]{1,0:T(8,128)(2,1)} %get-tuple-element.368), channel_id=1, source_target_pairs={{0,14},{1,15},{2,12},{3,13},{4,10},{5,11},{6,8},{7,9},{8,6},{9,7},... | collective-permute-start | bytes 786440 | tf_op jit(solution)/shard_map/ppermute | solution.py:206
  69.7 5.5 %collective-permute-start = (bf16[256,2048]{1,0:T(8,128)(2,1)S(1)}, bf16[256,2048]{1,0:T(8,128)(2,1)}, u32[]{:S(2)}, u32[]{:S(2)}) collective-permute-start(bf16[256,2048]{1,0:T(8,128)(2,1)S(1)} %get-tuple-element.191), channel_id=1, source_target_pairs={{0,1},{1,0},{2,3},{3,2},{4,5},{5,4},{6,7},{7,6},{8,9},{9,8},{10,11... | collective-permute-start | bytes 3145736 | tf_op jit(solution)/shard_map/cond/branch_1_fun/ppermute | solution.py:209
  69.7 28.7 %all-to-all-start.1 = ((bf16[4,64,2048]{2,1,0:T(8,128)(2,1)}), bf16[4,64,2048]{2,1,0:T(8,128)(2,1)}, u32[]{:S(2)}, u32[]{:S(2)}) async-start(bf16[4,64,2048]{2,1,0:T(8,128)(2,1)} %bitcast.5), calls=%async_computation.1 | async-start | bytes 2097152 | tf_op jit(solution)/shard_map/cond/branch_1_fun/all_to_all | solution.py:226
  78.0 2.9 %collective-permute-start.1 = (bf16[256,2048]{1,0:T(8,128)(2,1)S(1)}, bf16[256,2048]{1,0:T(8,128)(2,1)S(1)}, u32[]{:S(2)}, u32[]{:S(2)}) collective-permute-start(bf16[256,2048]{1,0:T(8,128)(2,1)S(1)} %get-tuple-element.193), channel_id=1, source_target_pairs={{0,1},{1,0},{2,3},{3,2},{4,5},{5,4},{6,7},{7,6},{8,9},{9,8},{10,11... | collective-permute-start | bytes 3145736 | tf_op jit(solution)/shard_map/cond/branch_1_fun/ppermute | solution.py:209
  98.4 49.8 %collective-permute-start.20 = (bf16[64,2048]{1,0:T(8,128)(2,1)}, bf16[64,2048]{1,0:T(8,128)(2,1)}, u32[]{:S(2)}, u32[]{:S(2)}) collective-permute-start(bf16[64,2048]{1,0:T(8,128)(2,1)} %get-tuple-element.370), channel_id=1, source_target_pairs={{0,8},{1,9},{2,10},{3,11},{4,12},{5,13},{6,14},{7,15},{8,0},{9,1},... | collective-permute-start | bytes 786440 | tf_op jit(solution)/shard_map/ppermute | solution.py:206
  102.1 46.2 %collective-permute-start.21 = (bf16[64,2048]{1,0:T(8,128)(2,1)}, bf16[64,2048]{1,0:T(8,128)(2,1)}, u32[]{:S(2)}, u32[]{:S(2)}) collective-permute-start(bf16[64,2048]{1,0:T(8,128)(2,1)} %get-tuple-element.371), channel_id=1, source_target_pairs={{0,10},{1,11},{2,8},{3,9},{4,14},{5,15},{6,12},{7,13},{8,2},{9,3},... | collective-permute-start | bytes 786440 | tf_op jit(solution)/shard_map/ppermute | solution.py:206
  102.4 45.9 %collective-permute-start.22 = (bf16[64,2048]{1,0:T(8,128)(2,1)}, bf16[64,2048]{1,0:T(8,128)(2,1)}, u32[]{:S(2)}, u32[]{:S(2)}) collective-permute-start(bf16[64,2048]{1,0:T(8,128)(2,1)} %get-tuple-element.372), channel_id=1, source_target_pairs={{0,12},{1,13},{2,14},{3,15},{4,8},{5,9},{6,10},{7,11},{8,4},{9,5},... | collective-permute-start | bytes 786440 | tf_op jit(solution)/shard_map/ppermute | solution.py:206
  106.0 42.3 %collective-permute-start.23 = (bf16[64,2048]{1,0:T(8,128)(2,1)}, bf16[64,2048]{1,0:T(8,128)(2,1)}, u32[]{:S(2)}, u32[]{:S(2)}) collective-permute-start(bf16[64,2048]{1,0:T(8,128)(2,1)} %get-tuple-element.373), channel_id=1, source_target_pairs={{0,14},{1,15},{2,12},{3,13},{4,10},{5,11},{6,8},{7,9},{8,6},{9,7},... | collective-permute-start | bytes 786440 | tf_op jit(solution)/shard_map/ppermute | solution.py:206
  106.8 0.7 copy-start.5
  106.8 0.8 copy-start.6
  109.3 4.3 %collective-permute-start.10 = (bf16[256,2048]{1,0:T(8,128)(2,1)S(1)}, bf16[256,2048]{1,0:T(8,128)(2,1)S(1)}, u32[]{:S(2)}, u32[]{:S(2)}) collective-permute-start(bf16[256,2048]{1,0:T(8,128)(2,1)S(1)} %get-tuple-element.208), channel_id=1, source_target_pairs={{0,1},{1,0},{2,3},{3,2},{4,5},{5,4},{6,7},{7,6},{8,9},{9,8},{10,11... | collective-permute-start | bytes 3145736 | tf_op jit(solution)/shard_map/cond/branch_1_fun/ppermute | solution.py:209
  109.4 38.9 %all-to-all-start.3 = ((bf16[4,64,2048]{2,1,0:T(8,128)(2,1)}), bf16[4,64,2048]{2,1,0:T(8,128)(2,1)}, u32[]{:S(2)}, u32[]{:S(2)}) async-start(bf16[4,64,2048]{2,1,0:T(8,128)(2,1)} %bitcast.69), calls=%async_computation.3 | async-start | bytes 2097152 | tf_op jit(solution)/shard_map/cond/branch_1_fun/all_to_all | solution.py:226
  117.1 5.7 %collective-permute-start.11 = (bf16[256,2048]{1,0:T(8,128)(2,1)}, bf16[256,2048]{1,0:T(8,128)(2,1)}, u32[]{:S(2)}, u32[]{:S(2)}) collective-permute-start(bf16[256,2048]{1,0:T(8,128)(2,1)} %get-tuple-element.210), channel_id=1, source_target_pairs={{0,1},{1,0},{2,3},{3,2},{4,5},{5,4},{6,7},{7,6},{8,9},{9,8},{10,11... | collective-permute-start | bytes 3145736 | tf_op jit(solution)/shard_map/cond/branch_1_fun/ppermute | solution.py:209
  148.3 3.1 %copy-start.7 = (f32[32,16,16]{0,2,1:T(8,128)}, f32[32,16,16]{0,2,1:T(8,128)S(1)}, u32[]{:S(2)}) copy-start(f32[32,16,16]{0,2,1:T(8,128)S(1)} %get-tuple-element.496) | copy-start | bytes 98308
  148.3 36.9 %collective-permute-start.24 = (bf16[64,2048]{1,0:T(8,128)(2,1)}, bf16[64,2048]{1,0:T(8,128)(2,1)}, u32[]{:S(2)}, u32[]{:S(2)}) collective-permute-start(bf16[64,2048]{1,0:T(8,128)(2,1)} %get-tuple-element.402), channel_id=1, source_target_pairs={{0,8},{1,9},{2,10},{3,11},{4,12},{5,13},{6,14},{7,15},{8,0},{9,1},... | collective-permute-start | bytes 786440 | tf_op jit(solution)/shard_map/ppermute | solution.py:206
  150.9 34.4 %collective-permute-start.25 = (bf16[64,2048]{1,0:T(8,128)(2,1)}, bf16[64,2048]{1,0:T(8,128)(2,1)}, u32[]{:S(2)}, u32[]{:S(2)}) collective-permute-start(bf16[64,2048]{1,0:T(8,128)(2,1)} %get-tuple-element.403), channel_id=1, source_target_pairs={{0,12},{1,13},{2,14},{3,15},{4,8},{5,9},{6,10},{7,11},{8,4},{9,5},... | collective-permute-start | bytes 786440 | tf_op jit(solution)/shard_map/ppermute | solution.py:206
  151.3 38.5 %copy-start.1 = (bf16[512,2048]{1,0:T(8,128)(2,1)S(1)}, bf16[512,2048]{1,0:T(8,128)(2,1)}, u32[]{:S(2)}) copy-start(bf16[512,2048]{1,0:T(8,128)(2,1)} %a.3) | copy-start | bytes 6291460
  155.8 6.5 %collective-permute-start.6 = (bf16[4,32,512]{2,1,0:T(8,128)(2,1)}, bf16[4,32,512]{2,1,0:T(8,128)(2,1)S(1)}, u32[]{:S(2)}, u32[]{:S(2)}) collective-permute-start(bf16[4,32,512]{2,1,0:T(8,128)(2,1)} %get-tuple-element.503), channel_id=1, source_target_pairs={{0,2},{1,3},{2,0},{3,1},{4,6},{5,7},{6,4},{7,5},{8,10},{9,11},{10,... | collective-permute-start | bytes 393224 | tf_op jit(solution)/shard_map/cond/branch_1_fun/ppermute | solution.py:209
  157.2 5.7 %collective-permute-start.7 = (bf16[4,32,512]{2,1,0:T(8,128)(2,1)S(1)}, bf16[4,32,512]{2,1,0:T(8,128)(2,1)S(1)}, u32[]{:S(2)}, u32[]{:S(2)}) collective-permute-start(bf16[4,32,512]{2,1,0:T(8,128)(2,1)S(1)} %get-tuple-element.504), channel_id=1, source_target_pairs={{0,3},{1,2},{2,1},{3,0},{4,7},{5,6},{6,5},{7,4},{8,11},{9,10},{10,... | collective-permute-start | bytes 393224 | tf_op jit(solution)/shard_map/cond/branch_1_fun/ppermute | solution.py:209
  157.2 28.0 %all-to-all-start.2 = ((bf16[4,64,2048]{2,1,0:T(8,128)(2,1)}), bf16[4,64,2048]{2,1,0:T(8,128)(2,1)}, u32[]{:S(2)}, u32[]{:S(2)}) async-start(bf16[4,64,2048]{2,1,0:T(8,128)(2,1)} %bitcast.17), calls=%async_computation.2 | async-start | bytes 2097152 | tf_op jit(solution)/shard_map/cond/branch_1_fun/all_to_all | solution.py:226
  161.5 1.8 collective-permute-start.5
  163.4 13.4 %collective-permute-start.8 = (bf16[4,32,512]{2,1,0:T(8,128)(2,1)S(1)}, bf16[4,32,512]{2,1,0:T(8,128)(2,1)S(1)}, u32[]{:S(2)}, u32[]{:S(2)}) collective-permute-start(bf16[4,32,512]{2,1,0:T(8,128)(2,1)S(1)} %fusion.16), channel_id=1, source_target_pairs={{0,8},{1,9},{2,10},{3,11},{4,12},{5,13},{6,14},{7,15},{8,0},{9,1},... | collective-permute-start | bytes 393224 | tf_op jit(solution)/shard_map/cond/branch_1_fun/ppermute | solution.py:206
  176.9 8.3 %collective-permute-start.9 = (bf16[4,32,512]{2,1,0:T(8,128)(2,1)S(1)}, bf16[4,32,512]{2,1,0:T(8,128)(2,1)S(1)}, u32[]{:S(2)}, u32[]{:S(2)}) collective-permute-start(bf16[4,32,512]{2,1,0:T(8,128)(2,1)S(1)} %add_convert_fusion.1), channel_id=1, source_target_pairs={{0,4},{1,5},{2,6},{3,7},{4,0},{5,1},{6,2},{7,3},{8,12},{9,13},{10,... | collective-permute-start | bytes 393224 | tf_op jit(solution)/shard_map/cond/branch_1_fun/ppermute | solution.py:206
  185.3 21.5 %collective-permute-start.26 = (bf16[64,2048]{1,0:T(8,128)(2,1)}, bf16[64,2048]{1,0:T(8,128)(2,1)S(1)}, u32[]{:S(2)}, u32[]{:S(2)}) collective-permute-start(bf16[64,2048]{1,0:T(8,128)(2,1)} %get-tuple-element.410), channel_id=1, source_target_pairs={{0,10},{1,11},{2,8},{3,9},{4,14},{5,15},{6,12},{7,13},{8,2},{9,3},... | collective-permute-start | bytes 786440 | tf_op jit(solution)/shard_map/ppermute | solution.py:206
  187.6 19.2 %collective-permute-start.27 = (bf16[64,2048]{1,0:T(8,128)(2,1)}, bf16[64,2048]{1,0:T(8,128)(2,1)S(1)}, u32[]{:S(2)}, u32[]{:S(2)}) collective-permute-start(bf16[64,2048]{1,0:T(8,128)(2,1)} %get-tuple-element.411), channel_id=1, source_target_pairs={{0,14},{1,15},{2,12},{3,13},{4,10},{5,11},{6,8},{7,9},{8,6},{9,7},... | collective-permute-start | bytes 786440 | tf_op jit(solution)/shard_map/ppermute | solution.py:206
  189.9 7.2 %collective-permute-start.2 = (bf16[4,32,512]{2,1,0:T(8,128)(2,1)S(1)}, bf16[4,32,512]{2,1,0:T(8,128)(2,1)S(1)}, u32[]{:S(2)}, u32[]{:S(2)}) collective-permute-start(bf16[4,32,512]{2,1,0:T(8,128)(2,1)S(1)} %get-tuple-element.238.refs_0_), channel_id=1, source_target_pairs={{0,2},{1,3},{2,0},{3,1},{4,6},{5,7},{6,4},{7,5},{8,10},{9,11},{10,... | collective-permute-start | bytes 393224 | tf_op jit(solution)/shard_map/cond/branch_1_fun/ppermute | solution.py:209
  190.7 6.9 %collective-permute-start.3 = (bf16[4,32,512]{2,1,0:T(8,128)(2,1)S(1)}, bf16[4,32,512]{2,1,0:T(8,128)(2,1)S(1)}, u32[]{:S(2)}, u32[]{:S(2)}) collective-permute-start(bf16[4,32,512]{2,1,0:T(8,128)(2,1)S(1)} %get-tuple-element.238.refs_0_), channel_id=1, source_target_pairs={{0,1},{1,0},{2,3},{3,2},{4,5},{5,4},{6,7},{7,6},{8,9},{9,8},{10,11... | collective-permute-start | bytes 393224 | tf_op jit(solution)/shard_map/cond/branch_1_fun/ppermute | solution.py:209
  190.7 2.7 %copy-start.3 = (bf16[512,512]{1,0:T(8,128)(2,1)S(1)}, bf16[512,512]{1,0:T(8,128)(2,1)}, u32[]{:S(2)}) copy-start(bf16[512,512]{1,0:T(8,128)(2,1)} %get-tuple-element.239.matrix) | copy-start | bytes 1572868 | tf_op jit(solution)/shard_map/cond
  197.1 1.5 collective-permute-start.4
  199.2 8.3 %copy-start.4 = (f32[512,512]{1,0:T(8,128)}, f32[512,512]{1,0:T(8,128)S(1)}, u32[]{:S(2)}) copy-start(f32[512,512]{1,0:T(8,128)S(1)} %get-tuple-element.483) | copy-start | bytes 3145732
